TPU v7x, 1024 devices: a whole 4x8x16 slice. The times are simulated.
1024 devices in a mesh: fsdp: 128 (over z, y_hi, x), head: 8 (over y_lo, core).
Axes of the slice: x: 4, y: 8 (y_hi: 2, y_lo: 4; y = y_hi * 4 + y_lo), z: 16, core: 2. Of those that a mesh axis runs over, the one named last changes fastest.
Arguments:
- tokens: bfloat16 [32768, 5120], P(('fsdp', 'head')), may hold values from -6 to 6
- positions: int32 [32768], P(('fsdp', 'head')), may hold values from 0 to 2046, as said below
- offsets: int32 [32768], P(('fsdp', 'head')), may hold values from 0 to 32767, as said below
- q_weight: bfloat16 [5120, 2048], P('fsdp', 'head'), may hold values from -0.078125 to 0.078125
- x_weight: bfloat16 [5120, 2048], P('fsdp', 'head'), may hold values from -0.078125 to 0.078125
- shared_weight: bfloat16 [5120, 1024], P('fsdp', 'head'), may hold values from -0.078125 to 0.078125
- conv_x: float32 [4, 2048], P(None, 'head'), may hold values from -3 to 3
- conv_bc: float32 [4, 512], replicated, may hold values from -3 to 3
Outputs:
- q_rot: bfloat16 [32768, 2048], P('fsdp', 'head')
- k_rot: bfloat16 [32768, 512], P('fsdp')
- x_conv: bfloat16 [32768, 2048], P('fsdp', 'head')
- bc_conv: bfloat16 [32768, 512], P('fsdp')
Inputs may be any that keep to these rules, and one draw needn't show every extreme that they name: positions rise by one from row to row within a sequence. offsets[t] is the first row of row t's sequence; offsets[t] <= t and t - offsets[t] < 1024; sequences are runs of consecutive rows; the last row begins a sequence of its own.
All inputs are finite; a program needn't handle non-finite values.
Results may differ from a plain program's by a relative error of at most 0.012.
Values may be sent and summed in bfloat16 or wider, within the bound.
No kernel may reach another device: no remote copies, remote signals or barrier semaphores. Data moves between devices by JAX's collectives and lax.ppermute only.
A program may use at most 32 MiB of HBM per device.

v0:
```python
import jax
import jax.numpy as jnp
from jax import lax
from jax.sharding import PartitionSpec as P

HD = 128
KH = 4


rope_base = 10000.0


def from_behind(value, axis, steps):
    count = lax.axis_size(axis)
    first, last = (max(0, -steps), min(count, count - steps))
    return lax.ppermute(value, axis, [(source, source + steps) for source in range(first, last)])


def rotate(values, places, head_size):
    count_rows = values.shape[0]
    heads = values.reshape(count_rows, -1, head_size)
    half = head_size // 2
    index = jnp.arange(half, dtype=jnp.float32)
    inverse = jnp.exp(-jnp.log(jnp.float32(rope_base)) * index / jnp.float32(half))
    angle = places.astype(jnp.float32)[:, None] * inverse[None, :]
    cosine = jnp.cos(angle)[:, None, :]
    sine = jnp.sin(angle)[:, None, :]
    first = heads[..., :half]
    second = heads[..., half:]
    turned = jnp.concatenate(
        [first * cosine - second * sine, second * cosine + first * sine], axis=-1
    )
    return turned.reshape(count_rows, -1)


def causal_conv(extended, taps, row_ids, starts):
    lag_rows = taps.shape[0] - 1
    count_rows = row_ids.shape[0]
    total = jnp.zeros((count_rows, extended.shape[1]), jnp.float32)
    for step_back in range(taps.shape[0]):
        window = extended[lag_rows - step_back : lag_rows - step_back + count_rows].astype(
            jnp.float32
        )
        valid = (row_ids - step_back >= starts).astype(jnp.float32)
        total = total + taps[step_back][None, :] * window * valid[:, None]
    return jax.nn.silu(total).astype(jnp.bfloat16)


def shards(tokens, positions, offsets, q_weight, x_weight, shared_weight, conv_x, conv_bc):
    rows_tok, rows_pos, rows_off = (
        lax.all_gather(tokens, "head", axis=0, tiled=True),
        lax.all_gather(positions, "head", axis=0, tiled=True),
        lax.all_gather(offsets, "head", axis=0, tiled=True),
    )
    group_rows = rows_tok.shape[0]
    lag_rows = conv_x.shape[0] - 1
    first_row = lax.axis_index("fsdp") * group_rows

    def add_piece(piece):
        return jnp.dot(rows_tok, piece, preferred_element_type=jnp.float32)

    pieces = (
        lax.all_gather(q_weight, "fsdp", axis=0, tiled=True),
        lax.all_gather(x_weight, "fsdp", axis=0, tiled=True),
    )
    q_acc, x_acc = tuple((add_piece(piece) for piece in pieces))
    s_acc = add_piece(lax.all_gather(shared_weight, "fsdp", axis=0, tiled=True))
    q_proj = q_acc.astype(jnp.bfloat16)
    x_proj = x_acc.astype(jnp.bfloat16)
    s_proj = s_acc.astype(jnp.bfloat16)
    s_whole = lax.all_gather(s_proj, "head", axis=1, tiled=True)
    key_width = KH * HD
    halo_x, halo_bc = from_behind(
        (x_proj[group_rows - lag_rows :], s_whole[group_rows - lag_rows :, key_width:]), "fsdp", 1
    )
    x_ext = jnp.concatenate([halo_x, x_proj], axis=0)
    bc_ext = jnp.concatenate([halo_bc, s_whole[:, key_width:]], axis=0)
    q_rot = rotate(q_proj.astype(jnp.float32), rows_pos, HD).astype(jnp.bfloat16)
    k_rot = rotate(s_whole[:, :key_width].astype(jnp.float32), rows_pos, HD).astype(jnp.bfloat16)
    row_ids = first_row + jnp.arange(group_rows, dtype=jnp.int32)
    x_conv = causal_conv(x_ext, conv_x, row_ids, rows_off)
    bc_conv = causal_conv(bc_ext, conv_bc, row_ids, rows_off)
    return (q_rot, k_rot, x_conv, bc_conv)


def solution(mesh):
    in_specs = (
        P(("fsdp", "head"), None),
        P(("fsdp", "head")),
        P(("fsdp", "head")),
        P("fsdp", "head"),
        P("fsdp", "head"),
        P("fsdp", "head"),
        P(None, "head"),
        P(),
    )
    out_specs = (P("fsdp", "head"), P("fsdp", None), P("fsdp", "head"), P("fsdp", None))
    return jax.shard_map(shards, mesh=mesh, in_specs=in_specs, out_specs=out_specs, check_vma=False)
```

profile of v0, /device:TPU:1, one launch (start us, length us, event | category | flops | bytes accessed | tf_op | source)
XLA Modules:
  0.0 748.0 jit_solution(8457000390870276065)
XLA Ops:
  7.2 0.7 all-gather.9.cloned.1.call-update
  7.9 0.7 all-gather.5.cloned.1.call-update
  8.7 0.7 all-gather.11.cloned.1.call-update
  9.4 0.5 all-gather.7.cloned.1.call-update
  10.0 1.3 dynamic-slice
  11.9 0.9 dynamic-update-slice
  12.8 0.8 dynamic-update-slice.1
  13.6 16.3 %all-reduce.2 = (s32[256]{0:T(256)S(1)}, s32[256]{0:T(256)S(1)}) all-reduce(s32[256]{0:T(256)S(1)} %dynamic-update-slice, s32[256]{0:T(256)S(1)} %dynamic-update-slice.1), channel_id=1, replica_groups=mesh['fsdp'=128,'head'=8] {'head'}, use_global_device_ids=true, to_apply=%add | all-reduce | flops 512 | bytes 4096
  29.9 0.3 multiply_cosine_fusion
  30.2 0.8 copy.13
  31.0 0.8 copy.14
  31.7 1.4 fusion.6
  33.2 1.5 fusion.5
  34.7 188.7 %all-gather.9.cloned.1.call-done = bf16[5120,128]{1,0:T(8,128)(2,1)} async-done(((bf16[40,128]{1,0:T(8,128)(2,1)}), bf16[5120,128]{1,0:T(8,128)(2,1)}) %all-gather.9.cloned.1.call-update) | async-done | bytes 1310736 | tf_op jit(solution)/shard_map/all_gather | solution.py:67
  223.3 52.6 %all-gather.5.cloned.1.call-done = bf16[256,5120]{1,0:T(8,128)(2,1)} async-done(((bf16[32,5120]{1,0:T(8,128)(2,1)}), bf16[256,5120]{1,0:T(8,128)(2,1)}) %all-gather.5.cloned.1.call-update) | async-done | bytes 2621456 | tf_op jit(solution)/shard_map/all_gather | solution.py:51
  276.0 2.9 convolution_convert_fusion.2
  278.9 16.1 %all_gather.25 = bf16[256,1024]{1,0:T(8,128)(2,1)S(1)} all-gather(bf16[256,128]{1,0:T(8,128)(2,1)S(1)} %convolution_convert_fusion.2), channel_id=1, replica_groups=mesh['fsdp'=128,'head'=8] {'head'}, dimensions={1}, use_global_device_ids=true | all-gather | bytes 589824 | tf_op jit(solution)/shard_map/all_gather | solution.py:71
  295.0 0.6 slice.99
  295.6 3.1 collective-permute-start.1
  298.8 0.9 fusion.4
  299.7 1.4 reshape.85
  301.0 1.4 subtract_convert_fusion
  302.5 0.4 pad_maximum_fusion.1
  302.8 0.7 copy.18
  303.6 1.9 multiply_convert_fusion
  305.5 199.4 %all-gather.11.cloned.1.call-done = bf16[5120,256]{1,0:T(8,128)(2,1)} async-done(((bf16[40,256]{1,0:T(8,128)(2,1)}), bf16[5120,256]{1,0:T(8,128)(2,1)}) %all-gather.11.cloned.1.call-update) | async-done | bytes 2621456 | tf_op jit(solution)/shard_map/all_gather | solution.py:64
  505.0 2.6 convolution_convert_fusion
  507.6 3.4 collective-permute-start
  511.0 225.8 %all-gather.7.cloned.1.call-done = bf16[5120,256]{1,0:T(8,128)(2,1)} async-done(((bf16[40,256]{1,0:T(8,128)(2,1)}), bf16[5120,256]{1,0:T(8,128)(2,1)}) %all-gather.7.cloned.1.call-update) | async-done | bytes 2621456 | tf_op jit(solution)/shard_map/all_gather | solution.py:63
  736.8 2.9 convolution_convert_fusion.1
  739.8 0.8 copy.15
  740.6 0.9 multiply_convert_fusion.1
  (25 shorter events, 0.3 us)
Async XLA Ops:
  7.2 216.2 %all-gather.9.cloned.1.call-start = ((), (), s32[]{:S(2)}) async-start(), calls=%async_computation.2 | async-start | bytes 1320960 | tf_op jit(solution)/shard_map/all_gather | solution.py:67
  7.9 268.1 %all-gather.5.cloned.1.call-start = ((), (), s32[]{:S(2)}) async-start(), calls=%async_computation | async-start | bytes 2949120 | tf_op jit(solution)/shard_map/all_gather | solution.py:51
  8.6 496.3 %all-gather.11.cloned.1.call-start = ((), (), s32[]{:S(2)}) async-start(), calls=%async_computation.3 | async-start | bytes 2641920 | tf_op jit(solution)/shard_map/all_gather | solution.py:64
  9.4 727.4 %all-gather.7.cloned.1.call-start = ((), (), s32[]{:S(2)}) async-start(), calls=%async_computation.1 | async-start | bytes 2641920 | tf_op jit(solution)/shard_map/all_gather | solution.py:63
  295.6 7.9 %collective-permute-start.1 = (bf16[3,512]{1,0:T(4,128)(2,1)}, bf16[3,512]{1,0:T(4,128)(2,1)}, u32[]{:S(2)}, u32[]{:S(2)}) collective-permute-start(bf16[3,512]{1,0:T(4,128)(2,1)} %slice.99), channel_id=1, source_target_pairs={{0,8},{8,16},{16,24},{24,32},{32,40},{40,48},{48,56},{56,64},{64,7... | collective-permute-start | bytes 9224 | tf_op jit(solution)/shard_map/ppermute | solution.py:16
  299.6 205.3 %copy-start = (bf16[256,5120]{1,0:T(8,128)(2,1)S(1)}, bf16[256,5120]{1,0:T(8,128)(2,1)}, u32[]{:S(2)}) copy-start(bf16[256,5120]{1,0:T(8,128)(2,1)} %all-gather.5.cloned.1.call-done) | copy-start | bytes 7864324
  507.6 233.0 %copy-start.1 = (f32[1,256]{1,0:T(1,128)S(1)}, f32[1,256]{1,0:T(1,128)}, u32[]{:S(2)}) copy-start(f32[1,256]{1,0:T(1,128)} %get-tuple-element.16) | copy-start | bytes 3076
  507.6 233.0 %copy-start.2 = (f32[1,256]{1,0:T(1,128)S(1)}, f32[1,256]{1,0:T(1,128)}, u32[]{:S(2)}) copy-start(f32[1,256]{1,0:T(1,128)} %get-tuple-element.17) | copy-start | bytes 3076
  507.6 233.0 %copy-start.3 = (f32[1,256]{1,0:T(1,128)S(1)}, f32[1,256]{1,0:T(1,128)}, u32[]{:S(2)}) copy-start(f32[1,256]{1,0:T(1,128)} %get-tuple-element.18) | copy-start | bytes 3076
  507.6 233.0 %copy-start.4 = (f32[1,256]{1,0:T(1,128)S(1)}, f32[1,256]{1,0:T(1,128)}, u32[]{:S(2)}) copy-start(f32[1,256]{1,0:T(1,128)} %get-tuple-element.19) | copy-start | bytes 3076
  507.6 233.0 %collective-permute-start = (bf16[3,256]{1,0:T(4,128)(2,1)S(1)}, bf16[3,256]{1,0:T(4,128)(2,1)S(1)}, u32[]{:S(2)}, u32[]{:S(2)}) collective-permute-start(bf16[3,256]{1,0:T(4,128)(2,1)S(1)} %slice.93), channel_id=1, source_target_pairs={{0,8},{8,16},{16,24},{24,32},{32,40},{40,48},{48,56},{56,64},{64,7... | collective-permute-start | bytes 4616 | tf_op jit(solution)/shard_map/ppermute | solution.py:16
Sparse Core Ops, SparseCore 0:
  13.8 209.4 all-gather.8
  226.0 49.9 all-gather.4
  281.8 223.1 all-gather.10
  510.6 226.1 all-gather.6
where the time goes:
time: 761 us; the launch traced here: 748 us
  waiting for transfers between devices  669 us (88%)
  blocking collectives  32.4 us (4%)
  between operations  14.6 us (2%)
  local copies, waits for them, and re-layouts  10.9 us (1%)
  matrix products  8.37 us (1%)
    all_gather x1, waiting for transfers between devices, shards(): lax.all_gather(q_weight, 'fsdp', axis=0, tiled=True)  226 us
    all_gather x1, waiting for transfers between devices, shards(): lax.all_gather(x_weight, 'fsdp', axis=0, tiled=True)  199 us
    all_gather x1, waiting for transfers between devices, shards(): s_acc = add_piece(lax.all_gather(shared_weight, 'fsdp', axis=0, tiled=True))  189 us
    all_gather x1, waiting for transfers between devices, shards(): lax.all_gather(tokens, 'head', axis=0, tiled=True)  52.6 us
    unnamed x1, blocking collectives  16.3 us
    all_gather x1, blocking collectives, shards(): s_whole = lax.all_gather(s_proj, 'head', axis=1, tiled=True)  16.1 us
  transfers between devices with their start and end apart: 6, of which 4 were waited for; matrix products, arithmetic and copies ran while one was open for 3% of the time, Pallas kernels for 0%

commit v1 on v0

v1 whole, which is shorter than its diff:
```python
import jax
import jax.numpy as jnp
from jax import lax
from jax.experimental import pallas as pl
from jax.experimental.pallas import tpu as pltpu
from jax.sharding import Mesh, PartitionSpec as P

HD = 128
KH = 4
HALO = 16
rope_base = 10000.0

AXES = ("zh", "zl", "yh", "x", "yl", "c")
SIZES = (4, 4, 2, 4, 4, 2)
FSDP = AXES[:4]


def fsdp_index(zh, zl, yh, x):
    return ((zh * 4 + zl) * 2 + yh) * 4 + x


def weight_moves(flip):
    moves = []
    for zh in range(4):
        for zl in range(4):
            for yh in range(2):
                for x in range(4):
                    inner = 2 * (zh % 2) + (yh if not flip else 1 - yh)
                    moves.append((fsdp_index(x, zl, zh // 2, inner), fsdp_index(zh, zl, yh, x)))
    return moves


def partial_kernel(core_ref, own_ref, other_ref, w_ref, out_ref, w_vmem, sems):
    copies = []
    for zh in range(4):
        for zl in range(4):
            copies.append(
                pltpu.make_async_copy(
                    w_ref.at[pl.ds((zh * 4 + zl) * 80, 80)],
                    w_vmem.at[pl.ds((zl * 4 + zh) * 80, 80)],
                    sems.at[zh * 4 + zl],
                )
            )
    for copy in copies:
        copy.start()
    for copy in copies:
        copy.wait()
    core = core_ref[0]
    for rows_ref, place in ((own_ref, core), (other_ref, 1 - core)):
        for first, width in ((0, 256), (256, 256), (512, 128)):
            part = jnp.dot(
                rows_ref[...], w_vmem[:, first : first + width], preferred_element_type=jnp.float32
            ).astype(jnp.bfloat16)
            for x in range(4):
                for yl in range(4):
                    piece = part[(x * 4 + yl) * 32 : (x * 4 + yl + 1) * 32]
                    at = pl.multiple_of(yl * 64 + place * 32, 32)
                    out_ref[x, pl.ds(at, 32), first : first + width] = piece


def final_kernel(
    halo_ref, proj_ref, s_ref, cos_ref, sin_ref, rel_ref, tx_ref, tbc_ref,
    q_ref, k_ref, x_ref, bc_ref, ext_ref,
):
    rows = proj_ref.shape[0]
    cosine = cos_ref[...]
    sine = sin_ref[...]

    def turned(values):
        return (values * cosine + pltpu.roll(values, HD // 2, 1) * sine).astype(jnp.bfloat16)

    def convolved(taps_ref, first):
        total = ext_ref[pl.ds(HALO, rows), :] * taps_ref[0:1, first : first + HD]
        for step_back in range(1, 4):
            window = ext_ref[pl.ds(HALO - step_back, rows), :] * taps_ref[step_back : step_back + 1, first : first + HD]
            total = total + jnp.where(rel_ref[...] >= step_back, window, 0.0)
        return (total / (1.0 + jnp.exp(-total))).astype(jnp.bfloat16)

    for head in range(2):
        cols = slice(head * HD, (head + 1) * HD)
        q_ref[:, cols] = turned(proj_ref[:, cols].astype(jnp.float32))
    for head in range(KH):
        k_ref[:, head * HD : (head + 1) * HD] = turned(s_ref[head, HALO:, :].astype(jnp.float32))
    for block in range(2):
        cols = slice(256 + block * HD, 256 + (block + 1) * HD)
        ext_ref[0:HALO, :] = halo_ref[:, cols].astype(jnp.float32)
        ext_ref[HALO:, :] = proj_ref[:, cols].astype(jnp.float32)
        x_ref[:, block * HD : (block + 1) * HD] = convolved(tx_ref, block * HD)
    for block in range(4):
        ext_ref[...] = s_ref[KH + block].astype(jnp.float32)
        bc_ref[:, block * HD : (block + 1) * HD] = convolved(tbc_ref, block * HD)


def shards(tokens, positions, offsets, q_weight, x_weight, shared_weight, conv_x, conv_bc):
    bf16 = jnp.bfloat16
    weight = jnp.concatenate([q_weight, x_weight, shared_weight], axis=1)
    own_w = lax.ppermute(weight, FSDP, weight_moves(False))
    other_w = lax.ppermute(weight, FSDP, weight_moves(True))
    low = lax.axis_index("yh") == 0
    pair = jnp.concatenate([jnp.where(low, own_w, other_w), jnp.where(low, other_w, own_w)], axis=0)
    quarter = lax.all_gather(pair, ("zh", "zl"), axis=0, tiled=True)

    rows, width = tokens.shape
    split = tokens.reshape(rows, 4, width // 4).transpose(1, 0, 2)
    split = jnp.broadcast_to(split[:, None], (4, 4, rows, width // 4)).reshape(16, rows, width // 4)
    own_t = lax.all_to_all(split, ("x", "yl"), 0, 0).reshape(16 * rows, width // 4)
    other_t = lax.ppermute(own_t, "c", [(0, 1), (1, 0)])

    places = lax.all_gather(jnp.stack([positions, offsets]), ("yl", "c"), axis=1, tiled=True)
    group_rows = places.shape[1]
    half = HD // 2
    index = jnp.arange(half, dtype=jnp.float32)
    inverse = jnp.exp(-jnp.log(jnp.float32(rope_base)) * index / jnp.float32(half))
    angle = places[0].astype(jnp.float32)[:, None] * inverse[None, :]
    cosine, sine = jnp.cos(angle), jnp.sin(angle)
    cosine = jnp.concatenate([cosine, cosine], axis=1)
    sine = jnp.concatenate([-sine, sine], axis=1)
    row_ids = lax.axis_index(FSDP) * group_rows + jnp.arange(group_rows, dtype=jnp.int32)
    rel = jnp.broadcast_to((row_ids - places[1])[:, None], (group_rows, HD))

    columns = weight.shape[1]
    core = lax.axis_index("c").astype(jnp.int32).reshape(1)
    vmem = pl.BlockSpec(memory_space=pltpu.VMEM)
    partial = pl.pallas_call(
        partial_kernel,
        out_shape=jax.ShapeDtypeStruct((4, group_rows, columns), bf16),
        in_specs=[
            pl.BlockSpec(memory_space=pltpu.SMEM), vmem, vmem, pl.BlockSpec(memory_space=pl.ANY),
        ],
        out_specs=vmem,
        scratch_shapes=[pltpu.VMEM((width // 4, columns), bf16), pltpu.SemaphoreType.DMA((16,))],
        compiler_params=pltpu.CompilerParams(vmem_limit_bytes=40 * 2**20),
        name="partial_products",
    )(core, own_t, other_t, quarter)
    parts = lax.all_to_all(partial, "x", 0, 0)
    proj = jnp.sum(parts.astype(jnp.float32), axis=0).astype(bf16)

    count = 128
    halo = lax.ppermute(proj[group_rows - HALO :], FSDP, [(i, i + 1) for i in range(count - 1)])
    s_own = jnp.concatenate([halo[:, 512:], proj[:, 512:]], axis=0)
    s_all = lax.all_gather(s_own, ("yl", "c"), axis=0)

    return pl.pallas_call(
        final_kernel,
        out_shape=(
            jax.ShapeDtypeStruct((group_rows, 256), bf16),
            jax.ShapeDtypeStruct((group_rows, 512), bf16),
            jax.ShapeDtypeStruct((group_rows, 256), bf16),
            jax.ShapeDtypeStruct((group_rows, 512), bf16),
        ),
        in_specs=[vmem] * 8,
        out_specs=(vmem,) * 4,
        scratch_shapes=[pltpu.VMEM((group_rows + HALO, HD), jnp.float32)],
        compiler_params=pltpu.CompilerParams(vmem_limit_bytes=40 * 2**20),
        name="rotate_and_convolve",
    )(halo, proj, s_all, cosine, sine, rel, conv_x, conv_bc)


def solution(mesh):
    chips = Mesh(mesh.devices.reshape(SIZES), AXES)
    head = ("yl", "c")
    in_specs = (
        P(AXES, None), P(AXES), P(AXES),
        P(FSDP, head), P(FSDP, head), P(FSDP, head),
        P(None, head), P(),
    )
    out_specs = (P(FSDP, head), P(FSDP, None), P(FSDP, head), P(FSDP, None))
    return jax.shard_map(shards, mesh=chips, in_specs=in_specs, out_specs=out_specs, check_vma=False)
```

time: 761 us -> 192 us (0.25)
  the two profiles are of different devices: /device:TPU:1 before, /device:TPU:65 now
where the time goes in v1:
time: 192 us
  waiting for transfers between devices  82.3 us (43%)
  starting transfers between devices  43.8 us (23%)
  blocking collectives  38.3 us (20%)
  between operations  14.3 us (7%)
  Pallas kernels  7.19 us (4%)
  local copies, waits for them, and re-layouts  4.12 us (2%)
    all_gather x1, waiting for transfers between devices, shards(): quarter = lax.all_gather(pair, ('zh', 'zl'), axis=0, tiled=True)  68.1 us
    ppermute x1, starting transfers between devices, shards(): other_w = lax.ppermute(weight, FSDP, weight_moves(True))  24.5 us
    all_gather x1, blocking collectives, shards(): lax.all_gather(jnp.stack([positions, offsets]), ('yl', 'c'), axis=1, tile...  21.9 us
    all_gather x1, blocking collectives, shards(): s_all = lax.all_gather(s_own, ('yl', 'c'), axis=0)  16.4 us
    ppermute x1, waiting for transfers between devices, shards(): lax.ppermute(proj[group_rows - HALO:], FSDP, [(i, i + 1) for i in range(c...  7.63 us
    all_to_all x1, starting transfers between devices, shards(): lax.all_to_all(split, ('x', 'yl'), 0, 0).reshape(16 * rows, width // 4)  7.29 us
    pallas_call x1, Pallas kernels, shards(): pl.pallas_call(partial_kernel, out_shape=jax.ShapeDtypeStruct((4, group_r...  5.56 us
    all_to_all x1, waiting for transfers between devices, shards(): lax.all_to_all(split, ('x', 'yl'), 0, 0).reshape(16 * rows, width // 4)  5.43 us
  transfers between devices with their start and end apart: 7, of which 4 were waited for; matrix products, arithmetic and copies ran while one was open for 1% of the time, Pallas kernels for 0%

profile of v1, /device:TPU:65, one launch (start us, length us, event | category | flops | bytes accessed | tf_op | source)
XLA Modules:
  0.0 191.7 jit_solution(1524139692967473424)
XLA Ops:
  7.2 1.2 reshape.42
  8.4 1.2 broadcast_in_dim.4
  9.6 7.3 %all-to-all-start = ((bf16[16,32,1280]{2,1,0:T(8,128)(2,1)}), bf16[16,32,1280]{2,1,0:T(8,128)(2,1)S(1)}, u32[]{:S(2)}, u32[]{:S(2)}) async-start(bf16[16,32,1280]{2,1,0:T(8,128)(2,1)} %bitcast.2), calls=%async_computation | async-start | bytes 2621440 | tf_op jit(solution)/shard_map/all_to_all | solution.py:106
  16.9 0.0 all-gather.4.cloned.1.call-start
  17.0 0.7 collective-permute-start.1
  17.7 24.5 %collective-permute-start.2 = (bf16[40,640]{1,0:T(8,128)(2,1)S(1)}, bf16[40,640]{1,0:T(8,128)(2,1)S(1)}, u32[]{:S(2)}, u32[]{:S(2)}) collective-permute-start(bf16[40,640]{1,0:T(8,128)(2,1)S(1)} %constant_dynamic-update-slice_fusion), channel_id=1, source_target_pairs={{8,0},{264,8},{520,16},{776,24},{0,32},{256,40},{512,48},{768,56},... | collective-permute-start | bytes 153608 | tf_op jit(solution)/shard_map/ppermute | solution.py:98
  42.3 0.0 collective-permute-done.1
  42.3 1.2 collective-permute-done.2
  43.4 0.7 pad_maximum_fusion.2
  44.1 0.0 all-gather.4.cloned.1.call-update
  44.1 5.4 %all-to-all-done = bf16[16,32,1280]{2,1,0:T(8,128)(2,1)S(1)} async-done(((bf16[16,32,1280]{2,1,0:T(8,128)(2,1)}), bf16[16,32,1280]{2,1,0:T(8,128)(2,1)S(1)}, u32[]{:S(2)}, u32[]{:S(2)}) %all-to-all-start) | async-done | bytes 1310752 | tf_op jit(solution)/shard_map/all_to_all | solution.py:106
  49.5 3.6 %collective-permute-start = (bf16[512,1280]{1,0:T(8,128)(2,1)S(1)}, bf16[512,1280]{1,0:T(8,128)(2,1)S(1)}, u32[]{:S(2)}, u32[]{:S(2)}) collective-permute-start(bf16[512,1280]{1,0:T(8,128)(2,1)S(1)} %bitcast.16), channel_id=1, source_target_pairs={{0,1},{1,0},{2,3},{3,2},{4,5},{5,4},{6,7},{7,6},{8,9},{9,8},{10,11... | collective-permute-start | bytes 3932168 | tf_op jit(solution)/shard_map/ppermute | solution.py:107
  53.2 68.1 %all-gather.4.cloned.1.call-done.w_ref = bf16[1280,640]{1,0:T(8,128)(2,1)} async-done(((bf16[80,640]{1,0:T(8,128)(2,1)}), bf16[1280,640]{1,0:T(8,128)(2,1)}) %all-gather.4.cloned.1.call-update) | async-done | bytes 1638416 | tf_op jit(solution)/shard_map/all_gather | solution.py:101
  121.3 0.0 collective-permute-done.other_ref
  121.3 1.4 copy-done
  122.7 5.6 %partial_products.1 = bf16[4,256,640]{2,1,0:T(8,128)(2,1)} custom-call(s32[1]{0:T(128)} %bitcast.core_ref, bf16[512,1280]{1,0:T(8,128)(2,1)S(1)} %bitcast.17, bf16[512,1280]{1,0:T(8,128)(2,1)S(1)} %collective-permute-done.other_ref, bf16[1280,640]{1,0:T(8,128)(2,1)S(1)} %copy-done), custom_call_target="tpu_custom_call" | custom-call | tf_op jit(solution)/shard_map/partial_products/pallas_call | solution.py:124
  128.3 0.0 copy-start.6
  128.3 0.0 copy-start.7
  128.3 4.0 %all-to-all-start.1 = ((bf16[4,256,640]{2,1,0:T(8,128)(2,1)}), bf16[4,256,640]{2,1,0:T(8,128)(2,1)S(1)}, u32[]{:S(2)}, u32[]{:S(2)}) async-start(bf16[4,256,640]{2,1,0:T(8,128)(2,1)} %partial_products.1), calls=%async_computation.1 | async-start | bytes 2621440 | tf_op jit(solution)/shard_map/all_to_all | solution.py:135
  132.3 21.9 %all-gather.1 = s32[8,32,2]{1,2,0:T(2,128)S(1)} all-gather(s32[1,32,2]{1,2,0:T(2,128)S(1)} %add_bitcast_fusion), channel_id=1, replica_groups=mesh['zh'=4,'zl'=4,'yh'=2,'x'=4,'yl'=4,'c'=2] {'yl','c'}, dimensions={0}, use_global_device_ids=true | all-gather | bytes 2304 | tf_op jit(solution)/shard_map/all_gather | solution.py:109
  154.2 0.1 reshape.47
  154.3 0.5 fusion
  154.9 0.0 copy-start.1
  154.9 0.0 copy-start.2
  154.9 0.0 all-to-all-done.1
  154.9 0.3 reduce_sum.12.proj_ref
  155.3 3.7 %collective-permute-start.3 = (bf16[16,640]{1,0:T(8,128)(2,1)S(1)}, bf16[16,640]{1,0:T(8,128)(2,1)S(1)}, u32[]{:S(2)}, u32[]{:S(2)}) collective-permute-start(bf16[16,640]{1,0:T(8,128)(2,1)S(1)} %slice.20), channel_id=1, source_target_pairs={{0,8},{8,16},{16,24},{24,32},{32,40},{40,48},{48,56},{56,64},{64,7... | collective-permute-start | bytes 61448 | tf_op jit(solution)/shard_map/ppermute | solution.py:139
  158.9 0.1 pad_maximum_fusion
  159.1 7.6 %collective-permute-done.3.halo_ref = bf16[16,640]{1,0:T(8,128)(2,1)S(1)} collective-permute-done((bf16[16,640]{1,0:T(8,128)(2,1)S(1)}, bf16[16,640]{1,0:T(8,128)(2,1)S(1)}, u32[]{:S(2)}, u32[]{:S(2)}) %collective-permute-start.3) | collective-permute-done | bytes 20512 | tf_op jit(solution)/shard_map/ppermute | solution.py:139
  166.7 16.4 %all-gather = bf16[2176,128]{1,0:T(8,128)(2,1)S(1)} all-gather(bf16[272,128]{1,0:T(8,128)(2,1)S(1)} %pad_maximum_fusion.3), channel_id=2, replica_groups=mesh['zh'=4,'zl'=4,'yh'=2,'x'=4,'yl'=4,'c'=2] {'yl','c'}, dimensions={0}, use_global_device_ids=true | all-gather | bytes 626688 | tf_op jit(solution)/shard_map/all_gather | solution.py:141
  183.1 0.1 broadcast_in_dim.5.rel_ref
  183.3 1.6 rotate_and_convolve.1
  (25 shorter events, 0.1 us)
Async XLA Ops:
  9.6 7.4 %copy-start.3 = (bf16[40,256]{1,0:T(8,128)(2,1)S(1)}, bf16[40,256]{1,0:T(8,128)(2,1)}, u32[]{:S(2)}) copy-start(bf16[40,256]{1,0:T(8,128)(2,1)} %param.11) | copy-start | bytes 61444
  9.6 7.4 %copy-start.4 = (bf16[40,256]{1,0:T(8,128)(2,1)S(1)}, bf16[40,256]{1,0:T(8,128)(2,1)}, u32[]{:S(2)}) copy-start(bf16[40,256]{1,0:T(8,128)(2,1)} %param.12) | copy-start | bytes 61444
  9.6 7.4 %copy-start.5 = (bf16[40,128]{1,0:T(8,128)(2,1)S(1)}, bf16[40,128]{1,0:T(8,128)(2,1)}, u32[]{:S(2)}) copy-start(bf16[40,128]{1,0:T(8,128)(2,1)} %param.13) | copy-start | bytes 30724
  9.6 39.9 %all-to-all-start = ((bf16[16,32,1280]{2,1,0:T(8,128)(2,1)}), bf16[16,32,1280]{2,1,0:T(8,128)(2,1)S(1)}, u32[]{:S(2)}, u32[]{:S(2)}) async-start(bf16[16,32,1280]{2,1,0:T(8,128)(2,1)} %bitcast.2), calls=%async_computation | async-start | bytes 2621440 | tf_op jit(solution)/shard_map/all_to_all | solution.py:106
  16.9 104.3 %all-gather.4.cloned.1.call-start = ((), (), s32[]{:S(2)}) async-start(), calls=%async_computation.2 | async-start | bytes 1740800 | tf_op jit(solution)/shard_map/all_gather | solution.py:101
  17.0 25.2 %collective-permute-start.1 = (bf16[40,640]{1,0:T(8,128)(2,1)S(1)}, bf16[40,640]{1,0:T(8,128)(2,1)S(1)}, u32[]{:S(2)}, u32[]{:S(2)}) collective-permute-start(bf16[40,640]{1,0:T(8,128)(2,1)S(1)} %constant_dynamic-update-slice_fusion), channel_id=1, source_target_pairs={{0,0},{256,8},{512,16},{768,24},{8,32},{264,40},{520,48},{776,56},... | collective-permute-start | bytes 153608 | tf_op jit(solution)/shard_map/ppermute | solution.py:97
  17.7 25.7 %collective-permute-start.2 = (bf16[40,640]{1,0:T(8,128)(2,1)S(1)}, bf16[40,640]{1,0:T(8,128)(2,1)S(1)}, u32[]{:S(2)}, u32[]{:S(2)}) collective-permute-start(bf16[40,640]{1,0:T(8,128)(2,1)S(1)} %constant_dynamic-update-slice_fusion), channel_id=1, source_target_pairs={{8,0},{264,8},{520,16},{776,24},{0,32},{256,40},{512,48},{768,56},... | collective-permute-start | bytes 153608 | tf_op jit(solution)/shard_map/ppermute | solution.py:98
  49.5 71.7 %collective-permute-start = (bf16[512,1280]{1,0:T(8,128)(2,1)S(1)}, bf16[512,1280]{1,0:T(8,128)(2,1)S(1)}, u32[]{:S(2)}, u32[]{:S(2)}) collective-permute-start(bf16[512,1280]{1,0:T(8,128)(2,1)S(1)} %bitcast.16), channel_id=1, source_target_pairs={{0,1},{1,0},{2,3},{3,2},{4,5},{5,4},{6,7},{7,6},{8,9},{9,8},{10,11... | collective-permute-start | bytes 3932168 | tf_op jit(solution)/shard_map/ppermute | solution.py:107
  121.3 1.4 copy-start
  128.3 4.0 %copy-start.6 = (s32[32]{0:T(128)S(1)}, s32[32]{0:T(128)}, u32[]{:S(2)}) copy-start(s32[32]{0:T(128)} %param.10) | copy-start | bytes 388
  128.3 4.0 %copy-start.7 = (s32[32]{0:T(128)S(1)}, s32[32]{0:T(128)}, u32[]{:S(2)}) copy-start(s32[32]{0:T(128)} %param.9) | copy-start | bytes 388
  128.3 26.6 %all-to-all-start.1 = ((bf16[4,256,640]{2,1,0:T(8,128)(2,1)}), bf16[4,256,640]{2,1,0:T(8,128)(2,1)S(1)}, u32[]{:S(2)}, u32[]{:S(2)}) async-start(bf16[4,256,640]{2,1,0:T(8,128)(2,1)} %partial_products.1), calls=%async_computation.1 | async-start | bytes 2621440 | tf_op jit(solution)/shard_map/all_to_all | solution.py:135
  154.9 28.4 %copy-start.1 = (f32[4,512]{1,0:T(4,128)S(1)}, f32[4,512]{1,0:T(4,128)}, u32[]{:S(2)}) copy-start(f32[4,512]{1,0:T(4,128)} %tbc_ref.1) | copy-start | bytes 24580
  154.9 28.4 %copy-start.2 = (f32[4,256]{1,0:T(4,128)S(1)}, f32[4,256]{1,0:T(4,128)}, u32[]{:S(2)}) copy-start(f32[4,256]{1,0:T(4,128)} %tx_ref.1) | copy-start | bytes 12292
  155.3 11.4 %collective-permute-start.3 = (bf16[16,640]{1,0:T(8,128)(2,1)S(1)}, bf16[16,640]{1,0:T(8,128)(2,1)S(1)}, u32[]{:S(2)}, u32[]{:S(2)}) collective-permute-start(bf16[16,640]{1,0:T(8,128)(2,1)S(1)} %slice.20), channel_id=1, source_target_pairs={{0,8},{8,16},{16,24},{24,32},{32,40},{40,48},{48,56},{56,64},{64,7... | collective-permute-start | bytes 61448 | tf_op jit(solution)/shard_map/ppermute | solution.py:139
Sparse Core Ops, SparseCore 0:
  44.2 77.0 all-gather.3

commit v2 on v1

v2 whole, which is shorter than its diff:
```python
import jax
import jax.numpy as jnp
from jax import lax
from jax.experimental import pallas as pl
from jax.experimental.pallas import tpu as pltpu
from jax.sharding import Mesh, PartitionSpec as P

HD = 128
KH = 4
HALO = 16
rope_base = 10000.0

AXES = ("zh", "zl", "yh", "x", "yl", "c")
SIZES = (4, 4, 2, 4, 4, 2)
FSDP = AXES[:4]


def fsdp_index(zh, zl, yh, x):
    return ((zh * 4 + zl) * 2 + yh) * 4 + x


def weight_moves(flip):
    moves = []
    for zh in range(4):
        for zl in range(4):
            for yh in range(2):
                for x in range(4):
                    inner = 2 * (zh % 2) + (yh if not flip else 1 - yh)
                    moves.append((fsdp_index(x, zl, zh // 2, inner), fsdp_index(zh, zl, yh, x)))
    return moves


def shifted(count, steps):
    return [((i + steps) % count, i) for i in range(count)]


def partial_kernel(
    place_ref, own_ref, other_ref, tail_ref, w0_ref, up_ref, down_ref, up2_ref, down2_ref, out_ref, w_vmem, sems
):
    core, zl = place_ref[0], place_ref[1]
    copies = []
    for source, step, offset in (
        (w0_ref, 0, 0), (up_ref, 1, 0), (down_ref, 3, 0), (up2_ref, 2, 0), (down2_ref, 2, 160),
    ):
        first = pl.multiple_of(lax.rem(zl + step, 4) * 320 + offset, 32)
        copies.append(
            pltpu.make_async_copy(source, w_vmem.at[pl.ds(first, source.shape[0])], sems.at[len(copies)])
        )
    for copy in copies:
        copy.start()
    for copy in copies:
        copy.wait()
    for first, width in ((0, 256), (256, 256), (512, 128)):
        cols = slice(first, first + width)
        w = w_vmem[:, cols]
        for mine in (True, False):
            rows = own_ref[...] if mine else jnp.concatenate([other_ref[...], tail_ref[...]], axis=0)
            part = jnp.dot(rows, w, preferred_element_type=jnp.float32).astype(jnp.bfloat16)
            place = core if mine else 1 - core
            for x in range(4):
                for yl in range(4):
                    at = pl.multiple_of(HALO + yl * 64 + place * 32, 16)
                    out_ref[x, pl.ds(at, 32), cols] = part[(x * 4 + yl) * 32 : (x * 4 + yl + 1) * 32]
            if not mine:
                out_ref[0, 0:HALO, cols] = part[512 : 512 + HALO]
    for x in range(3):
        out_ref[x + 1, 0:HALO, :] = out_ref[x, 256 : 256 + HALO, :]


def final_kernel(
    core_ref, proj_ref, own_ref, other_ref, cos_ref, sin_ref, rel_ref, tx_ref, tbc_ref,
    q_ref, k_ref, x_ref, bc_ref, ext_ref,
):
    rows = q_ref.shape[0]
    core = core_ref[0]
    cosine = cos_ref[...]
    sine = sin_ref[...]

    def turned(values):
        return (values * cosine + pltpu.roll(values, HD // 2, 1) * sine).astype(jnp.bfloat16)

    def convolved(taps_ref, cols):
        taps = taps_ref[:, cols]
        total = ext_ref[pl.ds(HALO, rows), :] * taps[0:1]
        for step_back in range(1, 4):
            window = ext_ref[pl.ds(HALO - step_back, rows), :] * taps[step_back : step_back + 1]
            total = total + jnp.where(rel_ref[...] >= step_back, window, 0.0)
        return (total / (1.0 + jnp.exp(-total))).astype(jnp.bfloat16)

    for block in range(2):
        cols = slice(block * HD, (block + 1) * HD)
        q_ref[:, cols] = turned(proj_ref[HALO:, cols].astype(jnp.float32))
    for block in range(2):
        cols = slice(block * HD, (block + 1) * HD)
        ext_ref[...] = proj_ref[:, 256 + block * HD : 256 + (block + 1) * HD].astype(jnp.float32)
        x_ref[:, cols] = convolved(tx_ref, cols)
    for s_ref, place in ((own_ref, core), (other_ref, 1 - core)):
        for yl in range(2):
            cols = pl.ds(pl.multiple_of((2 * yl + place) * HD, HD), HD)
            k_ref[:, cols] = turned(s_ref[yl, HALO:, :].astype(jnp.float32))
            ext_ref[...] = s_ref[2 + yl].astype(jnp.float32)
            bc_ref[:, cols] = convolved(tbc_ref, cols)


def shards(tokens, positions, offsets, q_weight, x_weight, shared_weight, conv_x, conv_bc):
    bf16 = jnp.bfloat16
    rows, width = tokens.shape
    quarter = width // 4
    weight = jnp.concatenate([q_weight, x_weight, shared_weight], axis=1)
    depth, columns = weight.shape
    own_w = lax.ppermute(weight, FSDP, weight_moves(False))
    other_w = lax.ppermute(weight, FSDP, weight_moves(True))
    low = lax.axis_index("yh") == 0
    pair = jnp.concatenate([jnp.where(low, own_w, other_w), jnp.where(low, other_w, own_w)], axis=0)

    tokens, pair = lax.optimization_barrier((tokens, pair))
    split = tokens.reshape(rows, 4, quarter).transpose(1, 0, 2)
    split = jnp.broadcast_to(split[:, None], (4, 4, rows, quarter)).reshape(16, rows, quarter)
    own_t = lax.all_to_all(split, ("x", "yl"), 0, 0).reshape(16 * rows, quarter)

    far = [pair] + [lax.ppermute(pair, "zh", shifted(4, steps)) for steps in (1, 2, 3)]
    turn = lax.rem(4 - lax.axis_index("zh"), 4) * (2 * depth)
    near = lax.dynamic_slice(jnp.concatenate(far + far[:3], axis=0), (turn, 0), (8 * depth, columns))

    own_t, _ = lax.optimization_barrier((own_t, near))
    other_t = lax.ppermute(own_t, "c", [(0, 1), (1, 0)])

    z = ("zh", "zl")
    up = lax.ppermute(near, z, shifted(16, 1))
    down = lax.ppermute(near, z, shifted(16, -1))
    up2 = lax.ppermute(near[:160], z, shifted(16, 2))
    down2 = lax.ppermute(near[160:], z, shifted(16, -2))

    core = lax.axis_index("c").astype(jnp.int32)
    tail = jnp.where(core == 1, own_t[16 * rows - HALO :], other_t[16 * rows - HALO :])
    tail = lax.ppermute(tail, ("zh", "zl", "yh"), [(i, i + 1) for i in range(31)])

    places = lax.all_gather(jnp.stack([positions, offsets]), ("yl", "c"), axis=1, tiled=True)
    group_rows = places.shape[1]
    half = HD // 2
    index = jnp.arange(half, dtype=jnp.float32)
    inverse = jnp.exp(-jnp.log(jnp.float32(rope_base)) * index / jnp.float32(half))
    angle = places[0].astype(jnp.float32)[:, None] * inverse[None, :]
    cosine, sine = jnp.cos(angle), jnp.sin(angle)
    cosine = jnp.concatenate([cosine, cosine], axis=1)
    sine = jnp.concatenate([-sine, sine], axis=1)
    row_ids = lax.axis_index(FSDP) * group_rows + jnp.arange(group_rows, dtype=jnp.int32)
    rel = jnp.broadcast_to((row_ids - places[1])[:, None], (group_rows, HD))

    vmem = pl.BlockSpec(memory_space=pltpu.VMEM)
    smem = pl.BlockSpec(memory_space=pltpu.SMEM)
    partial = pl.pallas_call(
        partial_kernel,
        out_shape=jax.ShapeDtypeStruct((4, HALO + group_rows, columns), bf16),
        in_specs=[smem, vmem, vmem, vmem] + [pl.BlockSpec(memory_space=pl.ANY)] * 5,
        out_specs=vmem,
        scratch_shapes=[pltpu.VMEM((quarter, columns), bf16), pltpu.SemaphoreType.DMA((5,))],
        compiler_params=pltpu.CompilerParams(vmem_limit_bytes=40 * 2**20),
        name="partial_products",
    )(
        jnp.stack([core, lax.axis_index("zl").astype(jnp.int32)]),
        own_t, other_t, tail, near, up, down, up2, down2,
    )
    parts = lax.all_to_all(partial, "x", 0, 0)
    proj = jnp.sum(parts.astype(jnp.float32), axis=0).astype(bf16)

    s_proj = jnp.broadcast_to(proj[:, 512:], (4, HALO + group_rows, HD))
    own_s = lax.all_to_all(s_proj, "yl", 0, 0)
    other_s = lax.ppermute(own_s, "c", [(0, 1), (1, 0)])

    return pl.pallas_call(
        final_kernel,
        out_shape=(
            jax.ShapeDtypeStruct((group_rows, 256), bf16),
            jax.ShapeDtypeStruct((group_rows, 512), bf16),
            jax.ShapeDtypeStruct((group_rows, 256), bf16),
            jax.ShapeDtypeStruct((group_rows, 512), bf16),
        ),
        in_specs=[smem] + [vmem] * 8,
        out_specs=(vmem,) * 4,
        scratch_shapes=[pltpu.VMEM((group_rows + HALO, HD), jnp.float32)],
        compiler_params=pltpu.CompilerParams(vmem_limit_bytes=40 * 2**20),
        name="rotate_and_convolve",
    )(core.reshape(1), proj, own_s, other_s, cosine, sine, rel, conv_x, conv_bc)


def solution(mesh):
    chips = Mesh(mesh.devices.reshape(SIZES), AXES)
    head = ("yl", "c")
    in_specs = (
        P(AXES, None), P(AXES), P(AXES),
        P(FSDP, head), P(FSDP, head), P(FSDP, head),
        P(None, head), P(),
    )
    out_specs = (P(FSDP, head), P(FSDP, None), P(FSDP, head), P(FSDP, None))
    return jax.shard_map(shards, mesh=chips, in_specs=in_specs, out_specs=out_specs, check_vma=False)
```

time: 192 us -> 163 us (0.85)
  the two profiles are of different devices: /device:TPU:65 before, /device:TPU:1 now
where the time goes in v2:
time: 163 us; the launch traced here: 161 us
  starting transfers between devices  99.8 us (61%)
  waiting for transfers between devices  35.4 us (22%)
  blocking collectives  9.23 us (6%)
  local copies, waits for them, and re-layouts  7.64 us (5%)
  Pallas kernels  6.72 us (4%)
    ppermute x3, starting transfers between devices, shards(): lax.ppermute(pair, 'zh', shifted(4, steps))  27.3 us
    ppermute x1, starting transfers between devices, shards(): other_w = lax.ppermute(weight, FSDP, weight_moves(True))  26.2 us
    ppermute x3, waiting for transfers between devices, shards(): lax.ppermute(pair, 'zh', shifted(4, steps))  13.8 us
    all_gather x1, blocking collectives, shards(): lax.all_gather(jnp.stack([positions, offsets]), ('yl', 'c'), axis=1, tile...  9.23 us
    all_to_all x1, waiting for transfers between devices, shards(): parts = lax.all_to_all(partial, 'x', 0, 0)  8.54 us
    all_to_all x1, starting transfers between devices, shards(): own_t = lax.all_to_all(split, ('x', 'yl'), 0, 0).reshape(16 * rows, quarter)  8.03 us
    ppermute x1, starting transfers between devices, shards(): up = lax.ppermute(near, z, shifted(16, 1))  7.25 us
    ppermute x1, starting transfers between devices, shards(): other_s = lax.ppermute(own_s, 'c', [(0, 1), (1, 0)])  6.24 us
  transfers between devices with their start and end apart: 15, of which 8 were waited for; matrix products, arithmetic and copies ran while one was open for 1% of the time, Pallas kernels for 0%

profile of v2, /device:TPU:1, one launch (start us, length us, event | category | flops | bytes accessed | tf_op | source)
XLA Modules:
  0.0 161.0 jit_solution(9858469576245994149)
XLA Ops:
  0.6 0.7 constant_dynamic-update-slice_fusion.2
  1.4 0.7 constant_dynamic-update-slice_fusion.1
  2.1 0.7 constant_dynamic-update-slice_fusion
  3.5 26.2 %collective-permute-start.1 = (bf16[40,640]{1,0:T(8,128)(2,1)S(1)}, bf16[40,640]{1,0:T(8,128)(2,1)S(1)}, u32[]{:S(2)}, u32[]{:S(2)}) collective-permute-start(bf16[40,640]{1,0:T(8,128)(2,1)S(1)} %constant_dynamic-update-slice_fusion), channel_id=1, source_target_pairs={{8,0},{264,8},{520,16},{776,24},{0,32},{256,40},{512,48},{768,56},... | collective-permute-start | bytes 153608 | tf_op jit(solution)/shard_map/ppermute | solution.py:112
  29.7 1.2 collective-permute-done.1
  30.9 1.2 reshape.42
  32.2 1.2 broadcast_in_dim.6
  33.4 8.0 %all-to-all-start = ((bf16[16,32,1280]{2,1,0:T(8,128)(2,1)}), bf16[16,32,1280]{2,1,0:T(8,128)(2,1)S(1)}, u32[]{:S(2)}, u32[]{:S(2)}) async-start(bf16[16,32,1280]{2,1,0:T(8,128)(2,1)} %bitcast.3), calls=%async_computation | async-start | bytes 2621440 | tf_op jit(solution)/shard_map/all_to_all | solution.py:119
  41.4 15.5 %collective-permute-start.2 = (bf16[80,640]{1,0:T(8,128)(2,1)S(1)}, bf16[80,640]{1,0:T(8,128)(2,1)S(1)}, u32[]{:S(2)}, u32[]{:S(2)}) collective-permute-start(bf16[80,640]{1,0:T(8,128)(2,1)S(1)} %pad_maximum_fusion.2), channel_id=1, source_target_pairs={{256,0},{512,256},{768,512},{0,768},{257,1},{513,257},{769,513},{1... | collective-permute-start | bytes 307208 | tf_op jit(solution)/shard_map/ppermute | solution.py:121
  56.9 4.5 %collective-permute-start.3 = (bf16[80,640]{1,0:T(8,128)(2,1)S(1)}, bf16[80,640]{1,0:T(8,128)(2,1)S(1)}, u32[]{:S(2)}, u32[]{:S(2)}) collective-permute-start(bf16[80,640]{1,0:T(8,128)(2,1)S(1)} %pad_maximum_fusion.2), channel_id=1, source_target_pairs={{512,0},{768,256},{0,512},{256,768},{513,1},{769,257},{1,513},{257... | collective-permute-start | bytes 307208 | tf_op jit(solution)/shard_map/ppermute | solution.py:121
  61.5 7.3 %collective-permute-start.4 = (bf16[80,640]{1,0:T(8,128)(2,1)S(1)}, bf16[80,640]{1,0:T(8,128)(2,1)S(1)}, u32[]{:S(2)}, u32[]{:S(2)}) collective-permute-start(bf16[80,640]{1,0:T(8,128)(2,1)S(1)} %pad_maximum_fusion.2), channel_id=1, source_target_pairs={{768,0},{0,256},{256,512},{512,768},{769,1},{1,257},{257,513},{513... | collective-permute-start | bytes 307208 | tf_op jit(solution)/shard_map/ppermute | solution.py:121
  68.7 2.7 %collective-permute-done.2 = bf16[80,640]{1,0:T(8,128)(2,1)S(1)} collective-permute-done((bf16[80,640]{1,0:T(8,128)(2,1)S(1)}, bf16[80,640]{1,0:T(8,128)(2,1)S(1)}, u32[]{:S(2)}, u32[]{:S(2)}) %collective-permute-start.2) | collective-permute-done | bytes 102432 | tf_op jit(solution)/shard_map/ppermute | solution.py:121
  71.5 10.8 %collective-permute-done.3 = bf16[80,640]{1,0:T(8,128)(2,1)S(1)} collective-permute-done((bf16[80,640]{1,0:T(8,128)(2,1)S(1)}, bf16[80,640]{1,0:T(8,128)(2,1)S(1)}, u32[]{:S(2)}, u32[]{:S(2)}) %collective-permute-start.3) | collective-permute-done | bytes 102432 | tf_op jit(solution)/shard_map/ppermute | solution.py:121
  82.7 0.9 copy-done.2
  83.6 2.4 %collective-permute-start.5 = (bf16[512,1280]{1,0:T(8,128)(2,1)S(1)}, bf16[512,1280]{1,0:T(8,128)(2,1)S(1)}, u32[]{:S(2)}, u32[]{:S(2)}) collective-permute-start(bf16[512,1280]{1,0:T(8,128)(2,1)S(1)} %bitcast.16), channel_id=1, source_target_pairs={{0,1},{1,0},{2,3},{3,2},{4,5},{5,4},{6,7},{7,6},{8,9},{9,8},{10,11... | collective-permute-start | bytes 3932168 | tf_op jit(solution)/shard_map/ppermute | solution.py:126
  86.0 7.2 %collective-permute-start.7 = (bf16[320,640]{1,0:T(8,128)(2,1)S(1)}, bf16[320,640]{1,0:T(8,128)(2,1)S(1)}, u32[]{:S(2)}, u32[]{:S(2)}) collective-permute-start(bf16[320,640]{1,0:T(8,128)(2,1)S(1)} %constant_dynamic-slice_fusion.2.w0_ref), channel_id=1, source_target_pairs={{64,0},{128,64},{192,128},{256,192},{320,256},{384,320},{448,384},... | collective-permute-start | bytes 1228808 | tf_op jit(solution)/shard_map/ppermute | solution.py:129
  93.3 1.9 %collective-permute-start.8 = (bf16[320,640]{1,0:T(8,128)(2,1)S(1)}, bf16[320,640]{1,0:T(8,128)(2,1)S(1)}, u32[]{:S(2)}, u32[]{:S(2)}) collective-permute-start(bf16[320,640]{1,0:T(8,128)(2,1)S(1)} %constant_dynamic-slice_fusion.2.w0_ref), channel_id=1, source_target_pairs={{960,0},{0,64},{64,128},{128,192},{192,256},{256,320},{320,384},{3... | collective-permute-start | bytes 1228808 | tf_op jit(solution)/shard_map/ppermute | solution.py:130
  95.2 1.1 constant_dynamic-slice_fusion.1
  96.3 1.9 %collective-permute-start.10 = (bf16[160,640]{1,0:T(8,128)(2,1)S(1)}, bf16[160,640]{1,0:T(8,128)(2,1)S(1)}, u32[]{:S(2)}, u32[]{:S(2)}) collective-permute-start(bf16[160,640]{1,0:T(8,128)(2,1)S(1)} %get-tuple-element.10), channel_id=1, source_target_pairs={{896,0},{960,64},{0,128},{64,192},{128,256},{192,320},{256,384},{3... | collective-permute-start | bytes 614408 | tf_op jit(solution)/shard_map/ppermute | solution.py:132
  98.2 5.5 %collective-permute-start.9 = (bf16[160,640]{1,0:T(8,128)(2,1)S(1)}, bf16[160,640]{1,0:T(8,128)(2,1)S(1)}, u32[]{:S(2)}, u32[]{:S(2)}) collective-permute-start(bf16[160,640]{1,0:T(8,128)(2,1)S(1)} %get-tuple-element.11), channel_id=1, source_target_pairs={{128,0},{192,64},{256,128},{320,192},{384,256},{448,320},{512,384}... | collective-permute-start | bytes 614408 | tf_op jit(solution)/shard_map/ppermute | solution.py:131
  103.7 5.4 %collective-permute-start.6 = (bf16[16,1280]{1,0:T(8,128)(2,1)S(1)}, bf16[16,1280]{1,0:T(8,128)(2,1)S(1)}, u32[]{:S(2)}, u32[]{:S(2)}) collective-permute-start(bf16[16,1280]{1,0:T(8,128)(2,1)S(1)} %slice_select_fusion), channel_id=1, source_target_pairs={{0,32},{32,64},{64,96},{96,128},{128,160},{160,192},{192,224},{224... | collective-permute-start | bytes 122888 | tf_op jit(solution)/shard_map/ppermute | solution.py:136
  109.1 5.6 %collective-permute-done.10.down2_ref = bf16[160,640]{1,0:T(8,128)(2,1)S(1)} collective-permute-done((bf16[160,640]{1,0:T(8,128)(2,1)S(1)}, bf16[160,640]{1,0:T(8,128)(2,1)S(1)}, u32[]{:S(2)}, u32[]{:S(2)}) %collective-permute-start.10) | collective-permute-done | bytes 204832 | tf_op jit(solution)/shard_map/ppermute | solution.py:132
  114.8 5.1 %partial_products.1 = bf16[4,272,640]{2,1,0:T(8,128)(2,1)} custom-call(s32[2]{0:T(128)S(1)} %pad_add_fusion.place_ref, bf16[512,1280]{1,0:T(8,128)(2,1)S(1)} %bitcast.18, bf16[512,1280]{1,0:T(8,128)(2,1)S(1)} %collective-permute-done.5.other_ref, bf16[16,1280]{1,0:T(8,128)(2,1)S(1)} %collective-permute-done.6.tail_ref, ...), custom_call_target="tpu_custom_call" | custom-call | tf_op jit(solution)/shard_map/partial_products/pallas_call | solution.py:152
  119.9 3.6 %all-to-all-start.1 = ((bf16[4,272,640]{2,1,0:T(8,128)(2,1)}), bf16[4,272,640]{2,1,0:T(8,128)(2,1)S(1)}, u32[]{:S(2)}, u32[]{:S(2)}) async-start(bf16[4,272,640]{2,1,0:T(8,128)(2,1)} %partial_products.1), calls=%async_computation.1 | async-start | bytes 2785280 | tf_op jit(solution)/shard_map/all_to_all | solution.py:164
  123.5 9.2 %all-gather = s32[8,32,2]{1,2,0:T(2,128)S(1)} all-gather(s32[1,32,2]{1,2,0:T(2,128)S(1)} %add_bitcast_fusion), channel_id=1, replica_groups=mesh['zh'=4,'zl'=4,'yh'=2,'x'=4,'yl'=4,'c'=2] {'yl','c'}, dimensions={0}, use_global_device_ids=true | all-gather | bytes 2304 | tf_op jit(solution)/shard_map/all_gather | solution.py:138
  132.9 8.5 %all-to-all-done.1 = bf16[4,272,640]{2,1,0:T(8,128)(2,1)S(1)} async-done(((bf16[4,272,640]{2,1,0:T(8,128)(2,1)}), bf16[4,272,640]{2,1,0:T(8,128)(2,1)S(1)}, u32[]{:S(2)}, u32[]{:S(2)}) %all-to-all-start.1) | async-done | bytes 1392672 | tf_op jit(solution)/shard_map/all_to_all | solution.py:164
  141.8 0.7 broadcast_in_dim.7
  142.6 3.4 %all-to-all-start.2 = ((bf16[4,272,128]{2,1,0:T(8,128)(2,1)}), bf16[4,272,128]{2,1,0:T(8,128)(2,1)S(1)}, u32[]{:S(2)}, u32[]{:S(2)}) async-start(bf16[4,272,128]{2,1,0:T(8,128)(2,1)} %broadcast_in_dim.7), calls=%async_computation.2 | async-start | bytes 557056 | tf_op jit(solution)/shard_map/all_to_all | solution.py:168
  146.6 5.3 %all-to-all-done.2.own_ref = bf16[4,272,128]{2,1,0:T(8,128)(2,1)S(1)} async-done(((bf16[4,272,128]{2,1,0:T(8,128)(2,1)}), bf16[4,272,128]{2,1,0:T(8,128)(2,1)S(1)}, u32[]{:S(2)}, u32[]{:S(2)}) %all-to-all-start.2) | async-done | bytes 278560 | tf_op jit(solution)/shard_map/all_to_all | solution.py:168
  151.8 6.2 %collective-permute-start.11 = (bf16[4,272,128]{2,1,0:T(8,128)(2,1)S(1)}, bf16[4,272,128]{2,1,0:T(8,128)(2,1)S(1)}, u32[]{:S(2)}, u32[]{:S(2)}) collective-permute-start(bf16[4,272,128]{2,1,0:T(8,128)(2,1)S(1)} %all-to-all-done.2.own_ref), channel_id=1, source_target_pairs={{0,1},{1,0},{2,3},{3,2},{4,5},{5,4},{6,7},{7,6},{8,9},{9,8},{10,11... | collective-permute-start | bytes 835592 | tf_op jit(solution)/shard_map/ppermute | solution.py:169
  158.3 1.0 collective-permute-done.11.other_ref
  159.4 1.6 rotate_and_convolve.1
  (42 shorter events, 2.5 us)
Async XLA Ops:
  2.8 26.9 %collective-permute-start = (bf16[40,640]{1,0:T(8,128)(2,1)S(1)}, bf16[40,640]{1,0:T(8,128)(2,1)S(1)}, u32[]{:S(2)}, u32[]{:S(2)}) collective-permute-start(bf16[40,640]{1,0:T(8,128)(2,1)S(1)} %constant_dynamic-update-slice_fusion), channel_id=1, source_target_pairs={{0,0},{256,8},{512,16},{768,24},{8,32},{264,40},{520,48},{776,56},... | collective-permute-start | bytes 153608 | tf_op jit(solution)/shard_map/ppermute | solution.py:111
  3.5 27.4 %collective-permute-start.1 = (bf16[40,640]{1,0:T(8,128)(2,1)S(1)}, bf16[40,640]{1,0:T(8,128)(2,1)S(1)}, u32[]{:S(2)}, u32[]{:S(2)}) collective-permute-start(bf16[40,640]{1,0:T(8,128)(2,1)S(1)} %constant_dynamic-update-slice_fusion), channel_id=1, source_target_pairs={{8,0},{264,8},{520,16},{776,24},{0,32},{256,40},{512,48},{768,56},... | collective-permute-start | bytes 153608 | tf_op jit(solution)/shard_map/ppermute | solution.py:112
  33.4 50.2 %all-to-all-start = ((bf16[16,32,1280]{2,1,0:T(8,128)(2,1)}), bf16[16,32,1280]{2,1,0:T(8,128)(2,1)S(1)}, u32[]{:S(2)}, u32[]{:S(2)}) async-start(bf16[16,32,1280]{2,1,0:T(8,128)(2,1)} %bitcast.3), calls=%async_computation | async-start | bytes 2621440 | tf_op jit(solution)/shard_map/all_to_all | solution.py:119
  41.4 30.0 %collective-permute-start.2 = (bf16[80,640]{1,0:T(8,128)(2,1)S(1)}, bf16[80,640]{1,0:T(8,128)(2,1)S(1)}, u32[]{:S(2)}, u32[]{:S(2)}) collective-permute-start(bf16[80,640]{1,0:T(8,128)(2,1)S(1)} %pad_maximum_fusion.2), channel_id=1, source_target_pairs={{256,0},{512,256},{768,512},{0,768},{257,1},{513,257},{769,513},{1... | collective-permute-start | bytes 307208 | tf_op jit(solution)/shard_map/ppermute | solution.py:121
  56.9 25.4 %collective-permute-start.3 = (bf16[80,640]{1,0:T(8,128)(2,1)S(1)}, bf16[80,640]{1,0:T(8,128)(2,1)S(1)}, u32[]{:S(2)}, u32[]{:S(2)}) collective-permute-start(bf16[80,640]{1,0:T(8,128)(2,1)S(1)} %pad_maximum_fusion.2), channel_id=1, source_target_pairs={{512,0},{768,256},{0,512},{256,768},{513,1},{769,257},{1,513},{257... | collective-permute-start | bytes 307208 | tf_op jit(solution)/shard_map/ppermute | solution.py:121
  61.5 21.1 %collective-permute-start.4 = (bf16[80,640]{1,0:T(8,128)(2,1)S(1)}, bf16[80,640]{1,0:T(8,128)(2,1)S(1)}, u32[]{:S(2)}, u32[]{:S(2)}) collective-permute-start(bf16[80,640]{1,0:T(8,128)(2,1)S(1)} %pad_maximum_fusion.2), channel_id=1, source_target_pairs={{768,0},{0,256},{256,512},{512,768},{769,1},{1,257},{257,513},{513... | collective-permute-start | bytes 307208 | tf_op jit(solution)/shard_map/ppermute | solution.py:121
  82.7 0.9 copy-start.2
  83.6 20.1 %collective-permute-start.5 = (bf16[512,1280]{1,0:T(8,128)(2,1)S(1)}, bf16[512,1280]{1,0:T(8,128)(2,1)S(1)}, u32[]{:S(2)}, u32[]{:S(2)}) collective-permute-start(bf16[512,1280]{1,0:T(8,128)(2,1)S(1)} %bitcast.16), channel_id=1, source_target_pairs={{0,1},{1,0},{2,3},{3,2},{4,5},{5,4},{6,7},{7,6},{8,9},{9,8},{10,11... | collective-permute-start | bytes 3932168 | tf_op jit(solution)/shard_map/ppermute | solution.py:126
  86.0 28.7 %collective-permute-start.7 = (bf16[320,640]{1,0:T(8,128)(2,1)S(1)}, bf16[320,640]{1,0:T(8,128)(2,1)S(1)}, u32[]{:S(2)}, u32[]{:S(2)}) collective-permute-start(bf16[320,640]{1,0:T(8,128)(2,1)S(1)} %constant_dynamic-slice_fusion.2.w0_ref), channel_id=1, source_target_pairs={{64,0},{128,64},{192,128},{256,192},{320,256},{384,320},{448,384},... | collective-permute-start | bytes 1228808 | tf_op jit(solution)/shard_map/ppermute | solution.py:129
  93.3 21.5 %collective-permute-start.8 = (bf16[320,640]{1,0:T(8,128)(2,1)S(1)}, bf16[320,640]{1,0:T(8,128)(2,1)S(1)}, u32[]{:S(2)}, u32[]{:S(2)}) collective-permute-start(bf16[320,640]{1,0:T(8,128)(2,1)S(1)} %constant_dynamic-slice_fusion.2.w0_ref), channel_id=1, source_target_pairs={{960,0},{0,64},{64,128},{128,192},{192,256},{256,320},{320,384},{3... | collective-permute-start | bytes 1228808 | tf_op jit(solution)/shard_map/ppermute | solution.py:130
  96.3 18.5 %collective-permute-start.10 = (bf16[160,640]{1,0:T(8,128)(2,1)S(1)}, bf16[160,640]{1,0:T(8,128)(2,1)S(1)}, u32[]{:S(2)}, u32[]{:S(2)}) collective-permute-start(bf16[160,640]{1,0:T(8,128)(2,1)S(1)} %get-tuple-element.10), channel_id=1, source_target_pairs={{896,0},{960,64},{0,128},{64,192},{128,256},{192,320},{256,384},{3... | collective-permute-start | bytes 614408 | tf_op jit(solution)/shard_map/ppermute | solution.py:132
  98.2 16.6 %collective-permute-start.9 = (bf16[160,640]{1,0:T(8,128)(2,1)S(1)}, bf16[160,640]{1,0:T(8,128)(2,1)S(1)}, u32[]{:S(2)}, u32[]{:S(2)}) collective-permute-start(bf16[160,640]{1,0:T(8,128)(2,1)S(1)} %get-tuple-element.11), channel_id=1, source_target_pairs={{128,0},{192,64},{256,128},{320,192},{384,256},{448,320},{512,384}... | collective-permute-start | bytes 614408 | tf_op jit(solution)/shard_map/ppermute | solution.py:131
  103.7 11.1 %collective-permute-start.6 = (bf16[16,1280]{1,0:T(8,128)(2,1)S(1)}, bf16[16,1280]{1,0:T(8,128)(2,1)S(1)}, u32[]{:S(2)}, u32[]{:S(2)}) collective-permute-start(bf16[16,1280]{1,0:T(8,128)(2,1)S(1)} %slice_select_fusion), channel_id=1, source_target_pairs={{0,32},{32,64},{64,96},{96,128},{128,160},{160,192},{192,224},{224... | collective-permute-start | bytes 122888 | tf_op jit(solution)/shard_map/ppermute | solution.py:136
  119.9 3.6 %copy-start.3 = (s32[32]{0:T(128)S(1)}, s32[32]{0:T(128)}, u32[]{:S(2)}) copy-start(s32[32]{0:T(128)} %param.10) | copy-start | bytes 388
  119.9 3.6 %copy-start.4 = (s32[32]{0:T(128)S(1)}, s32[32]{0:T(128)}, u32[]{:S(2)}) copy-start(s32[32]{0:T(128)} %param.9) | copy-start | bytes 388
  119.9 21.5 %all-to-all-start.1 = ((bf16[4,272,640]{2,1,0:T(8,128)(2,1)}), bf16[4,272,640]{2,1,0:T(8,128)(2,1)S(1)}, u32[]{:S(2)}, u32[]{:S(2)}) async-start(bf16[4,272,640]{2,1,0:T(8,128)(2,1)} %partial_products.1), calls=%async_computation.1 | async-start | bytes 2785280 | tf_op jit(solution)/shard_map/all_to_all | solution.py:164
  141.8 17.6 %copy-start = (f32[4,512]{1,0:T(4,128)S(1)}, f32[4,512]{1,0:T(4,128)}, u32[]{:S(2)}) copy-start(f32[4,512]{1,0:T(4,128)} %tbc_ref.1) | copy-start | bytes 24580
  141.8 17.6 %copy-start.1 = (f32[4,256]{1,0:T(4,128)S(1)}, f32[4,256]{1,0:T(4,128)}, u32[]{:S(2)}) copy-start(f32[4,256]{1,0:T(4,128)} %tx_ref.1) | copy-start | bytes 12292
  142.6 9.3 %all-to-all-start.2 = ((bf16[4,272,128]{2,1,0:T(8,128)(2,1)}), bf16[4,272,128]{2,1,0:T(8,128)(2,1)S(1)}, u32[]{:S(2)}, u32[]{:S(2)}) async-start(bf16[4,272,128]{2,1,0:T(8,128)(2,1)} %broadcast_in_dim.7), calls=%async_computation.2 | async-start | bytes 557056 | tf_op jit(solution)/shard_map/all_to_all | solution.py:168
  151.8 7.4 %collective-permute-start.11 = (bf16[4,272,128]{2,1,0:T(8,128)(2,1)S(1)}, bf16[4,272,128]{2,1,0:T(8,128)(2,1)S(1)}, u32[]{:S(2)}, u32[]{:S(2)}) collective-permute-start(bf16[4,272,128]{2,1,0:T(8,128)(2,1)S(1)} %all-to-all-done.2.own_ref), channel_id=1, source_target_pairs={{0,1},{1,0},{2,3},{3,2},{4,5},{5,4},{6,7},{7,6},{8,9},{9,8},{10,11... | collective-permute-start | bytes 835592 | tf_op jit(solution)/shard_map/ppermute | solution.py:169

commit v3 on v2

--- a/solution.py
+++ b/solution.py
@@ -15,23 +15,24 @@
 FSDP = AXES[:4]
 
 
-def fsdp_index(zh, zl, yh, x):
-    return ((zh * 4 + zl) * 2 + yh) * 4 + x
+def shifted(count, steps):
+    return [((i + steps) % count, i) for i in range(count)]
 
 
-def weight_moves(flip):
-    moves = []
-    for zh in range(4):
-        for zl in range(4):
-            for yh in range(2):
-                for x in range(4):
-                    inner = 2 * (zh % 2) + (yh if not flip else 1 - yh)
-                    moves.append((fsdp_index(x, zl, zh // 2, inner), fsdp_index(zh, zl, yh, x)))
-    return moves
-
-
-def shifted(count, steps):
-    return [((i + steps) % count, i) for i in range(count)]
+def permute_kernel(tokens_ref, out_ref, stack_ref):
+    for p in range(8):
+        stack_ref[p * 32 : (p + 1) * 32, :] = tokens_ref[:, p * 640 : (p + 1) * 640]
+    source = lax.broadcasted_iota(jnp.int32, (640, 640), 0)
+    target = lax.broadcasted_iota(jnp.int32, (640, 640), 1)
+    wanted = (target // 40) % 4 * 160 + target // 160 * 40 + target % 40
+    pick = jnp.where(source == wanted, 1.0, 0.0).astype(jnp.bfloat16)
+    moved = jnp.dot(stack_ref[...], pick, preferred_element_type=jnp.float32)
+    for x in range(4):
+        piece = jnp.concatenate(
+            [moved[p * 32 : (p + 1) * 32, x * 160 : (x + 1) * 160] for p in range(8)], axis=1
+        ).astype(jnp.bfloat16)
+        for yl in range(4):
+            out_ref[x * 4 + yl] = piece
 
 
 def partial_kernel(
@@ -39,13 +40,15 @@
 ):
     core, zl = place_ref[0], place_ref[1]
     copies = []
-    for source, step, offset in (
-        (w0_ref, 0, 0), (up_ref, 1, 0), (down_ref, 3, 0), (up2_ref, 2, 0), (down2_ref, 2, 160),
+    for source, step, zhs in (
+        (w0_ref, 0, range(4)), (up_ref, 1, range(4)), (down_ref, 3, range(4)),
+        (up2_ref, 2, range(2)), (down2_ref, 2, range(2, 4)),
     ):
-        first = pl.multiple_of(lax.rem(zl + step, 4) * 320 + offset, 32)
-        copies.append(
-            pltpu.make_async_copy(source, w_vmem.at[pl.ds(first, source.shape[0])], sems.at[len(copies)])
-        )
+        for at, zh in enumerate(zhs):
+            first = pl.multiple_of((zh * 4 + lax.rem(zl + step, 4)) * 80, 16)
+            copies.append(
+                pltpu.make_async_copy(source.at[pl.ds(at * 80, 80)], w_vmem.at[pl.ds(first, 80)], sems.at[len(copies)])
+            )
     for copy in copies:
         copy.start()
     for copy in copies:
@@ -106,30 +109,31 @@
     bf16 = jnp.bfloat16
     rows, width = tokens.shape
     quarter = width // 4
+    vmem = pl.BlockSpec(memory_space=pltpu.VMEM)
+    smem = pl.BlockSpec(memory_space=pltpu.SMEM)
     weight = jnp.concatenate([q_weight, x_weight, shared_weight], axis=1)
-    depth, columns = weight.shape
-    own_w = lax.ppermute(weight, FSDP, weight_moves(False))
-    other_w = lax.ppermute(weight, FSDP, weight_moves(True))
-    low = lax.axis_index("yh") == 0
-    pair = jnp.concatenate([jnp.where(low, own_w, other_w), jnp.where(low, other_w, own_w)], axis=0)
-
-    tokens, pair = lax.optimization_barrier((tokens, pair))
-    split = tokens.reshape(rows, 4, quarter).transpose(1, 0, 2)
-    split = jnp.broadcast_to(split[:, None], (4, 4, rows, quarter)).reshape(16, rows, quarter)
-    own_t = lax.all_to_all(split, ("x", "yl"), 0, 0).reshape(16 * rows, quarter)
-
-    far = [pair] + [lax.ppermute(pair, "zh", shifted(4, steps)) for steps in (1, 2, 3)]
-    turn = lax.rem(4 - lax.axis_index("zh"), 4) * (2 * depth)
-    near = lax.dynamic_slice(jnp.concatenate(far + far[:3], axis=0), (turn, 0), (8 * depth, columns))
-
-    own_t, _ = lax.optimization_barrier((own_t, near))
-    other_t = lax.ppermute(own_t, "c", [(0, 1), (1, 0)])
+    columns = weight.shape[1]
+    near = lax.all_gather(weight, ("zh", "yh"), axis=0, tiled=True)
 
     z = ("zh", "zl")
     up = lax.ppermute(near, z, shifted(16, 1))
     down = lax.ppermute(near, z, shifted(16, -1))
     up2 = lax.ppermute(near[:160], z, shifted(16, 2))
     down2 = lax.ppermute(near[160:], z, shifted(16, -2))
+
+    tokens, _ = lax.optimization_barrier((tokens, near))
+    split = pl.pallas_call(
+        permute_kernel,
+        out_shape=jax.ShapeDtypeStruct((16, rows, quarter), bf16),
+        in_specs=[vmem],
+        out_specs=vmem,
+        scratch_shapes=[pltpu.VMEM((8 * rows, width // 8), bf16)],
+        compiler_params=pltpu.CompilerParams(vmem_limit_bytes=40 * 2**20),
+        name="permute_columns",
+    )(tokens)
+    own_t = lax.all_to_all(split, ("x", "yl"), 0, 0).reshape(16 * rows, quarter)
+    own_t, *_ = lax.optimization_barrier((own_t, up, down, up2, down2))
+    other_t = lax.ppermute(own_t, "c", [(0, 1), (1, 0)])
 
     core = lax.axis_index("c").astype(jnp.int32)
     tail = jnp.where(core == 1, own_t[16 * rows - HALO :], other_t[16 * rows - HALO :])
@@ -147,14 +151,12 @@
     row_ids = lax.axis_index(FSDP) * group_rows + jnp.arange(group_rows, dtype=jnp.int32)
     rel = jnp.broadcast_to((row_ids - places[1])[:, None], (group_rows, HD))
 
-    vmem = pl.BlockSpec(memory_space=pltpu.VMEM)
-    smem = pl.BlockSpec(memory_space=pltpu.SMEM)
     partial = pl.pallas_call(
         partial_kernel,
         out_shape=jax.ShapeDtypeStruct((4, HALO + group_rows, columns), bf16),
         in_specs=[smem, vmem, vmem, vmem] + [pl.BlockSpec(memory_space=pl.ANY)] * 5,
         out_specs=vmem,
-        scratch_shapes=[pltpu.VMEM((quarter, columns), bf16), pltpu.SemaphoreType.DMA((5,))],
+        scratch_shapes=[pltpu.VMEM((quarter, columns), bf16), pltpu.SemaphoreType.DMA((16,))],
         compiler_params=pltpu.CompilerParams(vmem_limit_bytes=40 * 2**20),
         name="partial_products",
     )(

time: 163 us -> 171 us (1.049)
  blocking collectives: 9.23 us -> 75.5 us
  starting transfers between devices: 99.8 us -> 46.6 us
  waiting for transfers between devices: 35.4 us -> 27.5 us
  Pallas kernels: 6.72 us -> 9.54 us
    all_gather x0 -> x1, blocking collectives: none -> 62.5 us  [shards(): near = lax.all_gather(weight, ('zh', 'yh'), axis=0, tiled=True)]
    ppermute x5 -> x0, starting transfers between devices: 54.2 us -> none  [the longest x3 27.3 us: shards(): lax.ppermute(pair, 'zh', shifted(4, steps))]
    ppermute x5 -> x0, waiting for transfers between devices: 14.9 us -> none  [the longest x3 13.8 us: shards(): lax.ppermute(pair, 'zh', shifted(4, steps))]
    ppermute x1, waiting for transfers between devices: 0.01 us -> 5.87 us  [shards(): up2 = lax.ppermute(near[:160], z, shifted(16, 2))]
    all_to_all x1, waiting for transfers between devices: 0.01 us -> 5.07 us  [shards(): own_t = lax.all_to_all(split, ('x', 'yl'), 0, 0).reshape(16 * rows, quarter)]
    all_to_all x1, waiting for transfers between devices: 8.54 us -> 4.21 us  [shards(): parts = lax.all_to_all(partial, 'x', 0, 0)]
    all_gather x1, blocking collectives: 9.23 us -> 13 us  [shards(): lax.all_gather(jnp.stack([positions, offsets]), ('yl', 'c'), axis=1, tile...]
    unnamed x19 -> x23, local copies, waits for them, and re-layouts: 2.53 us -> 6.04 us
  transfers between devices with their start and end apart: 15 -> 10, of which waited for: 8 -> 8; matrix products, arithmetic and copies ran while one was open for 1% -> 1% of each run, Pallas kernels for 0% -> 0%
where the time goes in v3:
time: 171 us; the launch traced here: 169 us
  blocking collectives  75.5 us (44%)
  starting transfers between devices  46.6 us (27%)
  waiting for transfers between devices  27.5 us (16%)
  Pallas kernels  9.54 us (6%)
  local copies, waits for them, and re-layouts  6.92 us (4%)
  other arithmetic  1.92 us (1%)
    all_gather x1, blocking collectives, shards(): near = lax.all_gather(weight, ('zh', 'yh'), axis=0, tiled=True)  62.5 us
    all_gather x1, blocking collectives, shards(): lax.all_gather(jnp.stack([positions, offsets]), ('yl', 'c'), axis=1, tile...  13 us
    ppermute x1, starting transfers between devices, shards(): up = lax.ppermute(near, z, shifted(16, 1))  7 us
    all_to_all x1, starting transfers between devices, shards(): own_t = lax.all_to_all(split, ('x', 'yl'), 0, 0).reshape(16 * rows, quarter)  6.72 us
    pallas_call x1, Pallas kernels, shards(): pl.pallas_call(partial_kernel, out_shape=jax.ShapeDtypeStruct((4, HALO +...  6.28 us
    unnamed x23, local copies, waits for them, and re-layouts  6.04 us
    ppermute x1, waiting for transfers between devices, shards(): up2 = lax.ppermute(near[:160], z, shifted(16, 2))  5.87 us
    ppermute x1, starting transfers between devices, shards(): other_s = lax.ppermute(own_s, 'c', [(0, 1), (1, 0)])  5.76 us
  transfers between devices with their start and end apart: 10, of which 8 were waited for; matrix products, arithmetic and copies ran while one was open for 1% of the time, Pallas kernels for 0%

profile of v3, /device:TPU:1, one launch (start us, length us, event | category | flops | bytes accessed | tf_op | source)
XLA Modules:
  0.0 168.8 jit_solution(8025677175989207715)
XLA Ops:
  0.6 0.8 pad_maximum_fusion.2
  1.4 62.5 %all_gather.6.w0_ref = bf16[320,640]{1,0:T(8,128)(2,1)S(1)} all-gather(bf16[40,640]{1,0:T(8,128)(2,1)S(1)} %pad_maximum_fusion.2), channel_id=1, replica_groups=mesh['zh'=4,'zl'=4,'yh'=2,'x'=4,'yl'=4,'c'=2] {'zh','yh'}, dimensions={0}, use_global_device_ids=true | all-gather | bytes 460800 | tf_op jit(solution)/shard_map/all_gather | solution.py:116
  63.9 1.0 copy-done.2
  64.9 1.6 permute_columns.1
  66.5 6.7 %all-to-all-start = ((bf16[16,32,1280]{2,1,0:T(8,128)(2,1)}), bf16[16,32,1280]{2,1,0:T(8,128)(2,1)S(1)}, u32[]{:S(2)}, u32[]{:S(2)}) async-start(bf16[16,32,1280]{2,1,0:T(8,128)(2,1)} %permute_columns.1), calls=%async_computation | async-start | bytes 2621440 | tf_op jit(solution)/shard_map/all_to_all | solution.py:134
  73.3 7.0 %collective-permute-start = (bf16[320,640]{1,0:T(8,128)(2,1)S(1)}, bf16[320,640]{1,0:T(8,128)(2,1)S(1)}, u32[]{:S(2)}, u32[]{:S(2)}) collective-permute-start(bf16[320,640]{1,0:T(8,128)(2,1)S(1)} %all_gather.6.w0_ref), channel_id=1, source_target_pairs={{64,0},{128,64},{192,128},{256,192},{320,256},{384,320},{448,384},... | collective-permute-start | bytes 1228808 | tf_op jit(solution)/shard_map/ppermute | solution.py:119
  80.3 1.9 %collective-permute-start.1 = (bf16[320,640]{1,0:T(8,128)(2,1)S(1)}, bf16[320,640]{1,0:T(8,128)(2,1)S(1)}, u32[]{:S(2)}, u32[]{:S(2)}) collective-permute-start(bf16[320,640]{1,0:T(8,128)(2,1)S(1)} %all_gather.6.w0_ref), channel_id=1, source_target_pairs={{960,0},{0,64},{64,128},{128,192},{192,256},{256,320},{320,384},{3... | collective-permute-start | bytes 1228808 | tf_op jit(solution)/shard_map/ppermute | solution.py:120
  82.2 3.1 %collective-permute-start.2 = (bf16[160,640]{1,0:T(8,128)(2,1)S(1)}, bf16[160,640]{1,0:T(8,128)(2,1)S(1)}, u32[]{:S(2)}, u32[]{:S(2)}) collective-permute-start(bf16[160,640]{1,0:T(8,128)(2,1)S(1)} %get-tuple-element.9), channel_id=1, source_target_pairs={{128,0},{192,64},{256,128},{320,192},{384,256},{448,320},{512,384}... | collective-permute-start | bytes 614408 | tf_op jit(solution)/shard_map/ppermute | solution.py:121
  85.3 3.1 %collective-permute-start.3 = (bf16[160,640]{1,0:T(8,128)(2,1)S(1)}, bf16[160,640]{1,0:T(8,128)(2,1)S(1)}, u32[]{:S(2)}, u32[]{:S(2)}) collective-permute-start(bf16[160,640]{1,0:T(8,128)(2,1)S(1)} %get-tuple-element.8), channel_id=1, source_target_pairs={{896,0},{960,64},{0,128},{64,192},{128,256},{192,320},{256,384},{3... | collective-permute-start | bytes 614408 | tf_op jit(solution)/shard_map/ppermute | solution.py:122
  88.4 5.9 %collective-permute-done.2.up2_ref = bf16[160,640]{1,0:T(8,128)(2,1)S(1)} collective-permute-done((bf16[160,640]{1,0:T(8,128)(2,1)S(1)}, bf16[160,640]{1,0:T(8,128)(2,1)S(1)}, u32[]{:S(2)}, u32[]{:S(2)}) %collective-permute-start.2) | collective-permute-done | bytes 204832 | tf_op jit(solution)/shard_map/ppermute | solution.py:121
  94.3 0.7 copy-done.3
  95.0 2.5 %collective-permute-done.3.down2_ref = bf16[160,640]{1,0:T(8,128)(2,1)S(1)} collective-permute-done((bf16[160,640]{1,0:T(8,128)(2,1)S(1)}, bf16[160,640]{1,0:T(8,128)(2,1)S(1)}, u32[]{:S(2)}, u32[]{:S(2)}) %collective-permute-start.3) | collective-permute-done | bytes 204832 | tf_op jit(solution)/shard_map/ppermute | solution.py:122
  97.5 0.7 copy-done.5
  98.2 0.7 copy-done
  99.0 5.1 %all-to-all-done = bf16[16,32,1280]{2,1,0:T(8,128)(2,1)S(1)} async-done(((bf16[16,32,1280]{2,1,0:T(8,128)(2,1)}), bf16[16,32,1280]{2,1,0:T(8,128)(2,1)S(1)}, u32[]{:S(2)}, u32[]{:S(2)}) %all-to-all-start) | async-done | bytes 1310752 | tf_op jit(solution)/shard_map/all_to_all | solution.py:134
  104.0 5.5 %collective-permute-start.4 = (bf16[512,1280]{1,0:T(8,128)(2,1)S(1)}, bf16[512,1280]{1,0:T(8,128)(2,1)S(1)}, u32[]{:S(2)}, u32[]{:S(2)}) collective-permute-start(bf16[512,1280]{1,0:T(8,128)(2,1)S(1)} %bitcast.14), channel_id=1, source_target_pairs={{0,1},{1,0},{2,3},{3,2},{4,5},{5,4},{6,7},{7,6},{8,9},{9,8},{10,11... | collective-permute-start | bytes 3932168 | tf_op jit(solution)/shard_map/ppermute | solution.py:136
  109.5 2.6 %collective-permute-done.4.other_ref = bf16[512,1280]{1,0:T(8,128)(2,1)S(1)} collective-permute-done((bf16[512,1280]{1,0:T(8,128)(2,1)S(1)}, bf16[512,1280]{1,0:T(8,128)(2,1)S(1)}, u32[]{:S(2)}, u32[]{:S(2)}) %collective-permute-start.4) | collective-permute-done | bytes 1310752 | tf_op jit(solution)/shard_map/ppermute | solution.py:136
  112.1 4.8 %collective-permute-start.5 = (bf16[16,1280]{1,0:T(8,128)(2,1)S(1)}, bf16[16,1280]{1,0:T(8,128)(2,1)S(1)}, u32[]{:S(2)}, u32[]{:S(2)}) collective-permute-start(bf16[16,1280]{1,0:T(8,128)(2,1)S(1)} %slice_select_fusion), channel_id=1, source_target_pairs={{0,32},{32,64},{64,96},{96,128},{128,160},{160,192},{192,224},{224... | collective-permute-start | bytes 122888 | tf_op jit(solution)/shard_map/ppermute | solution.py:140
  117.0 1.0 collective-permute-done.5.tail_ref
  118.0 1.0 copy-done.1
  119.0 0.9 copy-done.4
  120.0 0.9 copy-done.6
  120.9 6.3 %partial_products.1 = bf16[4,272,640]{2,1,0:T(8,128)(2,1)} custom-call(s32[2]{0:T(128)S(1)} %pad_add_fusion.place_ref, bf16[512,1280]{1,0:T(8,128)(2,1)S(1)} %bitcast.16, bf16[512,1280]{1,0:T(8,128)(2,1)S(1)} %collective-permute-done.4.other_ref, bf16[16,1280]{1,0:T(8,128)(2,1)S(1)} %collective-permute-done.5.tail_ref, ...), custom_call_target="tpu_custom_call" | custom-call | tf_op jit(solution)/shard_map/partial_products/pallas_call | solution.py:154
  127.2 4.5 %all-to-all-start.1 = ((bf16[4,272,640]{2,1,0:T(8,128)(2,1)}), bf16[4,272,640]{2,1,0:T(8,128)(2,1)S(1)}, u32[]{:S(2)}, u32[]{:S(2)}) async-start(bf16[4,272,640]{2,1,0:T(8,128)(2,1)} %partial_products.1), calls=%async_computation.1 | async-start | bytes 2785280 | tf_op jit(solution)/shard_map/all_to_all | solution.py:166
  131.7 13.0 %all-gather = s32[8,32,2]{1,2,0:T(2,128)S(1)} all-gather(s32[1,32,2]{1,2,0:T(2,128)S(1)} %add_bitcast_fusion), channel_id=1, replica_groups=mesh['zh'=4,'zl'=4,'yh'=2,'x'=4,'yl'=4,'c'=2] {'yl','c'}, dimensions={0}, use_global_device_ids=true | all-gather | bytes 2304 | tf_op jit(solution)/shard_map/all_gather | solution.py:142
  144.8 4.2 %all-to-all-done.1 = bf16[4,272,640]{2,1,0:T(8,128)(2,1)S(1)} async-done(((bf16[4,272,640]{2,1,0:T(8,128)(2,1)}), bf16[4,272,640]{2,1,0:T(8,128)(2,1)S(1)}, u32[]{:S(2)}, u32[]{:S(2)}) %all-to-all-start.1) | async-done | bytes 1392672 | tf_op jit(solution)/shard_map/all_to_all | solution.py:166
  149.4 0.7 broadcast_in_dim.4
  150.2 4.3 %all-to-all-start.2 = ((bf16[4,272,128]{2,1,0:T(8,128)(2,1)}), bf16[4,272,128]{2,1,0:T(8,128)(2,1)S(1)}, u32[]{:S(2)}, u32[]{:S(2)}) async-start(bf16[4,272,128]{2,1,0:T(8,128)(2,1)} %broadcast_in_dim.4), calls=%async_computation.2 | async-start | bytes 557056 | tf_op jit(solution)/shard_map/all_to_all | solution.py:170
  155.0 5.2 %all-to-all-done.2.own_ref = bf16[4,272,128]{2,1,0:T(8,128)(2,1)S(1)} async-done(((bf16[4,272,128]{2,1,0:T(8,128)(2,1)}), bf16[4,272,128]{2,1,0:T(8,128)(2,1)S(1)}, u32[]{:S(2)}, u32[]{:S(2)}) %all-to-all-start.2) | async-done | bytes 278560 | tf_op jit(solution)/shard_map/all_to_all | solution.py:170
  160.2 5.8 %collective-permute-start.6 = (bf16[4,272,128]{2,1,0:T(8,128)(2,1)S(1)}, bf16[4,272,128]{2,1,0:T(8,128)(2,1)S(1)}, u32[]{:S(2)}, u32[]{:S(2)}) collective-permute-start(bf16[4,272,128]{2,1,0:T(8,128)(2,1)S(1)} %all-to-all-done.2.own_ref), channel_id=1, source_target_pairs={{0,1},{1,0},{2,3},{3,2},{4,5},{5,4},{6,7},{7,6},{8,9},{9,8},{10,11... | collective-permute-start | bytes 835592 | tf_op jit(solution)/shard_map/ppermute | solution.py:171
  166.1 1.0 collective-permute-done.6.other_ref
  167.2 1.6 rotate_and_convolve.1
  (31 shorter events, 1.4 us)
Async XLA Ops:
  63.9 1.0 copy-start.2
  66.5 37.5 %all-to-all-start = ((bf16[16,32,1280]{2,1,0:T(8,128)(2,1)}), bf16[16,32,1280]{2,1,0:T(8,128)(2,1)S(1)}, u32[]{:S(2)}, u32[]{:S(2)}) async-start(bf16[16,32,1280]{2,1,0:T(8,128)(2,1)} %permute_columns.1), calls=%async_computation | async-start | bytes 2621440 | tf_op jit(solution)/shard_map/all_to_all | solution.py:134
  73.3 24.9 %collective-permute-start = (bf16[320,640]{1,0:T(8,128)(2,1)S(1)}, bf16[320,640]{1,0:T(8,128)(2,1)S(1)}, u32[]{:S(2)}, u32[]{:S(2)}) collective-permute-start(bf16[320,640]{1,0:T(8,128)(2,1)S(1)} %all_gather.6.w0_ref), channel_id=1, source_target_pairs={{64,0},{128,64},{192,128},{256,192},{320,256},{384,320},{448,384},... | collective-permute-start | bytes 1228808 | tf_op jit(solution)/shard_map/ppermute | solution.py:119
  80.3 17.9 %collective-permute-start.1 = (bf16[320,640]{1,0:T(8,128)(2,1)S(1)}, bf16[320,640]{1,0:T(8,128)(2,1)S(1)}, u32[]{:S(2)}, u32[]{:S(2)}) collective-permute-start(bf16[320,640]{1,0:T(8,128)(2,1)S(1)} %all_gather.6.w0_ref), channel_id=1, source_target_pairs={{960,0},{0,64},{64,128},{128,192},{192,256},{256,320},{320,384},{3... | collective-permute-start | bytes 1228808 | tf_op jit(solution)/shard_map/ppermute | solution.py:120
  82.2 12.1 %collective-permute-start.2 = (bf16[160,640]{1,0:T(8,128)(2,1)S(1)}, bf16[160,640]{1,0:T(8,128)(2,1)S(1)}, u32[]{:S(2)}, u32[]{:S(2)}) collective-permute-start(bf16[160,640]{1,0:T(8,128)(2,1)S(1)} %get-tuple-element.9), channel_id=1, source_target_pairs={{128,0},{192,64},{256,128},{320,192},{384,256},{448,320},{512,384}... | collective-permute-start | bytes 614408 | tf_op jit(solution)/shard_map/ppermute | solution.py:121
  85.3 12.2 %collective-permute-start.3 = (bf16[160,640]{1,0:T(8,128)(2,1)S(1)}, bf16[160,640]{1,0:T(8,128)(2,1)S(1)}, u32[]{:S(2)}, u32[]{:S(2)}) collective-permute-start(bf16[160,640]{1,0:T(8,128)(2,1)S(1)} %get-tuple-element.8), channel_id=1, source_target_pairs={{896,0},{960,64},{0,128},{64,192},{128,256},{192,320},{256,384},{3... | collective-permute-start | bytes 614408 | tf_op jit(solution)/shard_map/ppermute | solution.py:122
  94.3 0.7 copy-start.3
  97.5 0.7 copy-start.5
  98.2 0.7 copy-start
  104.0 8.1 %collective-permute-start.4 = (bf16[512,1280]{1,0:T(8,128)(2,1)S(1)}, bf16[512,1280]{1,0:T(8,128)(2,1)S(1)}, u32[]{:S(2)}, u32[]{:S(2)}) collective-permute-start(bf16[512,1280]{1,0:T(8,128)(2,1)S(1)} %bitcast.14), channel_id=1, source_target_pairs={{0,1},{1,0},{2,3},{3,2},{4,5},{5,4},{6,7},{7,6},{8,9},{9,8},{10,11... | collective-permute-start | bytes 3932168 | tf_op jit(solution)/shard_map/ppermute | solution.py:136
  112.1 5.9 %collective-permute-start.5 = (bf16[16,1280]{1,0:T(8,128)(2,1)S(1)}, bf16[16,1280]{1,0:T(8,128)(2,1)S(1)}, u32[]{:S(2)}, u32[]{:S(2)}) collective-permute-start(bf16[16,1280]{1,0:T(8,128)(2,1)S(1)} %slice_select_fusion), channel_id=1, source_target_pairs={{0,32},{32,64},{64,96},{96,128},{128,160},{160,192},{192,224},{224... | collective-permute-start | bytes 122888 | tf_op jit(solution)/shard_map/ppermute | solution.py:140
  118.0 1.0 copy-start.1
  119.0 0.9 copy-start.4
  120.0 0.9 copy-start.6
  127.2 4.5 %copy-start.9 = (s32[32]{0:T(128)S(1)}, s32[32]{0:T(128)}, u32[]{:S(2)}) copy-start(s32[32]{0:T(128)} %param.10) | copy-start | bytes 388
  127.2 4.5 %copy-start.10 = (s32[32]{0:T(128)S(1)}, s32[32]{0:T(128)}, u32[]{:S(2)}) copy-start(s32[32]{0:T(128)} %param.9) | copy-start | bytes 388
  127.2 21.8 %all-to-all-start.1 = ((bf16[4,272,640]{2,1,0:T(8,128)(2,1)}), bf16[4,272,640]{2,1,0:T(8,128)(2,1)S(1)}, u32[]{:S(2)}, u32[]{:S(2)}) async-start(bf16[4,272,640]{2,1,0:T(8,128)(2,1)} %partial_products.1), calls=%async_computation.1 | async-start | bytes 2785280 | tf_op jit(solution)/shard_map/all_to_all | solution.py:166
  149.4 17.8 %copy-start.7 = (f32[4,512]{1,0:T(4,128)S(1)}, f32[4,512]{1,0:T(4,128)}, u32[]{:S(2)}) copy-start(f32[4,512]{1,0:T(4,128)} %tbc_ref.1) | copy-start | bytes 24580
  149.4 17.8 %copy-start.8 = (f32[4,256]{1,0:T(4,128)S(1)}, f32[4,256]{1,0:T(4,128)}, u32[]{:S(2)}) copy-start(f32[4,256]{1,0:T(4,128)} %tx_ref.1) | copy-start | bytes 12292
  150.2 10.0 %all-to-all-start.2 = ((bf16[4,272,128]{2,1,0:T(8,128)(2,1)}), bf16[4,272,128]{2,1,0:T(8,128)(2,1)S(1)}, u32[]{:S(2)}, u32[]{:S(2)}) async-start(bf16[4,272,128]{2,1,0:T(8,128)(2,1)} %broadcast_in_dim.4), calls=%async_computation.2 | async-start | bytes 557056 | tf_op jit(solution)/shard_map/all_to_all | solution.py:170
  160.2 6.9 %collective-permute-start.6 = (bf16[4,272,128]{2,1,0:T(8,128)(2,1)S(1)}, bf16[4,272,128]{2,1,0:T(8,128)(2,1)S(1)}, u32[]{:S(2)}, u32[]{:S(2)}) collective-permute-start(bf16[4,272,128]{2,1,0:T(8,128)(2,1)S(1)} %all-to-all-done.2.own_ref), channel_id=1, source_target_pairs={{0,1},{1,0},{2,3},{3,2},{4,5},{5,4},{6,7},{7,6},{8,9},{9,8},{10,11... | collective-permute-start | bytes 835592 | tf_op jit(solution)/shard_map/ppermute | solution.py:171

commit v4 on v3

--- a/solution.py
+++ b/solution.py
@@ -15,50 +15,42 @@
 FSDP = AXES[:4]
 
 
-def shifted(count, steps):
-    return [((i + steps) % count, i) for i in range(count)]
-
-
 def permute_kernel(tokens_ref, out_ref, stack_ref):
     for p in range(8):
         stack_ref[p * 32 : (p + 1) * 32, :] = tokens_ref[:, p * 640 : (p + 1) * 640]
     source = lax.broadcasted_iota(jnp.int32, (640, 640), 0)
     target = lax.broadcasted_iota(jnp.int32, (640, 640), 1)
-    wanted = (target // 40) % 4 * 160 + target // 160 * 40 + target % 40
+    wanted = target // 40 % 2 * 320 + target // 80 % 2 * 160 + target // 160 * 40 + target % 40
     pick = jnp.where(source == wanted, 1.0, 0.0).astype(jnp.bfloat16)
     moved = jnp.dot(stack_ref[...], pick, preferred_element_type=jnp.float32)
     for x in range(4):
         piece = jnp.concatenate(
-            [moved[p * 32 : (p + 1) * 32, x * 160 : (x + 1) * 160] for p in range(8)], axis=1
+            [
+                moved[p * 32 : (p + 1) * 32, x * 160 + yh * 80 : x * 160 + (yh + 1) * 80]
+                for yh in range(2)
+                for p in range(8)
+            ],
+            axis=1,
         ).astype(jnp.bfloat16)
         for yl in range(4):
             out_ref[x * 4 + yl] = piece
 
 
-def partial_kernel(
-    place_ref, own_ref, other_ref, tail_ref, w0_ref, up_ref, down_ref, up2_ref, down2_ref, out_ref, w_vmem, sems
-):
-    core, zl = place_ref[0], place_ref[1]
-    copies = []
-    for source, step, zhs in (
-        (w0_ref, 0, range(4)), (up_ref, 1, range(4)), (down_ref, 3, range(4)),
-        (up2_ref, 2, range(2)), (down2_ref, 2, range(2, 4)),
-    ):
-        for at, zh in enumerate(zhs):
-            first = pl.multiple_of((zh * 4 + lax.rem(zl + step, 4)) * 80, 16)
-            copies.append(
-                pltpu.make_async_copy(source.at[pl.ds(at * 80, 80)], w_vmem.at[pl.ds(first, 80)], sems.at[len(copies)])
-            )
-    for copy in copies:
-        copy.start()
-    for copy in copies:
-        copy.wait()
+def partial_kernel(place_ref, own_ref, other_ref, tail_ref, w_own_ref, w_other_ref, out_ref):
+    core, yh = place_ref[0], place_ref[1]
+    half = w_own_ref.shape[0]
+    near = pl.ds(pl.multiple_of(yh * half, 128), half)
+    far = pl.ds(pl.multiple_of((1 - yh) * half, 128), half)
     for first, width in ((0, 256), (256, 256), (512, 128)):
         cols = slice(first, first + width)
-        w = w_vmem[:, cols]
         for mine in (True, False):
-            rows = own_ref[...] if mine else jnp.concatenate([other_ref[...], tail_ref[...]], axis=0)
-            part = jnp.dot(rows, w, preferred_element_type=jnp.float32).astype(jnp.bfloat16)
+            part = 0.0
+            for at_k, w_ref in ((near, w_own_ref), (far, w_other_ref)):
+                rows = own_ref[:, at_k]
+                if not mine:
+                    rows = jnp.concatenate([other_ref[:, at_k], tail_ref[:, at_k]], axis=0)
+                part = part + jnp.dot(rows, w_ref[:, cols], preferred_element_type=jnp.float32)
+            part = part.astype(jnp.bfloat16)
             place = core if mine else 1 - core
             for x in range(4):
                 for yl in range(4):
@@ -111,17 +103,6 @@
     quarter = width // 4
     vmem = pl.BlockSpec(memory_space=pltpu.VMEM)
     smem = pl.BlockSpec(memory_space=pltpu.SMEM)
-    weight = jnp.concatenate([q_weight, x_weight, shared_weight], axis=1)
-    columns = weight.shape[1]
-    near = lax.all_gather(weight, ("zh", "yh"), axis=0, tiled=True)
-
-    z = ("zh", "zl")
-    up = lax.ppermute(near, z, shifted(16, 1))
-    down = lax.ppermute(near, z, shifted(16, -1))
-    up2 = lax.ppermute(near[:160], z, shifted(16, 2))
-    down2 = lax.ppermute(near[160:], z, shifted(16, -2))
-
-    tokens, _ = lax.optimization_barrier((tokens, near))
     split = pl.pallas_call(
         permute_kernel,
         out_shape=jax.ShapeDtypeStruct((16, rows, quarter), bf16),
@@ -132,13 +113,23 @@
         name="permute_columns",
     )(tokens)
     own_t = lax.all_to_all(split, ("x", "yl"), 0, 0).reshape(16 * rows, quarter)
-    own_t, *_ = lax.optimization_barrier((own_t, up, down, up2, down2))
+
+    z = ("zh", "zl")
+    weight = jnp.concatenate([q_weight, x_weight, shared_weight], axis=1)
+    columns = weight.shape[1]
+    partner = lax.ppermute(weight, "yh", [(0, 1), (1, 0)])
+    w_own = lax.all_gather(weight, z, axis=0, tiled=True)
+    own_t, w_own, partner = lax.optimization_barrier((own_t, w_own, partner))
+
     other_t = lax.ppermute(own_t, "c", [(0, 1), (1, 0)])
+    tail = own_t[16 * rows - HALO :]
+    sources = [(2 * i + 1, 2 * i + 2) for i in range(31)]
+    tail = lax.ppermute(tail, ("zh", "zl", "yh", "c"), sources) + lax.ppermute(
+        tail, ("zh", "zl", "yh", "c"), [(source, target + 1) for source, target in sources]
+    )
+    w_other = lax.all_gather(partner, z, axis=0, tiled=True)
 
     core = lax.axis_index("c").astype(jnp.int32)
-    tail = jnp.where(core == 1, own_t[16 * rows - HALO :], other_t[16 * rows - HALO :])
-    tail = lax.ppermute(tail, ("zh", "zl", "yh"), [(i, i + 1) for i in range(31)])
-
     places = lax.all_gather(jnp.stack([positions, offsets]), ("yl", "c"), axis=1, tiled=True)
     group_rows = places.shape[1]
     half = HD // 2
@@ -154,14 +145,12 @@
     partial = pl.pallas_call(
         partial_kernel,
         out_shape=jax.ShapeDtypeStruct((4, HALO + group_rows, columns), bf16),
-        in_specs=[smem, vmem, vmem, vmem] + [pl.BlockSpec(memory_space=pl.ANY)] * 5,
+        in_specs=[smem] + [vmem] * 5,
         out_specs=vmem,
-        scratch_shapes=[pltpu.VMEM((quarter, columns), bf16), pltpu.SemaphoreType.DMA((16,))],
         compiler_params=pltpu.CompilerParams(vmem_limit_bytes=40 * 2**20),
         name="partial_products",
     )(
-        jnp.stack([core, lax.axis_index("zl").astype(jnp.int32)]),
-        own_t, other_t, tail, near, up, down, up2, down2,
+        jnp.stack([core, lax.axis_index("yh").astype(jnp.int32)]), own_t, other_t, tail, w_own, w_other,
     )
     parts = lax.all_to_all(partial, "x", 0, 0)
     proj = jnp.sum(parts.astype(jnp.float32), axis=0).astype(bf16)

time: 171 us -> 149 us (0.87); the launches traced: 169 us -> 149 us
  waiting for transfers between devices: 27.5 us -> 16.3 us
  local copies, waits for them, and re-layouts: 6.92 us -> 1.94 us
  starting transfers between devices: 46.6 us -> 43.1 us
  blocking collectives: 75.5 us -> 77.6 us
  Pallas kernels: 9.54 us -> 7.58 us
    ppermute x5 -> x3, waiting for transfers between devices: 9.4 us -> 0.01 us  [the longest x1 0.01 us: shards(): partner = lax.ppermute(weight, 'yh', [(0, 1), (1, 0)])]
    ppermute x5 -> x3, starting transfers between devices: 19.9 us -> 12.4 us  [the longest x1 4.76 us: shards(): partner = lax.ppermute(weight, 'yh', [(0, 1), (1, 0)])]
    all_to_all x1, waiting for transfers between devices: 5.07 us -> 0.01 us  [shards(): own_t = lax.all_to_all(split, ('x', 'yl'), 0, 0).reshape(16 * rows, quarter)]
    unnamed x23 -> x19, local copies, waits for them, and re-layouts: 6.04 us -> 1.09 us
    all_gather x1 -> x2, blocking collectives: 62.5 us -> 66.5 us  [the longest x1 40.8 us: shards(): w_own = lax.all_gather(weight, z, axis=0, tiled=True)]
    ppermute x1, starting transfers between devices: 5.45 us -> 9.45 us  [shards(): other_t = lax.ppermute(own_t, 'c', [(0, 1), (1, 0)])]
    all_to_all x1, waiting for transfers between devices: 4.21 us -> 8.11 us  [shards(): parts = lax.all_to_all(partial, 'x', 0, 0)]
    ppermute x1, waiting for transfers between devices: 2.63 us -> 0.01 us  [shards(): other_t = lax.ppermute(own_t, 'c', [(0, 1), (1, 0)])]
  transfers between devices with their start and end apart: 10 -> 8, of which waited for: 8 -> 3; matrix products, arithmetic and copies ran while one was open for 1% -> 1% of each run, Pallas kernels for 0% -> 0%
where the time goes in v4:
time: 149 us
  blocking collectives  77.6 us (52%)
  starting transfers between devices  43.1 us (29%)
  waiting for transfers between devices  16.3 us (11%)
  Pallas kernels  7.58 us (5%)
  local copies, waits for them, and re-layouts  1.94 us (1%)
    all_gather x1, blocking collectives, shards(): w_own = lax.all_gather(weight, z, axis=0, tiled=True)  40.8 us
    all_gather x1, blocking collectives, shards(): w_other = lax.all_gather(partner, z, axis=0, tiled=True)  25.7 us
    all_gather x1, blocking collectives, shards(): lax.all_gather(jnp.stack([positions, offsets]), ('yl', 'c'), axis=1, tile...  11.1 us
    ppermute x1, starting transfers between devices, shards(): other_t = lax.ppermute(own_t, 'c', [(0, 1), (1, 0)])  9.45 us
    all_to_all x1, starting transfers between devices, shards(): own_t = lax.all_to_all(split, ('x', 'yl'), 0, 0).reshape(16 * rows, quarter)  8.12 us
    all_to_all x1, waiting for transfers between devices, shards(): parts = lax.all_to_all(partial, 'x', 0, 0)  8.11 us
    all_to_all x1, waiting for transfers between devices, shards(): own_s = lax.all_to_all(s_proj, 'yl', 0, 0)  7.22 us
    ppermute x1, starting transfers between devices, shards(): partner = lax.ppermute(weight, 'yh', [(0, 1), (1, 0)])  4.76 us
  transfers between devices with their start and end apart: 8, of which 3 were waited for; matrix products, arithmetic and copies ran while one was open for 1% of the time, Pallas kernels for 0%

profile of v4, /device:TPU:1, one launch (start us, length us, event | category | flops | bytes accessed | tf_op | source)
XLA Modules:
  0.0 148.6 jit_solution(13850836342320887110)
XLA Ops:
  0.6 1.0 copy-done
  1.6 1.7 %permute_columns.1 = bf16[16,32,1280]{2,1,0:T(8,128)(2,1)} custom-call(bf16[32,5120]{1,0:T(8,128)(2,1)S(1)} %copy-done), custom_call_target="tpu_custom_call" | custom-call | tf_op jit(solution)/shard_map/permute_columns/pallas_call | solution.py:106
  3.3 8.1 %all-to-all-start = ((bf16[16,32,1280]{2,1,0:T(8,128)(2,1)}), bf16[16,32,1280]{2,1,0:T(8,128)(2,1)S(1)}, u32[]{:S(2)}, u32[]{:S(2)}) async-start(bf16[16,32,1280]{2,1,0:T(8,128)(2,1)} %permute_columns.1), calls=%async_computation | async-start | bytes 2621440 | tf_op jit(solution)/shard_map/all_to_all | solution.py:115
  11.5 4.8 %collective-permute-start = (bf16[40,640]{1,0:T(8,128)(2,1)S(1)}, bf16[40,640]{1,0:T(8,128)(2,1)S(1)}, u32[]{:S(2)}, u32[]{:S(2)}) collective-permute-start(bf16[40,640]{1,0:T(8,128)(2,1)S(1)} %constant_dynamic-update-slice_fusion), channel_id=1, source_target_pairs={{0,32},{32,0},{1,33},{33,1},{2,34},{34,2},{3,35},{35,3},{4,36},{36... | collective-permute-start | bytes 153608 | tf_op jit(solution)/shard_map/ppermute | solution.py:120
  16.3 40.8 %all_gather.9.w_own_ref = bf16[640,640]{1,0:T(8,128)(2,1)S(1)} all-gather(bf16[40,640]{1,0:T(8,128)(2,1)S(1)} %constant_dynamic-update-slice_fusion), channel_id=1, replica_groups=mesh['zh'=4,'zl'=4,'yh'=2,'x'=4,'yl'=4,'c'=2] {'zh','zl'}, dimensions={0}, use_global_device_ids=true | all-gather | bytes 870400 | tf_op jit(solution)/shard_map/all_gather | solution.py:121
  57.1 0.0 collective-permute-done
  57.1 0.0 all-to-all-done
  57.1 9.4 %collective-permute-start.1 = (bf16[512,1280]{1,0:T(8,128)(2,1)S(1)}, bf16[512,1280]{1,0:T(8,128)(2,1)S(1)}, u32[]{:S(2)}, u32[]{:S(2)}) collective-permute-start(bf16[512,1280]{1,0:T(8,128)(2,1)S(1)} %bitcast.14), channel_id=1, source_target_pairs={{0,1},{1,0},{2,3},{3,2},{4,5},{5,4},{6,7},{7,6},{8,9},{9,8},{10,11... | collective-permute-start | bytes 3932168 | tf_op jit(solution)/shard_map/ppermute | solution.py:124
  66.5 0.1 pad_add_fusion.place_ref
  66.6 4.3 %collective-permute-start.2 = (bf16[16,1280]{1,0:T(8,128)(2,1)S(1)}, bf16[16,1280]{1,0:T(8,128)(2,1)S(1)}, u32[]{:S(2)}, u32[]{:S(2)}) collective-permute-start(bf16[16,1280]{1,0:T(8,128)(2,1)S(1)} %slice.12), channel_id=1, source_target_pairs={{1,32},{33,64},{65,96},{97,128},{129,160},{161,192},{193,224},{225... | collective-permute-start | bytes 122888 | tf_op jit(solution)/shard_map/ppermute | solution.py:127
  70.9 3.3 %collective-permute-start.3 = (bf16[16,1280]{1,0:T(8,128)(2,1)S(1)}, bf16[16,1280]{1,0:T(8,128)(2,1)S(1)}, u32[]{:S(2)}, u32[]{:S(2)}) collective-permute-start(bf16[16,1280]{1,0:T(8,128)(2,1)S(1)} %slice.12), channel_id=1, source_target_pairs={{1,33},{33,65},{65,97},{97,129},{129,161},{161,193},{193,225},{225... | collective-permute-start | bytes 122888 | tf_op jit(solution)/shard_map/ppermute | solution.py:127
  74.2 25.7 %all_gather.10.w_other_ref = bf16[640,640]{1,0:T(8,128)(2,1)S(1)} all-gather(bf16[40,640]{1,0:T(8,128)(2,1)S(1)} %collective-permute-done), channel_id=1, replica_groups=mesh['zh'=4,'zl'=4,'yh'=2,'x'=4,'yl'=4,'c'=2] {'zh','zl'}, dimensions={0}, use_global_device_ids=true | all-gather | bytes 870400 | tf_op jit(solution)/shard_map/all_gather | solution.py:130
  100.0 0.0 collective-permute-done.2
  100.0 0.0 collective-permute-done.3
  100.0 0.0 collective-permute-done.1.other_ref
  100.0 4.3 %partial_products.1 = bf16[4,272,640]{2,1,0:T(8,128)(2,1)} custom-call(s32[2]{0:T(128)S(1)} %pad_add_fusion.place_ref, bf16[512,1280]{1,0:T(8,128)(2,1)S(1)} %bitcast.16, bf16[512,1280]{1,0:T(8,128)(2,1)S(1)} %collective-permute-done.1.other_ref, bf16[16,1280]{1,0:T(8,128)(2,1)S(1)} %add.22.tail_ref, bf16[640,640]{1,0:T(8,128)(2,1)S(1)} %all_gather.9.w_own_ref, ...), custom_call_target="tpu_custom_call" | custom-call | tf_op jit(solution)/shard_map/partial_products/pallas_call | solution.py:145
  104.3 4.5 %all-to-all-start.1 = ((bf16[4,272,640]{2,1,0:T(8,128)(2,1)}), bf16[4,272,640]{2,1,0:T(8,128)(2,1)S(1)}, u32[]{:S(2)}, u32[]{:S(2)}) async-start(bf16[4,272,640]{2,1,0:T(8,128)(2,1)} %partial_products.1), calls=%async_computation.1 | async-start | bytes 2785280 | tf_op jit(solution)/shard_map/all_to_all | solution.py:155
  108.8 11.1 %all-gather = s32[8,32,2]{1,2,0:T(2,128)S(1)} all-gather(s32[1,32,2]{1,2,0:T(2,128)S(1)} %add_bitcast_fusion), channel_id=1, replica_groups=mesh['zh'=4,'zl'=4,'yh'=2,'x'=4,'yl'=4,'c'=2] {'yl','c'}, dimensions={0}, use_global_device_ids=true | all-gather | bytes 2304 | tf_op jit(solution)/shard_map/all_gather | solution.py:133
  119.9 0.1 reshape.37
  120.0 8.1 %all-to-all-done.1 = bf16[4,272,640]{2,1,0:T(8,128)(2,1)S(1)} async-done(((bf16[4,272,640]{2,1,0:T(8,128)(2,1)}), bf16[4,272,640]{2,1,0:T(8,128)(2,1)S(1)}, u32[]{:S(2)}, u32[]{:S(2)}) %all-to-all-start.1) | async-done | bytes 1392672 | tf_op jit(solution)/shard_map/all_to_all | solution.py:155
  128.1 0.4 reduce_sum.12.proj_ref
  128.5 0.0 copy-start.1
  128.5 0.0 copy-start.2
  128.5 0.7 broadcast_in_dim.4
  129.3 4.3 %all-to-all-start.2 = ((bf16[4,272,128]{2,1,0:T(8,128)(2,1)}), bf16[4,272,128]{2,1,0:T(8,128)(2,1)S(1)}, u32[]{:S(2)}, u32[]{:S(2)}) async-start(bf16[4,272,128]{2,1,0:T(8,128)(2,1)} %broadcast_in_dim.4), calls=%async_computation.2 | async-start | bytes 557056 | tf_op jit(solution)/shard_map/all_to_all | solution.py:159
  133.5 0.5 fusion
  134.1 7.2 %all-to-all-done.2.own_ref = bf16[4,272,128]{2,1,0:T(8,128)(2,1)S(1)} async-done(((bf16[4,272,128]{2,1,0:T(8,128)(2,1)}), bf16[4,272,128]{2,1,0:T(8,128)(2,1)S(1)}, u32[]{:S(2)}, u32[]{:S(2)}) %all-to-all-start.2) | async-done | bytes 278560 | tf_op jit(solution)/shard_map/all_to_all | solution.py:159
  141.3 4.4 %collective-permute-start.4 = (bf16[4,272,128]{2,1,0:T(8,128)(2,1)S(1)}, bf16[4,272,128]{2,1,0:T(8,128)(2,1)S(1)}, u32[]{:S(2)}, u32[]{:S(2)}) collective-permute-start(bf16[4,272,128]{2,1,0:T(8,128)(2,1)S(1)} %all-to-all-done.2.own_ref), channel_id=1, source_target_pairs={{0,1},{1,0},{2,3},{3,2},{4,5},{5,4},{6,7},{7,6},{8,9},{9,8},{10,11... | collective-permute-start | bytes 835592 | tf_op jit(solution)/shard_map/ppermute | solution.py:160
  145.7 0.1 pad_maximum_fusion
  145.8 1.0 collective-permute-done.4.other_ref
  146.8 0.1 broadcast_in_dim.5.rel_ref
  146.9 1.6 %rotate_and_convolve.1 = (bf16[256,256]{1,0:T(8,128)(2,1)}, bf16[256,512]{1,0:T(8,128)(2,1)}, bf16[256,256]{1,0:T(8,128)(2,1)}, bf16[256,512]{1,0:T(8,128)(2,1)}) custom-call(s32[1]{0:T(128)} %bitcast.core_ref, bf16[272,640]{1,0:T(8,128)(2,1)S(1)} %reduce_sum.12.proj_ref, bf16[4,272,128]{2,1,0:T(8,128)(2,1)S(1)} %all-to-all-done.2.own_ref, ...), custom_call_target="tpu_custom_call" | custom-call | tf_op jit(solution)/shard_map/rotate_and_convolve/pallas_call | solution.py:162
  (24 shorter events, 0.1 us)
Async XLA Ops:
  0.6 1.0 copy-start
  3.3 8.1 %copy-start.3 = (bf16[40,256]{1,0:T(8,128)(2,1)S(1)}, bf16[40,256]{1,0:T(8,128)(2,1)}, u32[]{:S(2)}) copy-start(bf16[40,256]{1,0:T(8,128)(2,1)} %param.11) | copy-start | bytes 61444
  3.3 8.2 %copy-start.4 = (bf16[40,256]{1,0:T(8,128)(2,1)S(1)}, bf16[40,256]{1,0:T(8,128)(2,1)}, u32[]{:S(2)}) copy-start(bf16[40,256]{1,0:T(8,128)(2,1)} %param.12) | copy-start | bytes 61444
  3.3 8.2 %copy-start.5 = (bf16[40,128]{1,0:T(8,128)(2,1)S(1)}, bf16[40,128]{1,0:T(8,128)(2,1)}, u32[]{:S(2)}) copy-start(bf16[40,128]{1,0:T(8,128)(2,1)} %param.13) | copy-start | bytes 30724
  3.3 53.8 %all-to-all-start = ((bf16[16,32,1280]{2,1,0:T(8,128)(2,1)}), bf16[16,32,1280]{2,1,0:T(8,128)(2,1)S(1)}, u32[]{:S(2)}, u32[]{:S(2)}) async-start(bf16[16,32,1280]{2,1,0:T(8,128)(2,1)} %permute_columns.1), calls=%async_computation | async-start | bytes 2621440 | tf_op jit(solution)/shard_map/all_to_all | solution.py:115
  11.5 45.6 %collective-permute-start = (bf16[40,640]{1,0:T(8,128)(2,1)S(1)}, bf16[40,640]{1,0:T(8,128)(2,1)S(1)}, u32[]{:S(2)}, u32[]{:S(2)}) collective-permute-start(bf16[40,640]{1,0:T(8,128)(2,1)S(1)} %constant_dynamic-update-slice_fusion), channel_id=1, source_target_pairs={{0,32},{32,0},{1,33},{33,1},{2,34},{34,2},{3,35},{35,3},{4,36},{36... | collective-permute-start | bytes 153608 | tf_op jit(solution)/shard_map/ppermute | solution.py:120
  57.1 42.9 %collective-permute-start.1 = (bf16[512,1280]{1,0:T(8,128)(2,1)S(1)}, bf16[512,1280]{1,0:T(8,128)(2,1)S(1)}, u32[]{:S(2)}, u32[]{:S(2)}) collective-permute-start(bf16[512,1280]{1,0:T(8,128)(2,1)S(1)} %bitcast.14), channel_id=1, source_target_pairs={{0,1},{1,0},{2,3},{3,2},{4,5},{5,4},{6,7},{7,6},{8,9},{9,8},{10,11... | collective-permute-start | bytes 3932168 | tf_op jit(solution)/shard_map/ppermute | solution.py:124
  66.6 33.4 %collective-permute-start.2 = (bf16[16,1280]{1,0:T(8,128)(2,1)S(1)}, bf16[16,1280]{1,0:T(8,128)(2,1)S(1)}, u32[]{:S(2)}, u32[]{:S(2)}) collective-permute-start(bf16[16,1280]{1,0:T(8,128)(2,1)S(1)} %slice.12), channel_id=1, source_target_pairs={{1,32},{33,64},{65,96},{97,128},{129,160},{161,192},{193,224},{225... | collective-permute-start | bytes 122888 | tf_op jit(solution)/shard_map/ppermute | solution.py:127
  70.9 29.1 %collective-permute-start.3 = (bf16[16,1280]{1,0:T(8,128)(2,1)S(1)}, bf16[16,1280]{1,0:T(8,128)(2,1)S(1)}, u32[]{:S(2)}, u32[]{:S(2)}) collective-permute-start(bf16[16,1280]{1,0:T(8,128)(2,1)S(1)} %slice.12), channel_id=1, source_target_pairs={{1,33},{33,65},{65,97},{97,129},{129,161},{161,193},{193,225},{225... | collective-permute-start | bytes 122888 | tf_op jit(solution)/shard_map/ppermute | solution.py:127
  104.3 4.5 %copy-start.6 = (s32[32]{0:T(128)S(1)}, s32[32]{0:T(128)}, u32[]{:S(2)}) copy-start(s32[32]{0:T(128)} %param.10) | copy-start | bytes 388
  104.3 4.5 %copy-start.7 = (s32[32]{0:T(128)S(1)}, s32[32]{0:T(128)}, u32[]{:S(2)}) copy-start(s32[32]{0:T(128)} %param.9) | copy-start | bytes 388
  104.3 23.8 %all-to-all-start.1 = ((bf16[4,272,640]{2,1,0:T(8,128)(2,1)}), bf16[4,272,640]{2,1,0:T(8,128)(2,1)S(1)}, u32[]{:S(2)}, u32[]{:S(2)}) async-start(bf16[4,272,640]{2,1,0:T(8,128)(2,1)} %partial_products.1), calls=%async_computation.1 | async-start | bytes 2785280 | tf_op jit(solution)/shard_map/all_to_all | solution.py:155
  128.5 18.4 %copy-start.1 = (f32[4,512]{1,0:T(4,128)S(1)}, f32[4,512]{1,0:T(4,128)}, u32[]{:S(2)}) copy-start(f32[4,512]{1,0:T(4,128)} %tbc_ref.1) | copy-start | bytes 24580
  128.5 18.4 %copy-start.2 = (f32[4,256]{1,0:T(4,128)S(1)}, f32[4,256]{1,0:T(4,128)}, u32[]{:S(2)}) copy-start(f32[4,256]{1,0:T(4,128)} %tx_ref.1) | copy-start | bytes 12292
  129.3 12.0 %all-to-all-start.2 = ((bf16[4,272,128]{2,1,0:T(8,128)(2,1)}), bf16[4,272,128]{2,1,0:T(8,128)(2,1)S(1)}, u32[]{:S(2)}, u32[]{:S(2)}) async-start(bf16[4,272,128]{2,1,0:T(8,128)(2,1)} %broadcast_in_dim.4), calls=%async_computation.2 | async-start | bytes 557056 | tf_op jit(solution)/shard_map/all_to_all | solution.py:159
  141.3 5.5 %collective-permute-start.4 = (bf16[4,272,128]{2,1,0:T(8,128)(2,1)S(1)}, bf16[4,272,128]{2,1,0:T(8,128)(2,1)S(1)}, u32[]{:S(2)}, u32[]{:S(2)}) collective-permute-start(bf16[4,272,128]{2,1,0:T(8,128)(2,1)S(1)} %all-to-all-done.2.own_ref), channel_id=1, source_target_pairs={{0,1},{1,0},{2,3},{3,2},{4,5},{5,4},{6,7},{7,6},{8,9},{9,8},{10,11... | collective-permute-start | bytes 835592 | tf_op jit(solution)/shard_map/ppermute | solution.py:160

commit v5 on v4

v5 whole, which is shorter than its diff:
```python
import jax
import jax.numpy as jnp
from jax import lax
from jax.experimental import pallas as pl
from jax.experimental.pallas import tpu as pltpu
from jax.sharding import Mesh, PartitionSpec as P

HD = 128
HALO = 16
rope_base = 10000.0

AXES = ("zh", "zl", "yh", "x", "yl", "c")
SIZES = (4, 4, 2, 4, 4, 2)
FSDP = AXES[:4]


def permute_kernel(tokens_ref, extra_ref, out_ref, stack_ref):
    for p in range(8):
        stack_ref[p * 32 : (p + 1) * 32, :] = tokens_ref[:, p * 640 : (p + 1) * 640]
    source = lax.broadcasted_iota(jnp.int32, (640, 640), 0)
    target = lax.broadcasted_iota(jnp.int32, (640, 640), 1)
    wanted = target // 40 % 4 * 160 + target // 160 * 40 + target % 40
    pick = jnp.where(source == wanted, 1.0, 0.0).astype(jnp.bfloat16)
    moved = jnp.dot(stack_ref[...], pick, preferred_element_type=jnp.float32)
    for x in range(4):
        piece = jnp.concatenate(
            [moved[p * 32 : (p + 1) * 32, x * 160 : (x + 1) * 160] for p in range(8)], axis=1
        ).astype(jnp.bfloat16)
        for yl in range(4):
            out_ref[x * 4 + yl, :, 0:1280] = piece
            out_ref[x * 4 + yl, :, 1280:] = extra_ref[...]


def partial_kernel(core_ref, own_ref, other_ref, *refs):
    tail_ref, w_ref, out_ref = refs if len(refs) == 3 else (None,) + refs
    core = core_ref[0]
    width, columns = w_ref.shape
    lead = 0 if tail_ref is None else HALO
    for first in range(0, columns, 256):
        cols = slice(first, min(first + 256, columns))
        for mine in (True, False):
            rows = (own_ref if mine else other_ref)[:, 0:width]
            if lead and not mine:
                rows = jnp.concatenate([rows, tail_ref[...]], axis=0)
            part = jnp.dot(rows, w_ref[:, cols], preferred_element_type=jnp.float32).astype(jnp.bfloat16)
            place = core if mine else 1 - core
            for x in range(4):
                for yl in range(4):
                    at = pl.multiple_of(lead + yl * 64 + place * 32, 16)
                    out_ref[x, pl.ds(at, 32), cols] = part[(x * 4 + yl) * 32 : (x * 4 + yl + 1) * 32]
            if lead and not mine:
                out_ref[0, 0:HALO, cols] = part[512 : 512 + HALO]
    if lead:
        for x in range(3):
            out_ref[x + 1, 0:HALO, :] = out_ref[x, 256 : 256 + HALO, :]


def final_kernel(
    qparts_ref, xs_ref, s_ref, cos_ref, sin_ref, rel_ref, tx_ref, tbc_ref, q_ref, k_ref, x_ref, bc_ref, ext_ref
):
    rows = q_ref.shape[0]
    cosine = cos_ref[...]
    sine = sin_ref[...]

    def turned(values):
        values = values.astype(jnp.float32)
        return (values * cosine + pltpu.roll(values, HD // 2, 1) * sine).astype(jnp.bfloat16)

    def convolved(taps_ref, cols):
        taps = taps_ref[:, cols]
        total = ext_ref[pl.ds(HALO, rows), :] * taps[0:1]
        for step_back in range(1, 4):
            window = ext_ref[pl.ds(HALO - step_back, rows), :] * taps[step_back : step_back + 1]
            total = total + jnp.where(rel_ref[...] >= step_back, window, 0.0)
        return (total / (1.0 + jnp.exp(-total))).astype(jnp.bfloat16)

    for block in range(2):
        cols = slice(block * HD, (block + 1) * HD)
        total = qparts_ref[0, :, cols].astype(jnp.float32)
        for x in range(1, 4):
            total = total + qparts_ref[x, :, cols].astype(jnp.float32)
        q_ref[:, cols] = turned(total.astype(jnp.bfloat16))
        ext_ref[...] = xs_ref[:, cols].astype(jnp.float32)
        x_ref[:, cols] = convolved(tx_ref, cols)
    for block in range(4):
        cols = slice(block * HD, (block + 1) * HD)
        k_ref[:, cols] = turned(s_ref[block, HALO:, :])
        ext_ref[...] = s_ref[4 + block].astype(jnp.float32)
        bc_ref[:, cols] = convolved(tbc_ref, cols)


def shards(tokens, positions, offsets, q_weight, x_weight, shared_weight, conv_x, conv_bc):
    bf16 = jnp.bfloat16
    rows, width = tokens.shape
    quarter = width // 4
    group_rows = 8 * rows
    vmem = pl.BlockSpec(memory_space=pltpu.VMEM)
    smem = pl.BlockSpec(memory_space=pltpu.SMEM)
    params = pltpu.CompilerParams(vmem_limit_bytes=40 * 2**20)
    core = lax.axis_index("c").astype(jnp.int32)
    z = ("zh", "zl")

    weight = jnp.concatenate([q_weight, x_weight, shared_weight], axis=1)
    partner = lax.ppermute(weight, "yh", [(0, 1), (1, 0)])

    extra = jnp.stack([positions >> 8, positions & 255, offsets >> 8, offsets & 255], axis=1)
    extra = jnp.pad(extra, ((0, 0), (0, HD - 4))).astype(bf16)
    split = pl.pallas_call(
        permute_kernel,
        out_shape=jax.ShapeDtypeStruct((16, rows, quarter + HD), bf16),
        in_specs=[vmem, vmem],
        out_specs=vmem,
        scratch_shapes=[pltpu.VMEM((8 * rows, width // 8), bf16)],
        compiler_params=params,
        name="permute_columns",
    )(tokens, extra)
    split, partner = lax.optimization_barrier((split, partner))
    own_t = lax.all_to_all(split, ("x", "yl"), 0, 0).reshape(16 * rows, quarter + HD)

    low = lax.axis_index("yh") == 0
    pair = jnp.concatenate([jnp.where(low, weight, partner), jnp.where(low, partner, weight)], axis=0)

    w_xs = lax.all_gather(pair[:, 256:], z, axis=0, tiled=True)
    own_t, w_xs = lax.optimization_barrier((own_t, w_xs))
    other_t = lax.ppermute(own_t, "c", [(0, 1), (1, 0)])
    tail = own_t[16 * rows - HALO :, :quarter]
    sources = [(2 * i + 1, 2 * i + 2) for i in range(31)]
    tail = lax.ppermute(tail, ("zh", "zl", "yh", "c"), sources) + lax.ppermute(
        tail, ("zh", "zl", "yh", "c"), [(source, target + 1) for source, target in sources]
    )

    def partial(name, lead, operands):
        return pl.pallas_call(
            partial_kernel,
            out_shape=jax.ShapeDtypeStruct((4, lead + group_rows, operands[-1].shape[1]), bf16),
            in_specs=[smem] + [vmem] * len(operands),
            out_specs=vmem,
            compiler_params=params,
            name=name,
        )(core.reshape(1), *operands)

    xs_part = partial("partial_xs", HALO, (own_t, other_t, tail, w_xs))
    pair_q, xs_part = lax.optimization_barrier((pair[:, :256], xs_part))
    xs_parts = lax.all_to_all(xs_part, "x", 0, 0)
    w_q = lax.all_gather(pair_q, z, axis=0, tiled=True)
    xs_parts, w_q = lax.optimization_barrier((xs_parts, w_q))
    q_part = partial("partial_q", 0, (own_t, other_t, w_q))
    q_parts = lax.all_to_all(q_part, "x", 0, 0)

    xs = jnp.sum(xs_parts.astype(jnp.float32), axis=0).astype(bf16)
    s_own, _ = lax.optimization_barrier((xs[:, 256:], q_part))
    s_all = lax.all_gather(s_own, ("yl", "c"), axis=0)
    q_parts, s_all = lax.optimization_barrier((q_parts, s_all))

    at = lax.axis_index("x") * (4 * rows)
    near = lax.dynamic_slice(own_t, (at, quarter), (4 * rows, HD)).reshape(4, 1, rows, HD)
    far = lax.dynamic_slice(other_t, (at, quarter), (4 * rows, HD)).reshape(4, 1, rows, HD)
    first = jnp.where(core == 0, near, far)
    second = jnp.where(core == 0, far, near)
    places = jnp.concatenate([first, second], axis=1).reshape(group_rows, HD)[:, :4].astype(jnp.float32)
    half = HD // 2
    index = jnp.arange(half, dtype=jnp.float32)
    inverse = jnp.exp(-jnp.log(jnp.float32(rope_base)) * index / jnp.float32(half))
    angle = (places[:, 0] * 256.0 + places[:, 1])[:, None] * inverse[None, :]
    cosine, sine = jnp.cos(angle), jnp.sin(angle)
    cosine = jnp.concatenate([cosine, cosine], axis=1)
    sine = jnp.concatenate([-sine, sine], axis=1)
    starts = (places[:, 2] * 256.0 + places[:, 3]).astype(jnp.int32)
    row_ids = lax.axis_index(FSDP) * group_rows + jnp.arange(group_rows, dtype=jnp.int32)
    rel = jnp.broadcast_to((row_ids - starts)[:, None], (group_rows, HD))

    return pl.pallas_call(
        final_kernel,
        out_shape=(
            jax.ShapeDtypeStruct((group_rows, 256), bf16),
            jax.ShapeDtypeStruct((group_rows, 512), bf16),
            jax.ShapeDtypeStruct((group_rows, 256), bf16),
            jax.ShapeDtypeStruct((group_rows, 512), bf16),
        ),
        in_specs=[vmem] * 8,
        out_specs=(vmem,) * 4,
        scratch_shapes=[pltpu.VMEM((group_rows + HALO, HD), jnp.float32)],
        compiler_params=params,
        name="rotate_and_convolve",
    )(q_parts, xs, s_all, cosine, sine, rel, conv_x, conv_bc)


def solution(mesh):
    chips = Mesh(mesh.devices.reshape(SIZES), AXES)
    head = ("yl", "c")
    in_specs = (
        P(AXES, None), P(AXES), P(AXES),
        P(FSDP, head), P(FSDP, head), P(FSDP, head),
        P(None, head), P(),
    )
    out_specs = (P(FSDP, head), P(FSDP, None), P(FSDP, head), P(FSDP, None))
    return jax.shard_map(shards, mesh=chips, in_specs=in_specs, out_specs=out_specs, check_vma=False)
```

time: 149 us -> 152 us (1.020)
  waiting for transfers between devices: 16.3 us -> 0.47 us
  blocking collectives: 77.6 us -> 92.7 us
  other arithmetic: 1.15 us -> 6.27 us
  local copies, waits for them, and re-layouts: 1.94 us -> 6.3 us
  starting transfers between devices: 43.1 us -> 39.1 us
  Pallas kernels: 7.58 us -> 5.79 us
    all_to_all x3, waiting for transfers between devices: 15.3 us -> 0.01 us  [the longest x1 0.01 us: shards(): xs_parts = lax.all_to_all(xs_part, 'x', 0, 0)]
    all_gather x3, blocking collectives: 77.6 us -> 92.7 us  [the longest x1 44.3 us: shards(): w_xs = lax.all_gather(pair[:, 256:], z, axis=0, tiled=True)]
    ppermute x1 -> x0, starting transfers between devices: 4.36 us -> none  [shards(): other_s = lax.ppermute(own_s, 'c', [(0, 1), (1, 0)])]
    unnamed x19 -> x20, local copies, waits for them, and re-layouts: 1.09 us -> 5.38 us
    all_to_all x3, starting transfers between devices: 16.9 us -> 13.2 us  [the longest x1 5.45 us: shards(): lax.all_to_all(split, ('x', 'yl'), 0, 0).reshape(16 * rows, quarter + HD)]
    ppermute x1, starting transfers between devices: 4.76 us -> 8.27 us  [shards(): partner = lax.ppermute(weight, 'yh', [(0, 1), (1, 0)])]
    pallas_call x1 -> x2, Pallas kernels: 4.26 us -> 2.43 us  [partial(): pl.pallas_call(partial_kernel, out_shape=jax.ShapeDtypeStruct((4, lead +...]
    concatenate x0 -> x4, other arithmetic: none -> 1.77 us  [the longest x1 1.13 us: shards(): sine = jnp.concatenate([-sine, sine], axis=1)]
  transfers between devices with their start and end apart: 8 -> 7, of which waited for: 3 -> 1; matrix products, arithmetic and copies ran while one was open for 1% -> 4% of each run, Pallas kernels for 0% -> 1%
where the time goes in v5:
time: 152 us
  blocking collectives  92.7 us (61%)
  starting transfers between devices  39.1 us (26%)
  local copies, waits for them, and re-layouts  6.3 us (4%)
  other arithmetic  6.27 us (4%)
  Pallas kernels  5.79 us (4%)
    all_gather x1, blocking collectives, shards(): w_xs = lax.all_gather(pair[:, 256:], z, axis=0, tiled=True)  44.3 us
    all_gather x1, blocking collectives, shards(): w_q = lax.all_gather(pair_q, z, axis=0, tiled=True)  30.4 us
    all_gather x1, blocking collectives, shards(): s_all = lax.all_gather(s_own, ('yl', 'c'), axis=0)  18 us
    ppermute x1, starting transfers between devices, shards(): other_t = lax.ppermute(own_t, 'c', [(0, 1), (1, 0)])  9.67 us
    ppermute x1, starting transfers between devices, shards(): partner = lax.ppermute(weight, 'yh', [(0, 1), (1, 0)])  8.27 us
    all_to_all x1, starting transfers between devices, shards(): lax.all_to_all(split, ('x', 'yl'), 0, 0).reshape(16 * rows, quarter + HD)  5.45 us
    unnamed x20, local copies, waits for them, and re-layouts  5.38 us
    ppermute x1, starting transfers between devices, shards(): lax.ppermute(tail, ('zh', 'zl', 'yh', 'c'), sources)  5.37 us
  transfers between devices with their start and end apart: 7, of which 1 were waited for; matrix products, arithmetic and copies ran while one was open for 4% of the time, Pallas kernels for 1%

profile of v5, /device:TPU:1, one launch (start us, length us, event | category | flops | bytes accessed | tf_op | source)
XLA Modules:
  0.0 151.5 jit_solution(3839637918200510423)
XLA Ops:
  0.6 0.7 constant_dynamic-update-slice_fusion.2
  1.4 0.7 constant_dynamic-update-slice_fusion.1
  2.1 0.7 constant_dynamic-update-slice_fusion
  2.8 8.3 %collective-permute-start = (bf16[40,640]{1,0:T(8,128)(2,1)S(1)}, bf16[40,640]{1,0:T(8,128)(2,1)S(1)}, u32[]{:S(2)}, u32[]{:S(2)}) collective-permute-start(bf16[40,640]{1,0:T(8,128)(2,1)S(1)} %constant_dynamic-update-slice_fusion), channel_id=1, source_target_pairs={{0,32},{32,0},{1,33},{33,1},{2,34},{34,2},{3,35},{35,3},{4,36},{36... | collective-permute-start | bytes 153608 | tf_op jit(solution)/shard_map/ppermute | solution.py:104
  11.1 0.7 convert_bitcast_fusion.1
  11.8 0.1 copy.22
  11.9 1.0 copy-done.4
  12.9 1.7 %permute_columns.1 = bf16[16,32,1408]{2,1,0:T(8,128)(2,1)} custom-call(bf16[32,5120]{1,0:T(8,128)(2,1)S(1)} %copy-done.4, bf16[32,128]{1,0:T(8,128)(2,1)S(1)} %pad.5.extra_ref), custom_call_target="tpu_custom_call" | custom-call | tf_op jit(solution)/shard_map/permute_columns/pallas_call | solution.py:108
  14.6 5.4 %all-to-all-start = ((bf16[16,32,1408]{2,1,0:T(8,128)(2,1)}), bf16[16,32,1408]{2,1,0:T(8,128)(2,1)S(1)}, u32[]{:S(2)}, u32[]{:S(2)}) async-start(bf16[16,32,1408]{2,1,0:T(8,128)(2,1)} %permute_columns.1), calls=%async_computation | async-start | bytes 2883584 | tf_op jit(solution)/shard_map/all_to_all | solution.py:118
  20.1 44.3 %all_gather.12.refs_1_ = bf16[1280,384]{1,0:T(8,128)(2,1)} all-gather(bf16[80,384]{1,0:T(8,128)(2,1)S(1)} %fusion.4), channel_id=1, replica_groups=mesh['zh'=4,'zl'=4,'yh'=2,'x'=4,'yl'=4,'c'=2] {'zh','zl'}, dimensions={0}, use_global_device_ids=true | all-gather | bytes 1044480 | tf_op jit(solution)/shard_map/all_gather | solution.py:123
  64.4 9.7 %collective-permute-start.1 = (bf16[512,1408]{1,0:T(8,128)(2,1)S(1)}, bf16[512,1408]{1,0:T(8,128)(2,1)S(1)}, u32[]{:S(2)}, u32[]{:S(2)}) collective-permute-start(bf16[512,1408]{1,0:T(8,128)(2,1)S(1)} %bitcast.18), channel_id=1, source_target_pairs={{0,1},{1,0},{2,3},{3,2},{4,5},{5,4},{6,7},{7,6},{8,9},{9,8},{10,11... | collective-permute-start | bytes 4325384 | tf_op jit(solution)/shard_map/ppermute | solution.py:125
  74.1 5.4 %collective-permute-start.2 = (bf16[16,1280]{1,0:T(8,128)(2,1)S(1)}, bf16[16,1280]{1,0:T(8,128)(2,1)S(1)}, u32[]{:S(2)}, u32[]{:S(2)}) collective-permute-start(bf16[16,1280]{1,0:T(8,128)(2,1)S(1)} %slice.29), channel_id=1, source_target_pairs={{1,32},{33,64},{65,96},{97,128},{129,160},{161,192},{193,224},{225... | collective-permute-start | bytes 122888 | tf_op jit(solution)/shard_map/ppermute | solution.py:128
  79.5 2.6 %collective-permute-start.3 = (bf16[16,1280]{1,0:T(8,128)(2,1)S(1)}, bf16[16,1280]{1,0:T(8,128)(2,1)S(1)}, u32[]{:S(2)}, u32[]{:S(2)}) collective-permute-start(bf16[16,1280]{1,0:T(8,128)(2,1)S(1)} %slice.29), channel_id=1, source_target_pairs={{1,33},{33,65},{65,97},{97,129},{129,161},{161,193},{193,225},{225... | collective-permute-start | bytes 122888 | tf_op jit(solution)/shard_map/ppermute | solution.py:128
  82.0 0.6 pad_maximum_fusion.3
  82.7 0.5 collective-permute-done.3
  83.2 1.2 copy-done
  84.4 1.6 %partial_xs.1 = bf16[4,272,384]{2,1,0:T(8,128)(2,1)S(1)} custom-call(s32[1]{0:T(128)} %bitcast.core_ref, bf16[512,1408]{1,0:T(8,128)(2,1)S(1)} %bitcast.20, bf16[512,1408]{1,0:T(8,128)(2,1)S(1)} %collective-permute-done.1.other_ref, bf16[16,1280]{1,0:T(8,128)(2,1)S(1)} %add.39.refs_0_, bf16[1280,384]{1,0:T(8,128)(2,1)S(1)} %copy-done), custom_call_target="tpu_custom_call" | custom-call | tf_op jit(solution)/shard_map/partial_xs/pallas_call | solution.py:133
  86.0 0.9 copy-done.1
  86.9 4.2 %all-to-all-start.1 = ((bf16[4,272,384]{2,1,0:T(8,128)(2,1)}), bf16[4,272,384]{2,1,0:T(8,128)(2,1)}, u32[]{:S(2)}, u32[]{:S(2)}) async-start(bf16[4,272,384]{2,1,0:T(8,128)(2,1)} %copy-done.1), calls=%async_computation.1 | async-start | bytes 1671168 | tf_op jit(solution)/shard_map/all_to_all | solution.py:144
  91.2 0.2 fusion.3
  91.4 1.2 fusion.5
  92.6 0.8 pad_maximum_fusion.cos_ref
  93.4 30.4 %all_gather.13.refs_0_ = bf16[1280,256]{1,0:T(8,128)(2,1)S(1)} all-gather(bf16[80,256]{1,0:T(8,128)(2,1)} %pad_maximum_fusion.3), channel_id=1, replica_groups=mesh['zh'=4,'zl'=4,'yh'=2,'x'=4,'yl'=4,'c'=2] {'zh','zl'}, dimensions={0}, use_global_device_ids=true | all-gather | bytes 696320 | tf_op jit(solution)/shard_map/all_gather | solution.py:145
  123.7 0.9 partial_q.1
  124.6 0.8 copy-done.2
  125.4 3.6 %all-to-all-start.2 = ((bf16[4,256,256]{2,1,0:T(8,128)(2,1)}), bf16[4,256,256]{2,1,0:T(8,128)(2,1)S(1)}, u32[]{:S(2)}, u32[]{:S(2)}) async-start(bf16[4,256,256]{2,1,0:T(8,128)(2,1)} %copy-done.2), calls=%async_computation.2 | async-start | bytes 1048576 | tf_op jit(solution)/shard_map/all_to_all | solution.py:148
  129.1 1.1 pad_maximum_fusion.1.sin_ref
  130.2 0.2 fusion.2
  130.4 1.3 reduce_sum.12.xs_ref
  131.8 18.0 %all-gather = bf16[2176,128]{1,0:T(8,128)(2,1)S(1)} all-gather(bf16[272,128]{1,0:T(8,128)(2,1)S(1)} %slice.38), channel_id=2, replica_groups=mesh['zh'=4,'zl'=4,'yh'=2,'x'=4,'yl'=4,'c'=2] {'yl','c'}, dimensions={0}, use_global_device_ids=true | all-gather | bytes 626688 | tf_op jit(solution)/shard_map/all_gather | solution.py:152
  149.7 0.1 broadcast_in_dim.5.rel_ref
  149.9 1.7 %rotate_and_convolve.1 = (bf16[256,256]{1,0:T(8,128)(2,1)}, bf16[256,512]{1,0:T(8,128)(2,1)}, bf16[256,256]{1,0:T(8,128)(2,1)}, bf16[256,512]{1,0:T(8,128)(2,1)}) custom-call(bf16[4,256,256]{2,1,0:T(8,128)(2,1)S(1)} %all-to-all-done.2.qparts_ref, bf16[272,384]{1,0:T(8,128)(2,1)S(1)} %reduce_sum.12.xs_ref, bf16[8,272,128]{2,1,0:T(8,128)(2,1)S(1)} %bitcast.23, ...), custom_call_target="tpu_custom_call" | custom-call | tf_op jit(solution)/shard_map/rotate_and_convolve/pallas_call | solution.py:172
  (31 shorter events, 0.2 us)
Async XLA Ops:
  2.8 11.8 %collective-permute-start = (bf16[40,640]{1,0:T(8,128)(2,1)S(1)}, bf16[40,640]{1,0:T(8,128)(2,1)S(1)}, u32[]{:S(2)}, u32[]{:S(2)}) collective-permute-start(bf16[40,640]{1,0:T(8,128)(2,1)S(1)} %constant_dynamic-update-slice_fusion), channel_id=1, source_target_pairs={{0,32},{32,0},{1,33},{33,1},{2,34},{34,2},{3,35},{35,3},{4,36},{36... | collective-permute-start | bytes 153608 | tf_op jit(solution)/shard_map/ppermute | solution.py:104
  11.9 1.0 copy-start.4
  14.6 49.8 %all-to-all-start = ((bf16[16,32,1408]{2,1,0:T(8,128)(2,1)}), bf16[16,32,1408]{2,1,0:T(8,128)(2,1)S(1)}, u32[]{:S(2)}, u32[]{:S(2)}) async-start(bf16[16,32,1408]{2,1,0:T(8,128)(2,1)} %permute_columns.1), calls=%async_computation | async-start | bytes 2883584 | tf_op jit(solution)/shard_map/all_to_all | solution.py:118
  64.4 18.8 %collective-permute-start.1 = (bf16[512,1408]{1,0:T(8,128)(2,1)S(1)}, bf16[512,1408]{1,0:T(8,128)(2,1)S(1)}, u32[]{:S(2)}, u32[]{:S(2)}) collective-permute-start(bf16[512,1408]{1,0:T(8,128)(2,1)S(1)} %bitcast.18), channel_id=1, source_target_pairs={{0,1},{1,0},{2,3},{3,2},{4,5},{5,4},{6,7},{7,6},{8,9},{9,8},{10,11... | collective-permute-start | bytes 4325384 | tf_op jit(solution)/shard_map/ppermute | solution.py:125
  74.1 8.6 %collective-permute-start.2 = (bf16[16,1280]{1,0:T(8,128)(2,1)S(1)}, bf16[16,1280]{1,0:T(8,128)(2,1)S(1)}, u32[]{:S(2)}, u32[]{:S(2)}) collective-permute-start(bf16[16,1280]{1,0:T(8,128)(2,1)S(1)} %slice.29), channel_id=1, source_target_pairs={{1,32},{33,64},{65,96},{97,128},{129,160},{161,192},{193,224},{225... | collective-permute-start | bytes 122888 | tf_op jit(solution)/shard_map/ppermute | solution.py:128
  79.5 3.7 %collective-permute-start.3 = (bf16[16,1280]{1,0:T(8,128)(2,1)S(1)}, bf16[16,1280]{1,0:T(8,128)(2,1)S(1)}, u32[]{:S(2)}, u32[]{:S(2)}) collective-permute-start(bf16[16,1280]{1,0:T(8,128)(2,1)S(1)} %slice.29), channel_id=1, source_target_pairs={{1,33},{33,65},{65,97},{97,129},{129,161},{161,193},{193,225},{225... | collective-permute-start | bytes 122888 | tf_op jit(solution)/shard_map/ppermute | solution.py:128
  83.2 1.2 copy-start
  85.9 0.9 copy-start.1
  86.9 36.9 %all-to-all-start.1 = ((bf16[4,272,384]{2,1,0:T(8,128)(2,1)}), bf16[4,272,384]{2,1,0:T(8,128)(2,1)}, u32[]{:S(2)}, u32[]{:S(2)}) async-start(bf16[4,272,384]{2,1,0:T(8,128)(2,1)} %copy-done.1), calls=%async_computation.1 | async-start | bytes 1671168 | tf_op jit(solution)/shard_map/all_to_all | solution.py:144
  91.2 1.4 copy-start.7
  124.6 0.8 copy-start.2
  125.4 4.8 %copy-start.8 = (f32[256,4]{1,0:T(8,128)S(1)}, f32[256,4]{1,0:T(8,128)}, u32[]{:S(2)}) copy-start(f32[256,4]{1,0:T(8,128)} %copy-done.7) | copy-start | bytes 12292
  125.4 24.3 %all-to-all-start.2 = ((bf16[4,256,256]{2,1,0:T(8,128)(2,1)}), bf16[4,256,256]{2,1,0:T(8,128)(2,1)S(1)}, u32[]{:S(2)}, u32[]{:S(2)}) async-start(bf16[4,256,256]{2,1,0:T(8,128)(2,1)} %copy-done.2), calls=%async_computation.2 | async-start | bytes 1048576 | tf_op jit(solution)/shard_map/all_to_all | solution.py:148
  129.0 20.8 %copy-start.3 = (f32[256,128]{1,0:T(8,128)S(1)}, f32[256,128]{1,0:T(8,128)}, u32[]{:S(2)}) copy-start(f32[256,128]{1,0:T(8,128)} %pad_maximum_fusion.cos_ref) | copy-start | bytes 393220
  129.0 20.8 %copy-start.5 = (f32[4,512]{1,0:T(4,128)S(1)}, f32[4,512]{1,0:T(4,128)}, u32[]{:S(2)}) copy-start(f32[4,512]{1,0:T(4,128)} %tbc_ref.1) | copy-start | bytes 24580
  129.0 20.8 %copy-start.6 = (f32[4,256]{1,0:T(4,128)S(1)}, f32[4,256]{1,0:T(4,128)}, u32[]{:S(2)}) copy-start(f32[4,256]{1,0:T(4,128)} %tx_ref.1) | copy-start | bytes 12292

commit v6 on v5

v6 whole, which is shorter than its diff:
```python
import functools

import jax
import jax.numpy as jnp
from jax import lax
from jax.experimental import pallas as pl
from jax.experimental.pallas import tpu as pltpu
from jax.sharding import Mesh, PartitionSpec as P

HD = 128
HALO = 16
rope_base = 10000.0

AXES = ("zh", "zl", "yh", "x", "yl", "c")
SIZES = (4, 4, 2, 4, 4, 2)
FSDP = AXES[:4]


def permute_kernel(tokens_ref, extra_ref, out_ref, stack_ref):
    for p in range(8):
        stack_ref[p * 32 : (p + 1) * 32, :] = tokens_ref[:, p * 640 : (p + 1) * 640]
    source = lax.broadcasted_iota(jnp.int32, (640, 640), 0)
    target = lax.broadcasted_iota(jnp.int32, (640, 640), 1)
    wanted = target // 40 % 2 * 320 + target // 80 % 2 * 160 + target // 160 * 40 + target % 40
    pick = jnp.where(source == wanted, 1.0, 0.0).astype(jnp.bfloat16)
    moved = jnp.dot(stack_ref[...], pick, preferred_element_type=jnp.float32)
    for x in range(4):
        piece = jnp.concatenate(
            [
                moved[p * 32 : (p + 1) * 32, x * 160 + yh * 80 : x * 160 + (yh + 1) * 80]
                for yh in range(2)
                for p in range(8)
            ],
            axis=1,
        ).astype(jnp.bfloat16)
        for yl in range(4):
            out_ref[x * 4 + yl, :, 0:1280] = piece
            out_ref[x * 4 + yl, :, 1280:] = extra_ref[...]


def partial_kernel(first, place_ref, own_ref, other_ref, tail_ref, w_own_ref, w_other_ref, out_ref):
    core, yh = place_ref[0], place_ref[1]
    half = w_own_ref.shape[0]
    near = pl.ds(pl.multiple_of(yh * half, 128), half)
    far = pl.ds(pl.multiple_of((1 - yh) * half, 128), half)
    columns = out_ref.shape[2]
    for start in range(0, columns, 256):
        cols = slice(start, min(start + 256, columns))
        w_cols = slice(first + cols.start, first + cols.stop)
        for mine in (True, False):
            part = 0.0
            for at_k, w_ref in ((near, w_own_ref), (far, w_other_ref)):
                rows = (own_ref if mine else other_ref)[:, at_k]
                if not mine:
                    rows = jnp.concatenate([rows, tail_ref[:, at_k]], axis=0)
                part = part + jnp.dot(rows, w_ref[:, w_cols], preferred_element_type=jnp.float32)
            part = part.astype(jnp.bfloat16)
            place = core if mine else 1 - core
            for x in range(4):
                for yl in range(4):
                    at = pl.multiple_of(HALO + yl * 64 + place * 32, 16)
                    out_ref[x, pl.ds(at, 32), cols] = part[(x * 4 + yl) * 32 : (x * 4 + yl + 1) * 32]
            if not mine:
                out_ref[0, 0:HALO, cols] = part[512 : 512 + HALO]
    for x in range(3):
        out_ref[x + 1, 0:HALO, :] = out_ref[x, 256 : 256 + HALO, :]


def final_kernel(
    parts_ref, s_ref, cos_ref, sin_ref, rel_ref, tx_ref, tbc_ref, q_ref, k_ref, x_ref, bc_ref, ext_ref
):
    rows = q_ref.shape[0]
    cosine = cos_ref[...]
    sine = sin_ref[...]

    def turned(values):
        values = values.astype(jnp.float32)
        return (values * cosine + pltpu.roll(values, HD // 2, 1) * sine).astype(jnp.bfloat16)

    def convolved(taps_ref, cols):
        taps = taps_ref[:, cols]
        total = ext_ref[pl.ds(HALO, rows), :] * taps[0:1]
        for step_back in range(1, 4):
            window = ext_ref[pl.ds(HALO - step_back, rows), :] * taps[step_back : step_back + 1]
            total = total + jnp.where(rel_ref[...] >= step_back, window, 0.0)
        return (total / (1.0 + jnp.exp(-total))).astype(jnp.bfloat16)

    def summed(first, cols):
        total = parts_ref[0, first:, cols].astype(jnp.float32)
        for x in range(1, 4):
            total = total + parts_ref[x, first:, cols].astype(jnp.float32)
        return total.astype(jnp.bfloat16)

    for block in range(2):
        cols = slice(block * HD, (block + 1) * HD)
        q_ref[:, cols] = turned(summed(HALO, cols))
        ext_ref[...] = summed(0, slice(256 + block * HD, 256 + (block + 1) * HD)).astype(jnp.float32)
        x_ref[:, cols] = convolved(tx_ref, cols)
    for block in range(4):
        cols = slice(block * HD, (block + 1) * HD)
        k_ref[:, cols] = turned(s_ref[block, HALO:, :])
        ext_ref[...] = s_ref[4 + block].astype(jnp.float32)
        bc_ref[:, cols] = convolved(tbc_ref, cols)


def shards(tokens, positions, offsets, q_weight, x_weight, shared_weight, conv_x, conv_bc):
    bf16 = jnp.bfloat16
    rows, width = tokens.shape
    quarter = width // 4
    group_rows = 8 * rows
    vmem = pl.BlockSpec(memory_space=pltpu.VMEM)
    smem = pl.BlockSpec(memory_space=pltpu.SMEM)
    params = pltpu.CompilerParams(vmem_limit_bytes=40 * 2**20)
    core = lax.axis_index("c").astype(jnp.int32)
    z = ("zh", "zl")

    extra = jnp.stack([positions >> 8, positions & 255, offsets >> 8, offsets & 255], axis=1)
    extra = jnp.pad(extra, ((0, 0), (0, HD - 4))).astype(bf16)
    split = pl.pallas_call(
        permute_kernel,
        out_shape=jax.ShapeDtypeStruct((16, rows, quarter + HD), bf16),
        in_specs=[vmem, vmem],
        out_specs=vmem,
        scratch_shapes=[pltpu.VMEM((8 * rows, width // 8), bf16)],
        compiler_params=params,
        name="permute_columns",
    )(tokens, extra)
    own_t = lax.all_to_all(split, ("x", "yl"), 0, 0).reshape(16 * rows, quarter + HD)

    weight = jnp.concatenate([q_weight, x_weight, shared_weight], axis=1)
    partner = lax.ppermute(weight, "yh", [(0, 1), (1, 0)])
    w_own = lax.all_gather(weight, z, axis=0, tiled=True)
    own_t, w_own, partner = lax.optimization_barrier((own_t, w_own, partner))
    other_t = lax.ppermute(own_t, "c", [(0, 1), (1, 0)])
    tail = own_t[16 * rows - HALO :, :quarter]
    sources = [(2 * i + 1, 2 * i + 2) for i in range(31)]
    tail = lax.ppermute(tail, ("zh", "zl", "yh", "c"), sources) + lax.ppermute(
        tail, ("zh", "zl", "yh", "c"), [(source, target + 1) for source, target in sources]
    )

    w_other = lax.all_gather(partner, z, axis=0, tiled=True)

    place = jnp.stack([core, lax.axis_index("yh").astype(jnp.int32)])

    def partial(name, first, columns, *operands):
        return pl.pallas_call(
            functools.partial(partial_kernel, first),
            out_shape=jax.ShapeDtypeStruct((4, HALO + group_rows, columns), bf16),
            in_specs=[smem] + [vmem] * len(operands),
            out_specs=vmem,
            compiler_params=params,
            name=name,
        )(place, *operands)

    s_part = partial("partial_s", 512, HD, own_t, other_t, tail, w_own, w_other)
    tail, s_part = lax.optimization_barrier((tail, s_part))
    s_parts = lax.all_to_all(s_part, "x", 0, 0)
    qx_part = partial("partial_qx", 0, 512, own_t, other_t, tail, w_own, w_other)
    s_parts, qx_part = lax.optimization_barrier((s_parts, qx_part))
    qx_parts = lax.all_to_all(qx_part, "x", 0, 0)
    s_own = jnp.sum(s_parts.astype(jnp.float32), axis=0).astype(bf16)
    s_all = lax.all_gather(s_own, ("yl", "c"), axis=0)
    qx_parts, s_all = lax.optimization_barrier((qx_parts, s_all))

    at = lax.axis_index("x") * (4 * rows)
    near = lax.dynamic_slice(own_t, (at, quarter), (4 * rows, HD)).reshape(4, 1, rows, HD)
    far = lax.dynamic_slice(other_t, (at, quarter), (4 * rows, HD)).reshape(4, 1, rows, HD)
    first = jnp.where(core == 0, near, far)
    second = jnp.where(core == 0, far, near)
    places = jnp.concatenate([first, second], axis=1).reshape(group_rows, HD)[:, :4].astype(jnp.float32)
    half = HD // 2
    index = jnp.arange(half, dtype=jnp.float32)
    inverse = jnp.exp(-jnp.log(jnp.float32(rope_base)) * index / jnp.float32(half))
    angle = (places[:, 0] * 256.0 + places[:, 1])[:, None] * inverse[None, :]
    cosine, sine = jnp.cos(angle), jnp.sin(angle)
    cosine = jnp.concatenate([cosine, cosine], axis=1)
    sine = jnp.concatenate([-sine, sine], axis=1)
    starts = (places[:, 2] * 256.0 + places[:, 3]).astype(jnp.int32)
    row_ids = lax.axis_index(FSDP) * group_rows + jnp.arange(group_rows, dtype=jnp.int32)
    rel = jnp.broadcast_to((row_ids - starts)[:, None], (group_rows, HD))

    return pl.pallas_call(
        final_kernel,
        out_shape=(
            jax.ShapeDtypeStruct((group_rows, 256), bf16),
            jax.ShapeDtypeStruct((group_rows, 512), bf16),
            jax.ShapeDtypeStruct((group_rows, 256), bf16),
            jax.ShapeDtypeStruct((group_rows, 512), bf16),
        ),
        in_specs=[vmem] * 7,
        out_specs=(vmem,) * 4,
        scratch_shapes=[pltpu.VMEM((group_rows + HALO, HD), jnp.float32)],
        compiler_params=params,
        name="rotate_and_convolve",
    )(qx_parts, s_all, cosine, sine, rel, conv_x, conv_bc)


def solution(mesh):
    chips = Mesh(mesh.devices.reshape(SIZES), AXES)
    head = ("yl", "c")
    in_specs = (
        P(AXES, None), P(AXES), P(AXES),
        P(FSDP, head), P(FSDP, head), P(FSDP, head),
        P(None, head), P(),
    )
    out_specs = (P(FSDP, head), P(FSDP, None), P(FSDP, head), P(FSDP, None))
    return jax.shard_map(shards, mesh=chips, in_specs=in_specs, out_specs=out_specs, check_vma=False)
```

time: 152 us -> 138 us (0.908)
  blocking collectives: 92.7 us -> 84.8 us
  local copies, waits for them, and re-layouts: 6.3 us -> 2.21 us
  Pallas kernels: 5.79 us -> 9.7 us
  other arithmetic: 6.27 us -> 2.78 us
  starting transfers between devices: 39.1 us -> 36.4 us
    all_gather x2, blocking collectives: 74.7 us -> 68.3 us  [the longest x1 41.6 us: shards(): w_own = lax.all_gather(weight, z, axis=0, tiled=True)]
    pallas_call x2, Pallas kernels: 2.43 us -> 6.22 us  [partial(): pl.pallas_call(functools.partial(partial_kernel, first), out_shape=jax.Sh...]
    ppermute x1, starting transfers between devices: 8.27 us -> 4.76 us  [shards(): partner = lax.ppermute(weight, 'yh', [(0, 1), (1, 0)])]
    unnamed x20 -> x16, local copies, waits for them, and re-layouts: 5.38 us -> 1.99 us
    all_to_all x1, starting transfers between devices: 5.45 us -> 8.12 us  [shards(): lax.all_to_all(split, ('x', 'yl'), 0, 0).reshape(16 * rows, quarter + HD)]
  transfers between devices with their start and end apart: 7 -> 7, of which waited for: 1 -> 1; matrix products, arithmetic and copies ran while one was open for 4% -> 2% of each run, Pallas kernels for 1% -> 2%
where the time goes in v6:
time: 138 us
  blocking collectives  84.8 us (61%)
  starting transfers between devices  36.4 us (26%)
  Pallas kernels  9.7 us (7%)
  other arithmetic  2.78 us (2%)
  local copies, waits for them, and re-layouts  2.21 us (2%)
    all_gather x1, blocking collectives, shards(): w_own = lax.all_gather(weight, z, axis=0, tiled=True)  41.6 us
    all_gather x1, blocking collectives, shards(): w_other = lax.all_gather(partner, z, axis=0, tiled=True)  26.7 us
    all_gather x1, blocking collectives, shards(): s_all = lax.all_gather(s_own, ('yl', 'c'), axis=0)  16.6 us
    ppermute x1, starting transfers between devices, shards(): other_t = lax.ppermute(own_t, 'c', [(0, 1), (1, 0)])  8.68 us
    all_to_all x1, starting transfers between devices, shards(): lax.all_to_all(split, ('x', 'yl'), 0, 0).reshape(16 * rows, quarter + HD)  8.12 us
    pallas_call x2, Pallas kernels, partial(): pl.pallas_call(functools.partial(partial_kernel, first), out_shape=jax.Sh...  6.22 us
    ppermute x1, starting transfers between devices, shards(): partner = lax.ppermute(weight, 'yh', [(0, 1), (1, 0)])  4.76 us
    ppermute x1, starting transfers between devices, shards(): lax.ppermute(tail, ('zh', 'zl', 'yh', 'c'), sources)  4.32 us
  transfers between devices with their start and end apart: 7, of which 1 were waited for; matrix products, arithmetic and copies ran while one was open for 2% of the time, Pallas kernels for 2%

profile of v6, /device:TPU:1, one launch (start us, length us, event | category | flops | bytes accessed | tf_op | source)
XLA Modules:
  0.0 137.5 jit_solution(3266329786592056361)
XLA Ops:
  0.6 0.7 convert_bitcast_fusion.1
  1.3 0.1 copy.22
  1.4 1.0 copy-done.1
  2.4 1.7 %permute_columns.1 = bf16[16,32,1408]{2,1,0:T(8,128)(2,1)} custom-call(bf16[32,5120]{1,0:T(8,128)(2,1)S(1)} %copy-done.1, bf16[32,128]{1,0:T(8,128)(2,1)S(1)} %pad.5.extra_ref), custom_call_target="tpu_custom_call" | custom-call | tf_op jit(solution)/shard_map/permute_columns/pallas_call | solution.py:119
  4.2 8.1 %all-to-all-start = ((bf16[16,32,1408]{2,1,0:T(8,128)(2,1)}), bf16[16,32,1408]{2,1,0:T(8,128)(2,1)S(1)}, u32[]{:S(2)}, u32[]{:S(2)}) async-start(bf16[16,32,1408]{2,1,0:T(8,128)(2,1)} %permute_columns.1), calls=%async_computation | async-start | bytes 2883584 | tf_op jit(solution)/shard_map/all_to_all | solution.py:128
  12.4 4.8 %collective-permute-start = (bf16[40,640]{1,0:T(8,128)(2,1)S(1)}, bf16[40,640]{1,0:T(8,128)(2,1)S(1)}, u32[]{:S(2)}, u32[]{:S(2)}) collective-permute-start(bf16[40,640]{1,0:T(8,128)(2,1)S(1)} %constant_dynamic-update-slice_fusion), channel_id=1, source_target_pairs={{0,32},{32,0},{1,33},{33,1},{2,34},{34,2},{3,35},{35,3},{4,36},{36... | collective-permute-start | bytes 153608 | tf_op jit(solution)/shard_map/ppermute | solution.py:131
  17.1 41.6 %all_gather.12.w_own_ref = bf16[640,640]{1,0:T(8,128)(2,1)S(1)} all-gather(bf16[40,640]{1,0:T(8,128)(2,1)S(1)} %constant_dynamic-update-slice_fusion), channel_id=1, replica_groups=mesh['zh'=4,'zl'=4,'yh'=2,'x'=4,'yl'=4,'c'=2] {'zh','zl'}, dimensions={0}, use_global_device_ids=true | all-gather | bytes 870400 | tf_op jit(solution)/shard_map/all_gather | solution.py:132
  58.7 0.0 collective-permute-done
  58.7 8.7 %collective-permute-start.3 = (bf16[512,1408]{1,0:T(8,128)(2,1)S(1)}, bf16[512,1408]{1,0:T(8,128)(2,1)}, u32[]{:S(2)}, u32[]{:S(2)}) collective-permute-start(bf16[512,1408]{1,0:T(8,128)(2,1)S(1)} %bitcast.19), channel_id=1, source_target_pairs={{0,1},{1,0},{2,3},{3,2},{4,5},{5,4},{6,7},{7,6},{8,9},{9,8},{10,11... | collective-permute-start | bytes 4325384 | tf_op jit(solution)/shard_map/ppermute | solution.py:134
  67.4 0.1 pad_add_fusion.place_ref
  67.5 4.3 %collective-permute-start.1 = (bf16[16,1280]{1,0:T(8,128)(2,1)S(1)}, bf16[16,1280]{1,0:T(8,128)(2,1)S(1)}, u32[]{:S(2)}, u32[]{:S(2)}) collective-permute-start(bf16[16,1280]{1,0:T(8,128)(2,1)S(1)} %slice.18), channel_id=1, source_target_pairs={{1,32},{33,64},{65,96},{97,128},{129,160},{161,192},{193,224},{225... | collective-permute-start | bytes 122888 | tf_op jit(solution)/shard_map/ppermute | solution.py:137
  71.8 3.5 %collective-permute-start.2 = (bf16[16,1280]{1,0:T(8,128)(2,1)S(1)}, bf16[16,1280]{1,0:T(8,128)(2,1)S(1)}, u32[]{:S(2)}, u32[]{:S(2)}) collective-permute-start(bf16[16,1280]{1,0:T(8,128)(2,1)S(1)} %slice.18), channel_id=1, source_target_pairs={{1,33},{33,65},{65,97},{97,129},{129,161},{161,193},{193,225},{225... | collective-permute-start | bytes 122888 | tf_op jit(solution)/shard_map/ppermute | solution.py:137
  75.4 26.7 %all_gather.13.w_other_ref = bf16[640,640]{1,0:T(8,128)(2,1)S(1)} all-gather(bf16[40,640]{1,0:T(8,128)(2,1)S(1)} %collective-permute-done), channel_id=1, replica_groups=mesh['zh'=4,'zl'=4,'yh'=2,'x'=4,'yl'=4,'c'=2] {'zh','zl'}, dimensions={0}, use_global_device_ids=true | all-gather | bytes 870400 | tf_op jit(solution)/shard_map/all_gather | solution.py:141
  102.1 0.0 collective-permute-done.3.other_ref
  102.1 3.0 %partial_s.1 = bf16[4,272,128]{2,1,0:T(8,128)(2,1)} custom-call(s32[2]{0:T(128)S(1)} %pad_add_fusion.place_ref, bf16[512,1408]{1,0:T(8,128)(2,1)S(1)} %bitcast.21, bf16[512,1408]{1,0:T(8,128)(2,1)} %collective-permute-done.3.other_ref, bf16[16,1280]{1,0:T(8,128)(2,1)S(1)} %add.39.tail_ref, bf16[640,640]{1,0:T(8,128)(2,1)S(1)} %all_gather.12.w_own_ref, ...), custom_call_target="tpu_custom_call" | custom-call | tf_op jit(solution)/shard_map/partial_s/pallas_call | solution.py:146
  105.1 3.4 %all-to-all-start.1 = ((bf16[4,272,128]{2,1,0:T(8,128)(2,1)}), bf16[4,272,128]{2,1,0:T(8,128)(2,1)S(1)}, u32[]{:S(2)}, u32[]{:S(2)}) async-start(bf16[4,272,128]{2,1,0:T(8,128)(2,1)} %partial_s.1), calls=%async_computation.1 | async-start | bytes 557056 | tf_op jit(solution)/shard_map/all_to_all | solution.py:157
  108.6 0.8 broadcast_select_fusion.1
  109.4 3.2 %partial_qx.1 = bf16[4,272,512]{2,1,0:T(8,128)(2,1)S(1)} custom-call(s32[2]{0:T(128)S(1)} %pad_add_fusion.place_ref, bf16[512,1408]{1,0:T(8,128)(2,1)S(1)} %bitcast.23, bf16[512,1408]{1,0:T(8,128)(2,1)} %collective-permute-done.3.other_ref, bf16[16,1280]{1,0:T(8,128)(2,1)S(1)} %add.39.tail_ref, bf16[640,640]{1,0:T(8,128)(2,1)S(1)} %all_gather.12.w_own_ref, ...), custom_call_target="tpu_custom_call" | custom-call | tf_op jit(solution)/shard_map/partial_qx/pallas_call | solution.py:146
  112.6 1.0 copy-done
  113.6 0.7 all-to-all-done.1
  114.3 3.5 %all-to-all-start.2 = ((bf16[4,272,512]{2,1,0:T(8,128)(2,1)}), bf16[4,272,512]{2,1,0:T(8,128)(2,1)S(1)}, u32[]{:S(2)}, u32[]{:S(2)}) async-start(bf16[4,272,512]{2,1,0:T(8,128)(2,1)} %copy-done), calls=%async_computation.2 | async-start | bytes 2228224 | tf_op jit(solution)/shard_map/all_to_all | solution.py:160
  117.9 0.0 copy-start.2
  117.9 0.0 copy-start.3
  117.9 0.2 fusion.3
  118.1 0.5 fusion.4
  118.6 0.1 pad_maximum_fusion.cos_ref
  118.7 0.1 pad_maximum_fusion.1.sin_ref
  118.8 0.2 fusion.2
  119.1 16.6 %all-gather = bf16[2176,128]{1,0:T(8,128)(2,1)S(1)} all-gather(bf16[272,128]{1,0:T(8,128)(2,1)S(1)} %reduce_sum.12), channel_id=2, replica_groups=mesh['zh'=4,'zl'=4,'yh'=2,'x'=4,'yl'=4,'c'=2] {'yl','c'}, dimensions={0}, use_global_device_ids=true | all-gather | bytes 626688 | tf_op jit(solution)/shard_map/all_gather | solution.py:162
  135.7 0.0 all-to-all-done.2.parts_ref
  135.7 0.1 broadcast_in_dim.5.rel_ref
  135.8 1.7 %rotate_and_convolve.1 = (bf16[256,256]{1,0:T(8,128)(2,1)}, bf16[256,512]{1,0:T(8,128)(2,1)}, bf16[256,256]{1,0:T(8,128)(2,1)}, bf16[256,512]{1,0:T(8,128)(2,1)}) custom-call(bf16[4,272,512]{2,1,0:T(8,128)(2,1)S(1)} %all-to-all-done.2.parts_ref, bf16[8,272,128]{2,1,0:T(8,128)(2,1)S(1)} %bitcast.24, f32[256,128]{1,0:T(8,128)S(1)} %pad_maximum_fusion.cos_ref, ...), custom_call_target="tpu_custom_call" | custom-call | tf_op jit(solution)/shard_map/rotate_and_convolve/pallas_call | solution.py:182
  (24 shorter events, 0.2 us)
Async XLA Ops:
  1.4 1.0 copy-start.1
  4.2 8.1 %copy-start.4 = (bf16[40,256]{1,0:T(8,128)(2,1)S(1)}, bf16[40,256]{1,0:T(8,128)(2,1)}, u32[]{:S(2)}) copy-start(bf16[40,256]{1,0:T(8,128)(2,1)} %param.11) | copy-start | bytes 61444
  4.2 8.2 %copy-start.5 = (bf16[40,256]{1,0:T(8,128)(2,1)S(1)}, bf16[40,256]{1,0:T(8,128)(2,1)}, u32[]{:S(2)}) copy-start(bf16[40,256]{1,0:T(8,128)(2,1)} %param.12) | copy-start | bytes 61444
  4.2 8.2 %copy-start.6 = (bf16[40,128]{1,0:T(8,128)(2,1)S(1)}, bf16[40,128]{1,0:T(8,128)(2,1)}, u32[]{:S(2)}) copy-start(bf16[40,128]{1,0:T(8,128)(2,1)} %param.13) | copy-start | bytes 30724
  4.2 54.5 %all-to-all-start = ((bf16[16,32,1408]{2,1,0:T(8,128)(2,1)}), bf16[16,32,1408]{2,1,0:T(8,128)(2,1)S(1)}, u32[]{:S(2)}, u32[]{:S(2)}) async-start(bf16[16,32,1408]{2,1,0:T(8,128)(2,1)} %permute_columns.1), calls=%async_computation | async-start | bytes 2883584 | tf_op jit(solution)/shard_map/all_to_all | solution.py:128
  12.4 46.3 %collective-permute-start = (bf16[40,640]{1,0:T(8,128)(2,1)S(1)}, bf16[40,640]{1,0:T(8,128)(2,1)S(1)}, u32[]{:S(2)}, u32[]{:S(2)}) collective-permute-start(bf16[40,640]{1,0:T(8,128)(2,1)S(1)} %constant_dynamic-update-slice_fusion), channel_id=1, source_target_pairs={{0,32},{32,0},{1,33},{33,1},{2,34},{34,2},{3,35},{35,3},{4,36},{36... | collective-permute-start | bytes 153608 | tf_op jit(solution)/shard_map/ppermute | solution.py:131
  58.7 43.4 %collective-permute-start.3 = (bf16[512,1408]{1,0:T(8,128)(2,1)S(1)}, bf16[512,1408]{1,0:T(8,128)(2,1)}, u32[]{:S(2)}, u32[]{:S(2)}) collective-permute-start(bf16[512,1408]{1,0:T(8,128)(2,1)S(1)} %bitcast.19), channel_id=1, source_target_pairs={{0,1},{1,0},{2,3},{3,2},{4,5},{5,4},{6,7},{7,6},{8,9},{9,8},{10,11... | collective-permute-start | bytes 4325384 | tf_op jit(solution)/shard_map/ppermute | solution.py:134
  67.5 34.6 %collective-permute-start.1 = (bf16[16,1280]{1,0:T(8,128)(2,1)S(1)}, bf16[16,1280]{1,0:T(8,128)(2,1)S(1)}, u32[]{:S(2)}, u32[]{:S(2)}) collective-permute-start(bf16[16,1280]{1,0:T(8,128)(2,1)S(1)} %slice.18), channel_id=1, source_target_pairs={{1,32},{33,64},{65,96},{97,128},{129,160},{161,192},{193,224},{225... | collective-permute-start | bytes 122888 | tf_op jit(solution)/shard_map/ppermute | solution.py:137
  71.8 30.2 %collective-permute-start.2 = (bf16[16,1280]{1,0:T(8,128)(2,1)S(1)}, bf16[16,1280]{1,0:T(8,128)(2,1)S(1)}, u32[]{:S(2)}, u32[]{:S(2)}) collective-permute-start(bf16[16,1280]{1,0:T(8,128)(2,1)S(1)} %slice.18), channel_id=1, source_target_pairs={{1,33},{33,65},{65,97},{97,129},{129,161},{161,193},{193,225},{225... | collective-permute-start | bytes 122888 | tf_op jit(solution)/shard_map/ppermute | solution.py:137
  105.1 9.2 %all-to-all-start.1 = ((bf16[4,272,128]{2,1,0:T(8,128)(2,1)}), bf16[4,272,128]{2,1,0:T(8,128)(2,1)S(1)}, u32[]{:S(2)}, u32[]{:S(2)}) async-start(bf16[4,272,128]{2,1,0:T(8,128)(2,1)} %partial_s.1), calls=%async_computation.1 | async-start | bytes 557056 | tf_op jit(solution)/shard_map/all_to_all | solution.py:157
  112.6 1.0 copy-start
  114.3 21.3 %all-to-all-start.2 = ((bf16[4,272,512]{2,1,0:T(8,128)(2,1)}), bf16[4,272,512]{2,1,0:T(8,128)(2,1)S(1)}, u32[]{:S(2)}, u32[]{:S(2)}) async-start(bf16[4,272,512]{2,1,0:T(8,128)(2,1)} %copy-done), calls=%async_computation.2 | async-start | bytes 2228224 | tf_op jit(solution)/shard_map/all_to_all | solution.py:160
  117.9 17.9 %copy-start.2 = (f32[4,512]{1,0:T(4,128)S(1)}, f32[4,512]{1,0:T(4,128)}, u32[]{:S(2)}) copy-start(f32[4,512]{1,0:T(4,128)} %tbc_ref.1) | copy-start | bytes 24580
  117.9 17.9 %copy-start.3 = (f32[4,256]{1,0:T(4,128)S(1)}, f32[4,256]{1,0:T(4,128)}, u32[]{:S(2)}) copy-start(f32[4,256]{1,0:T(4,128)} %tx_ref.1) | copy-start | bytes 12292

commit v7 on v6

--- a/solution.py
+++ b/solution.py
@@ -46,10 +46,10 @@
     columns = out_ref.shape[2]
     for start in range(0, columns, 256):
         cols = slice(start, min(start + 256, columns))
-        w_cols = slice(first + cols.start, first + cols.stop)
+        own_cols = slice(first + cols.start, first + cols.stop)
         for mine in (True, False):
             part = 0.0
-            for at_k, w_ref in ((near, w_own_ref), (far, w_other_ref)):
+            for at_k, w_ref, w_cols in ((near, w_own_ref, own_cols), (far, w_other_ref, cols)):
                 rows = (own_ref if mine else other_ref)[:, at_k]
                 if not mine:
                     rows = jnp.concatenate([rows, tail_ref[:, at_k]], axis=0)
@@ -128,9 +128,10 @@
     own_t = lax.all_to_all(split, ("x", "yl"), 0, 0).reshape(16 * rows, quarter + HD)
 
     weight = jnp.concatenate([q_weight, x_weight, shared_weight], axis=1)
-    partner = lax.ppermute(weight, "yh", [(0, 1), (1, 0)])
     w_own = lax.all_gather(weight, z, axis=0, tiled=True)
-    own_t, w_own, partner = lax.optimization_barrier((own_t, w_own, partner))
+    own_t, w_own = lax.optimization_barrier((own_t, w_own))
+    swap = [(0, 1), (1, 0)]
+    w_other_s = lax.ppermute(w_own[:, 512:], "yh", swap)
     other_t = lax.ppermute(own_t, "c", [(0, 1), (1, 0)])
     tail = own_t[16 * rows - HALO :, :quarter]
     sources = [(2 * i + 1, 2 * i + 2) for i in range(31)]
@@ -138,7 +139,8 @@
         tail, ("zh", "zl", "yh", "c"), [(source, target + 1) for source, target in sources]
     )
 
-    w_other = lax.all_gather(partner, z, axis=0, tiled=True)
+    w_qx, w_other_s, tail = lax.optimization_barrier((w_own[:, :512], w_other_s, tail))
+    w_other_qx = lax.ppermute(w_qx, "yh", swap)
 
     place = jnp.stack([core, lax.axis_index("yh").astype(jnp.int32)])
 
@@ -152,10 +154,10 @@
             name=name,
         )(place, *operands)
 
-    s_part = partial("partial_s", 512, HD, own_t, other_t, tail, w_own, w_other)
+    s_part = partial("partial_s", 512, HD, own_t, other_t, tail, w_own, w_other_s)
     tail, s_part = lax.optimization_barrier((tail, s_part))
     s_parts = lax.all_to_all(s_part, "x", 0, 0)
-    qx_part = partial("partial_qx", 0, 512, own_t, other_t, tail, w_own, w_other)
+    qx_part = partial("partial_qx", 0, 512, own_t, other_t, tail, w_own, w_other_qx)
     s_parts, qx_part = lax.optimization_barrier((s_parts, qx_part))
     qx_parts = lax.all_to_all(qx_part, "x", 0, 0)
     s_own = jnp.sum(s_parts.astype(jnp.float32), axis=0).astype(bf16)

time: 138 us -> 142 us (1.029)
  blocking collectives: 84.8 us -> 73.3 us
  starting transfers between devices: 36.4 us -> 46 us
  waiting for transfers between devices: 0.75 us -> 5.9 us
    all_gather x1 -> x0, blocking collectives: 26.7 us -> none  [shards(): w_other = lax.all_gather(partner, z, axis=0, tiled=True)]
    all_gather x1, blocking collectives: 16.6 us -> 31.9 us  [shards(): s_all = lax.all_gather(s_own, ('yl', 'c'), axis=0)]
    ppermute x1 -> x2, starting transfers between devices: 4.76 us -> 12.4 us  [the longest x1 7.72 us: shards(): w_other_qx = lax.ppermute(w_qx, 'yh', swap)]
    ppermute x1 -> x2, waiting for transfers between devices: 0.01 us -> 4.76 us  [the longest x1 4.76 us: shards(): w_other_qx = lax.ppermute(w_qx, 'yh', swap)]
  transfers between devices with their start and end apart: 7 -> 8, of which waited for: 1 -> 2; matrix products, arithmetic and copies ran while one was open for 2% -> 2% of each run, Pallas kernels for 2% -> 5%
where the time goes in v7:
time: 142 us
  blocking collectives  73.3 us (52%)
  starting transfers between devices  46 us (32%)
  Pallas kernels  10.7 us (8%)
  waiting for transfers between devices  5.9 us (4%)
  other arithmetic  2.78 us (2%)
  local copies, waits for them, and re-layouts  2.1 us (1%)
    all_gather x1, blocking collectives, shards(): w_own = lax.all_gather(weight, z, axis=0, tiled=True)  41.5 us
    all_gather x1, blocking collectives, shards(): s_all = lax.all_gather(s_own, ('yl', 'c'), axis=0)  31.9 us
    ppermute x1, starting transfers between devices, shards(): other_t = lax.ppermute(own_t, 'c', [(0, 1), (1, 0)])  8.52 us
    all_to_all x1, starting transfers between devices, shards(): lax.all_to_all(split, ('x', 'yl'), 0, 0).reshape(16 * rows, quarter + HD)  8.12 us
    ppermute x1, starting transfers between devices, shards(): w_other_qx = lax.ppermute(w_qx, 'yh', swap)  7.72 us
    pallas_call x2, Pallas kernels, partial(): pl.pallas_call(functools.partial(partial_kernel, first), out_shape=jax.Sh...  7.24 us
    ppermute x1, waiting for transfers between devices, shards(): w_other_qx = lax.ppermute(w_qx, 'yh', swap)  4.76 us
    ppermute x1, starting transfers between devices, shards(): w_other_s = lax.ppermute(w_own[:, 512:], 'yh', swap)  4.7 us
  transfers between devices with their start and end apart: 8, of which 2 were waited for; matrix products, arithmetic and copies ran while one was open for 2% of the time, Pallas kernels for 5%

profile of v7, /device:TPU:1, one launch (start us, length us, event | category | flops | bytes accessed | tf_op | source)
XLA Modules:
  0.0 141.7 jit_solution(15996167614815263997)
XLA Ops:
  0.6 0.7 convert_bitcast_fusion.1
  1.3 0.1 copy.22
  1.4 1.0 copy-done
  2.4 1.7 %permute_columns.1 = bf16[16,32,1408]{2,1,0:T(8,128)(2,1)} custom-call(bf16[32,5120]{1,0:T(8,128)(2,1)S(1)} %copy-done, bf16[32,128]{1,0:T(8,128)(2,1)S(1)} %pad.5.extra_ref), custom_call_target="tpu_custom_call" | custom-call | tf_op jit(solution)/shard_map/permute_columns/pallas_call | solution.py:119
  4.2 8.1 %all-to-all-start = ((bf16[16,32,1408]{2,1,0:T(8,128)(2,1)}), bf16[16,32,1408]{2,1,0:T(8,128)(2,1)S(1)}, u32[]{:S(2)}, u32[]{:S(2)}) async-start(bf16[16,32,1408]{2,1,0:T(8,128)(2,1)} %permute_columns.1), calls=%async_computation | async-start | bytes 2883584 | tf_op jit(solution)/shard_map/all_to_all | solution.py:128
  12.3 41.5 %all_gather.9.w_own_ref = bf16[640,640]{1,0:T(8,128)(2,1)S(1)} all-gather(bf16[40,640]{1,0:T(8,128)(2,1)S(1)} %pad_maximum_fusion.3), channel_id=1, replica_groups=mesh['zh'=4,'zl'=4,'yh'=2,'x'=4,'yl'=4,'c'=2] {'zh','zl'}, dimensions={0}, use_global_device_ids=true | all-gather | bytes 870400 | tf_op jit(solution)/shard_map/all_gather | solution.py:131
  53.8 0.0 all-to-all-done
  53.8 8.5 %collective-permute-start.3 = (bf16[512,1408]{1,0:T(8,128)(2,1)S(1)}, bf16[512,1408]{1,0:T(8,128)(2,1)}, u32[]{:S(2)}, u32[]{:S(2)}) collective-permute-start(bf16[512,1408]{1,0:T(8,128)(2,1)S(1)} %bitcast.19), channel_id=1, source_target_pairs={{0,1},{1,0},{2,3},{3,2},{4,5},{5,4},{6,7},{7,6},{8,9},{9,8},{10,11... | collective-permute-start | bytes 4325384 | tf_op jit(solution)/shard_map/ppermute | solution.py:135
  62.3 4.7 %collective-permute-start = (bf16[640,128]{1,0:T(8,128)(2,1)S(1)}, bf16[640,128]{1,0:T(8,128)(2,1)S(1)}, u32[]{:S(2)}, u32[]{:S(2)}) collective-permute-start(bf16[640,128]{1,0:T(8,128)(2,1)S(1)} %slice.25), channel_id=1, source_target_pairs={{0,32},{32,0},{1,33},{33,1},{2,34},{34,2},{3,35},{35,3},{4,36},{36... | collective-permute-start | bytes 491528 | tf_op jit(solution)/shard_map/ppermute | solution.py:134
  67.1 4.7 %collective-permute-start.1 = (bf16[16,1280]{1,0:T(8,128)(2,1)S(1)}, bf16[16,1280]{1,0:T(8,128)(2,1)S(1)}, u32[]{:S(2)}, u32[]{:S(2)}) collective-permute-start(bf16[16,1280]{1,0:T(8,128)(2,1)S(1)} %slice.26), channel_id=1, source_target_pairs={{1,32},{33,64},{65,96},{97,128},{129,160},{161,192},{193,224},{225... | collective-permute-start | bytes 122888 | tf_op jit(solution)/shard_map/ppermute | solution.py:138
  71.7 3.5 %collective-permute-start.2 = (bf16[16,1280]{1,0:T(8,128)(2,1)S(1)}, bf16[16,1280]{1,0:T(8,128)(2,1)S(1)}, u32[]{:S(2)}, u32[]{:S(2)}) collective-permute-start(bf16[16,1280]{1,0:T(8,128)(2,1)S(1)} %slice.26), channel_id=1, source_target_pairs={{1,33},{33,65},{65,97},{97,129},{129,161},{161,193},{193,225},{225... | collective-permute-start | bytes 122888 | tf_op jit(solution)/shard_map/ppermute | solution.py:138
  75.3 0.9 slice.24
  76.2 0.0 collective-permute-done.1
  76.2 1.1 collective-permute-done.2
  77.3 0.0 collective-permute-done.w_other_ref
  77.3 7.7 %collective-permute-start.4 = (bf16[640,512]{1,0:T(8,128)(2,1)}, bf16[640,512]{1,0:T(8,128)(2,1)S(1)}, u32[]{:S(2)}, u32[]{:S(2)}) collective-permute-start(bf16[640,512]{1,0:T(8,128)(2,1)} %slice.24), channel_id=1, source_target_pairs={{0,32},{32,0},{1,33},{33,1},{2,34},{34,2},{3,35},{35,3},{4,36},{36... | collective-permute-start | bytes 1966088 | tf_op jit(solution)/shard_map/ppermute | solution.py:143
  85.1 0.1 pad_add_fusion.place_ref
  85.2 3.0 %partial_s.1 = bf16[4,272,128]{2,1,0:T(8,128)(2,1)} custom-call(s32[2]{0:T(128)S(1)} %pad_add_fusion.place_ref, bf16[512,1408]{1,0:T(8,128)(2,1)S(1)} %bitcast.21, bf16[512,1408]{1,0:T(8,128)(2,1)} %collective-permute-done.3.other_ref, bf16[16,1280]{1,0:T(8,128)(2,1)S(1)} %add.39.tail_ref, bf16[640,640]{1,0:T(8,128)(2,1)S(1)} %all_gather.9.w_own_ref, ...), custom_call_target="tpu_custom_call" | custom-call | tf_op jit(solution)/shard_map/partial_s/pallas_call | solution.py:148
  88.2 4.2 %all-to-all-start.1 = ((bf16[4,272,128]{2,1,0:T(8,128)(2,1)}), bf16[4,272,128]{2,1,0:T(8,128)(2,1)S(1)}, u32[]{:S(2)}, u32[]{:S(2)}) async-start(bf16[4,272,128]{2,1,0:T(8,128)(2,1)} %partial_s.1), calls=%async_computation.1 | async-start | bytes 557056 | tf_op jit(solution)/shard_map/all_to_all | solution.py:159
  92.4 0.8 broadcast_select_fusion.1
  93.2 4.8 %collective-permute-done.4.w_other_ref = bf16[640,512]{1,0:T(8,128)(2,1)S(1)} collective-permute-done((bf16[640,512]{1,0:T(8,128)(2,1)}, bf16[640,512]{1,0:T(8,128)(2,1)S(1)}, u32[]{:S(2)}, u32[]{:S(2)}) %collective-permute-start.4) | collective-permute-done | bytes 655392 | tf_op jit(solution)/shard_map/ppermute | solution.py:143
  98.0 4.2 %partial_qx.1 = bf16[4,272,512]{2,1,0:T(8,128)(2,1)} custom-call(s32[2]{0:T(128)S(1)} %pad_add_fusion.place_ref, bf16[512,1408]{1,0:T(8,128)(2,1)S(1)} %bitcast.23, bf16[512,1408]{1,0:T(8,128)(2,1)} %collective-permute-done.3.other_ref, bf16[16,1280]{1,0:T(8,128)(2,1)S(1)} %add.39.tail_ref, bf16[640,640]{1,0:T(8,128)(2,1)S(1)} %all_gather.9.w_own_ref, ...), custom_call_target="tpu_custom_call" | custom-call | tf_op jit(solution)/shard_map/partial_qx/pallas_call | solution.py:148
  102.2 4.5 %all-to-all-start.2 = ((bf16[4,272,512]{2,1,0:T(8,128)(2,1)}), bf16[4,272,512]{2,1,0:T(8,128)(2,1)S(1)}, u32[]{:S(2)}, u32[]{:S(2)}) async-start(bf16[4,272,512]{2,1,0:T(8,128)(2,1)} %partial_qx.1), calls=%async_computation.2 | async-start | bytes 2228224 | tf_op jit(solution)/shard_map/all_to_all | solution.py:162
  106.7 0.2 fusion.3
  106.9 0.5 fusion.4
  107.5 0.1 pad_maximum_fusion.cos_ref
  107.6 0.1 pad_maximum_fusion.1.sin_ref
  107.7 0.2 fusion.2
  108.0 31.9 %all-gather = bf16[2176,128]{1,0:T(8,128)(2,1)S(1)} all-gather(bf16[272,128]{1,0:T(8,128)(2,1)S(1)} %reduce_sum.12), channel_id=2, replica_groups=mesh['zh'=4,'zl'=4,'yh'=2,'x'=4,'yl'=4,'c'=2] {'yl','c'}, dimensions={0}, use_global_device_ids=true | all-gather | bytes 626688 | tf_op jit(solution)/shard_map/all_gather | solution.py:164
  139.8 0.0 all-to-all-done.2.parts_ref
  139.9 0.1 broadcast_in_dim.5.rel_ref
  140.0 1.7 %rotate_and_convolve.1 = (bf16[256,256]{1,0:T(8,128)(2,1)}, bf16[256,512]{1,0:T(8,128)(2,1)}, bf16[256,256]{1,0:T(8,128)(2,1)}, bf16[256,512]{1,0:T(8,128)(2,1)}) custom-call(bf16[4,272,512]{2,1,0:T(8,128)(2,1)S(1)} %all-to-all-done.2.parts_ref, bf16[8,272,128]{2,1,0:T(8,128)(2,1)S(1)} %bitcast.24, f32[256,128]{1,0:T(8,128)S(1)} %pad_maximum_fusion.cos_ref, ...), custom_call_target="tpu_custom_call" | custom-call | tf_op jit(solution)/shard_map/rotate_and_convolve/pallas_call | solution.py:184
  (23 shorter events, 0.2 us)
Async XLA Ops:
  1.4 1.0 copy-start
  4.2 8.1 %copy-start.3 = (bf16[40,256]{1,0:T(8,128)(2,1)S(1)}, bf16[40,256]{1,0:T(8,128)(2,1)}, u32[]{:S(2)}) copy-start(bf16[40,256]{1,0:T(8,128)(2,1)} %param.12) | copy-start | bytes 61444
  4.2 8.1 %copy-start.4 = (bf16[40,256]{1,0:T(8,128)(2,1)S(1)}, bf16[40,256]{1,0:T(8,128)(2,1)}, u32[]{:S(2)}) copy-start(bf16[40,256]{1,0:T(8,128)(2,1)} %param.11) | copy-start | bytes 61444
  4.2 8.2 %copy-start.5 = (bf16[40,128]{1,0:T(8,128)(2,1)S(1)}, bf16[40,128]{1,0:T(8,128)(2,1)}, u32[]{:S(2)}) copy-start(bf16[40,128]{1,0:T(8,128)(2,1)} %param.13) | copy-start | bytes 30724
  4.2 49.6 %all-to-all-start = ((bf16[16,32,1408]{2,1,0:T(8,128)(2,1)}), bf16[16,32,1408]{2,1,0:T(8,128)(2,1)S(1)}, u32[]{:S(2)}, u32[]{:S(2)}) async-start(bf16[16,32,1408]{2,1,0:T(8,128)(2,1)} %permute_columns.1), calls=%async_computation | async-start | bytes 2883584 | tf_op jit(solution)/shard_map/all_to_all | solution.py:128
  53.8 31.4 %collective-permute-start.3 = (bf16[512,1408]{1,0:T(8,128)(2,1)S(1)}, bf16[512,1408]{1,0:T(8,128)(2,1)}, u32[]{:S(2)}, u32[]{:S(2)}) collective-permute-start(bf16[512,1408]{1,0:T(8,128)(2,1)S(1)} %bitcast.19), channel_id=1, source_target_pairs={{0,1},{1,0},{2,3},{3,2},{4,5},{5,4},{6,7},{7,6},{8,9},{9,8},{10,11... | collective-permute-start | bytes 4325384 | tf_op jit(solution)/shard_map/ppermute | solution.py:135
  62.3 15.0 %collective-permute-start = (bf16[640,128]{1,0:T(8,128)(2,1)S(1)}, bf16[640,128]{1,0:T(8,128)(2,1)S(1)}, u32[]{:S(2)}, u32[]{:S(2)}) collective-permute-start(bf16[640,128]{1,0:T(8,128)(2,1)S(1)} %slice.25), channel_id=1, source_target_pairs={{0,32},{32,0},{1,33},{33,1},{2,34},{34,2},{3,35},{35,3},{4,36},{36... | collective-permute-start | bytes 491528 | tf_op jit(solution)/shard_map/ppermute | solution.py:134
  67.1 9.1 %collective-permute-start.1 = (bf16[16,1280]{1,0:T(8,128)(2,1)S(1)}, bf16[16,1280]{1,0:T(8,128)(2,1)S(1)}, u32[]{:S(2)}, u32[]{:S(2)}) collective-permute-start(bf16[16,1280]{1,0:T(8,128)(2,1)S(1)} %slice.26), channel_id=1, source_target_pairs={{1,32},{33,64},{65,96},{97,128},{129,160},{161,192},{193,224},{225... | collective-permute-start | bytes 122888 | tf_op jit(solution)/shard_map/ppermute | solution.py:138
  71.7 5.6 %collective-permute-start.2 = (bf16[16,1280]{1,0:T(8,128)(2,1)S(1)}, bf16[16,1280]{1,0:T(8,128)(2,1)S(1)}, u32[]{:S(2)}, u32[]{:S(2)}) collective-permute-start(bf16[16,1280]{1,0:T(8,128)(2,1)S(1)} %slice.26), channel_id=1, source_target_pairs={{1,33},{33,65},{65,97},{97,129},{129,161},{161,193},{193,225},{225... | collective-permute-start | bytes 122888 | tf_op jit(solution)/shard_map/ppermute | solution.py:138
  77.3 20.6 %collective-permute-start.4 = (bf16[640,512]{1,0:T(8,128)(2,1)}, bf16[640,512]{1,0:T(8,128)(2,1)S(1)}, u32[]{:S(2)}, u32[]{:S(2)}) collective-permute-start(bf16[640,512]{1,0:T(8,128)(2,1)} %slice.24), channel_id=1, source_target_pairs={{0,32},{32,0},{1,33},{33,1},{2,34},{34,2},{3,35},{35,3},{4,36},{36... | collective-permute-start | bytes 1966088 | tf_op jit(solution)/shard_map/ppermute | solution.py:143
  88.2 14.0 %all-to-all-start.1 = ((bf16[4,272,128]{2,1,0:T(8,128)(2,1)}), bf16[4,272,128]{2,1,0:T(8,128)(2,1)S(1)}, u32[]{:S(2)}, u32[]{:S(2)}) async-start(bf16[4,272,128]{2,1,0:T(8,128)(2,1)} %partial_s.1), calls=%async_computation.1 | async-start | bytes 557056 | tf_op jit(solution)/shard_map/all_to_all | solution.py:159
  102.2 37.6 %all-to-all-start.2 = ((bf16[4,272,512]{2,1,0:T(8,128)(2,1)}), bf16[4,272,512]{2,1,0:T(8,128)(2,1)S(1)}, u32[]{:S(2)}, u32[]{:S(2)}) async-start(bf16[4,272,512]{2,1,0:T(8,128)(2,1)} %partial_qx.1), calls=%async_computation.2 | async-start | bytes 2228224 | tf_op jit(solution)/shard_map/all_to_all | solution.py:162
  106.7 33.2 %copy-start.1 = (f32[4,512]{1,0:T(4,128)S(1)}, f32[4,512]{1,0:T(4,128)}, u32[]{:S(2)}) copy-start(f32[4,512]{1,0:T(4,128)} %tbc_ref.1) | copy-start | bytes 24580
  106.7 33.2 %copy-start.2 = (f32[4,256]{1,0:T(4,128)S(1)}, f32[4,256]{1,0:T(4,128)}, u32[]{:S(2)}) copy-start(f32[4,256]{1,0:T(4,128)} %tx_ref.1) | copy-start | bytes 12292

commit v8 on v7

--- a/solution.py
+++ b/solution.py
@@ -67,7 +67,7 @@
 
 
 def final_kernel(
-    parts_ref, s_ref, cos_ref, sin_ref, rel_ref, tx_ref, tbc_ref, q_ref, k_ref, x_ref, bc_ref, ext_ref
+    q_parts_ref, x_parts_ref, s_ref, cos_ref, sin_ref, rel_ref, tx_ref, tbc_ref, q_ref, k_ref, x_ref, bc_ref, ext_ref
 ):
     rows = q_ref.shape[0]
     cosine = cos_ref[...]
@@ -85,7 +85,7 @@
             total = total + jnp.where(rel_ref[...] >= step_back, window, 0.0)
         return (total / (1.0 + jnp.exp(-total))).astype(jnp.bfloat16)
 
-    def summed(first, cols):
+    def summed(parts_ref, first, cols):
         total = parts_ref[0, first:, cols].astype(jnp.float32)
         for x in range(1, 4):
             total = total + parts_ref[x, first:, cols].astype(jnp.float32)
@@ -93,8 +93,8 @@
 
     for block in range(2):
         cols = slice(block * HD, (block + 1) * HD)
-        q_ref[:, cols] = turned(summed(HALO, cols))
-        ext_ref[...] = summed(0, slice(256 + block * HD, 256 + (block + 1) * HD)).astype(jnp.float32)
+        q_ref[:, cols] = turned(summed(q_parts_ref, HALO, cols))
+        ext_ref[...] = summed(x_parts_ref, 0, cols).astype(jnp.float32)
         x_ref[:, cols] = convolved(tx_ref, cols)
     for block in range(4):
         cols = slice(block * HD, (block + 1) * HD)
@@ -139,8 +139,8 @@
         tail, ("zh", "zl", "yh", "c"), [(source, target + 1) for source, target in sources]
     )
 
-    w_qx, w_other_s, tail = lax.optimization_barrier((w_own[:, :512], w_other_s, tail))
-    w_other_qx = lax.ppermute(w_qx, "yh", swap)
+    w_x, w_other_s, tail = lax.optimization_barrier((w_own[:, 256:512], w_other_s, tail))
+    w_other_x = lax.ppermute(w_x, "yh", swap)
 
     place = jnp.stack([core, lax.axis_index("yh").astype(jnp.int32)])
 
@@ -155,14 +155,17 @@
         )(place, *operands)
 
     s_part = partial("partial_s", 512, HD, own_t, other_t, tail, w_own, w_other_s)
-    tail, s_part = lax.optimization_barrier((tail, s_part))
     s_parts = lax.all_to_all(s_part, "x", 0, 0)
-    qx_part = partial("partial_qx", 0, 512, own_t, other_t, tail, w_own, w_other_qx)
-    s_parts, qx_part = lax.optimization_barrier((s_parts, qx_part))
-    qx_parts = lax.all_to_all(qx_part, "x", 0, 0)
+    tail, _, w_q, w_other_x = lax.optimization_barrier((tail, s_part, w_own[:, :256], w_other_x))
+    w_other_q = lax.ppermute(w_q, "yh", swap)
+    x_part = partial("partial_x", 256, 256, own_t, other_t, tail, w_own, w_other_x)
+    s_parts, x_part = lax.optimization_barrier((s_parts, x_part))
+    x_parts = lax.all_to_all(x_part, "x", 0, 0)
     s_own = jnp.sum(s_parts.astype(jnp.float32), axis=0).astype(bf16)
     s_all = lax.all_gather(s_own, ("yl", "c"), axis=0)
-    qx_parts, s_all = lax.optimization_barrier((qx_parts, s_all))
+    x_parts, w_other_q, s_all = lax.optimization_barrier((x_parts, w_other_q, s_all))
+    q_part = partial("partial_q", 0, 256, own_t, other_t, tail, w_own, w_other_q)
+    q_parts = lax.all_to_all(q_part, "x", 0, 0)
 
     at = lax.axis_index("x") * (4 * rows)
     near = lax.dynamic_slice(own_t, (at, quarter), (4 * rows, HD)).reshape(4, 1, rows, HD)
@@ -189,12 +192,12 @@
             jax.ShapeDtypeStruct((group_rows, 256), bf16),
             jax.ShapeDtypeStruct((group_rows, 512), bf16),
         ),
-        in_specs=[vmem] * 7,
+        in_specs=[vmem] * 8,
         out_specs=(vmem,) * 4,
         scratch_shapes=[pltpu.VMEM((group_rows + HALO, HD), jnp.float32)],
         compiler_params=params,
         name="rotate_and_convolve",
-    )(qx_parts, s_all, cosine, sine, rel, conv_x, conv_bc)
+    )(q_parts, x_parts, s_all, cosine, sine, rel, conv_x, conv_bc)
 
 
 def solution(mesh):

time: 142 us -> 149 us (1.049)
  blocking collectives: 73.3 us -> 60.2 us
  waiting for transfers between devices: 5.9 us -> 17.1 us
  starting transfers between devices: 46 us -> 50.8 us
  Pallas kernels: 10.7 us -> 12.9 us
  other arithmetic: 2.78 us -> 4.57 us
    all_gather x1, blocking collectives: 31.9 us -> 18.8 us  [shards(): s_all = lax.all_gather(s_own, ('yl', 'c'), axis=0)]
    all_to_all x1 -> x2, waiting for transfers between devices: 0.01 us -> 7.87 us  [the longest x1 7.86 us: shards(): q_parts = lax.all_to_all(q_part, 'x', 0, 0)]
    all_to_all x1 -> x2, starting transfers between devices: 4.53 us -> 10.9 us  [the longest x1 6.26 us: shards(): x_parts = lax.all_to_all(x_part, 'x', 0, 0)]
    ppermute x1, waiting for transfers between devices: 0.01 us -> 5.87 us  [shards(): w_other_s = lax.ppermute(w_own[:, 512:], 'yh', swap)]
    pallas_call x2 -> x3, Pallas kernels: 7.24 us -> 9.43 us  [partial(): pl.pallas_call(functools.partial(partial_kernel, first), out_shape=jax.Sh...]
    ppermute x1 -> x2, starting transfers between devices: 7.72 us -> 6.22 us  [the longest x1 3.27 us: shards(): w_other_x = lax.ppermute(w_x, 'yh', swap)]
    ppermute x1 -> x2, waiting for transfers between devices: 4.76 us -> 3.3 us  [the longest x1 3.3 us: shards(): w_other_x = lax.ppermute(w_x, 'yh', swap)]
  transfers between devices with their start and end apart: 8 -> 10, of which waited for: 2 -> 3; matrix products, arithmetic and copies ran while one was open for 2% -> 3% of each run, Pallas kernels for 5% -> 4%
where the time goes in v8:
time: 149 us; the launch traced here: 148 us
  blocking collectives  60.2 us (40%)
  starting transfers between devices  50.8 us (34%)
  waiting for transfers between devices  17.1 us (11%)
  Pallas kernels  12.9 us (9%)
  other arithmetic  4.57 us (3%)
  local copies, waits for them, and re-layouts  2.09 us (1%)
    all_gather x1, blocking collectives, shards(): w_own = lax.all_gather(weight, z, axis=0, tiled=True)  41.5 us
    all_gather x1, blocking collectives, shards(): s_all = lax.all_gather(s_own, ('yl', 'c'), axis=0)  18.8 us
    pallas_call x3, Pallas kernels, partial(): pl.pallas_call(functools.partial(partial_kernel, first), out_shape=jax.Sh...  9.43 us
    ppermute x1, starting transfers between devices, shards(): other_t = lax.ppermute(own_t, 'c', [(0, 1), (1, 0)])  8.52 us
    all_to_all x1, starting transfers between devices, shards(): lax.all_to_all(split, ('x', 'yl'), 0, 0).reshape(16 * rows, quarter + HD)  8.12 us
    all_to_all x1, waiting for transfers between devices, shards(): q_parts = lax.all_to_all(q_part, 'x', 0, 0)  7.86 us
    all_to_all x1, starting transfers between devices, shards(): x_parts = lax.all_to_all(x_part, 'x', 0, 0)  6.26 us
    ppermute x1, waiting for transfers between devices, shards(): w_other_s = lax.ppermute(w_own[:, 512:], 'yh', swap)  5.87 us
  transfers between devices with their start and end apart: 10, of which 3 were waited for; matrix products, arithmetic and copies ran while one was open for 3% of the time, Pallas kernels for 4%

profile of v8, /device:TPU:1, one launch (start us, length us, event | category | flops | bytes accessed | tf_op | source)
XLA Modules:
  0.0 148.5 jit_solution(5187630641195358456)
XLA Ops:
  0.6 0.7 convert_bitcast_fusion.1
  1.3 0.1 copy.22
  1.4 1.0 copy-done
  2.4 1.7 %permute_columns.1 = bf16[16,32,1408]{2,1,0:T(8,128)(2,1)} custom-call(bf16[32,5120]{1,0:T(8,128)(2,1)S(1)} %copy-done, bf16[32,128]{1,0:T(8,128)(2,1)S(1)} %pad.5.extra_ref), custom_call_target="tpu_custom_call" | custom-call | tf_op jit(solution)/shard_map/permute_columns/pallas_call | solution.py:119
  4.1 8.1 %all-to-all-start = ((bf16[16,32,1408]{2,1,0:T(8,128)(2,1)}), bf16[16,32,1408]{2,1,0:T(8,128)(2,1)S(1)}, u32[]{:S(2)}, u32[]{:S(2)}) async-start(bf16[16,32,1408]{2,1,0:T(8,128)(2,1)} %permute_columns.1), calls=%async_computation | async-start | bytes 2883584 | tf_op jit(solution)/shard_map/all_to_all | solution.py:128
  12.3 41.5 %all_gather.9.w_own_ref = bf16[640,640]{1,0:T(8,128)(2,1)S(1)} all-gather(bf16[40,640]{1,0:T(8,128)(2,1)S(1)} %pad_maximum_fusion.3), channel_id=1, replica_groups=mesh['zh'=4,'zl'=4,'yh'=2,'x'=4,'yl'=4,'c'=2] {'zh','zl'}, dimensions={0}, use_global_device_ids=true | all-gather | bytes 870400 | tf_op jit(solution)/shard_map/all_gather | solution.py:131
  53.8 8.5 %collective-permute-start = (bf16[512,1408]{1,0:T(8,128)(2,1)S(1)}, bf16[512,1408]{1,0:T(8,128)(2,1)}, u32[]{:S(2)}, u32[]{:S(2)}) collective-permute-start(bf16[512,1408]{1,0:T(8,128)(2,1)S(1)} %bitcast.19), channel_id=1, source_target_pairs={{0,1},{1,0},{2,3},{3,2},{4,5},{5,4},{6,7},{7,6},{8,9},{9,8},{10,11... | collective-permute-start | bytes 4325384 | tf_op jit(solution)/shard_map/ppermute | solution.py:135
  62.3 4.6 %collective-permute-start.2 = (bf16[16,1280]{1,0:T(8,128)(2,1)S(1)}, bf16[16,1280]{1,0:T(8,128)(2,1)S(1)}, u32[]{:S(2)}, u32[]{:S(2)}) collective-permute-start(bf16[16,1280]{1,0:T(8,128)(2,1)S(1)} %slice.29), channel_id=1, source_target_pairs={{1,32},{33,64},{65,96},{97,128},{129,160},{161,192},{193,224},{225... | collective-permute-start | bytes 122888 | tf_op jit(solution)/shard_map/ppermute | solution.py:138
  66.9 3.3 %collective-permute-start.3 = (bf16[16,1280]{1,0:T(8,128)(2,1)S(1)}, bf16[16,1280]{1,0:T(8,128)(2,1)S(1)}, u32[]{:S(2)}, u32[]{:S(2)}) collective-permute-start(bf16[16,1280]{1,0:T(8,128)(2,1)S(1)} %slice.29), channel_id=1, source_target_pairs={{1,33},{33,65},{65,97},{97,129},{129,161},{161,193},{193,225},{225... | collective-permute-start | bytes 122888 | tf_op jit(solution)/shard_map/ppermute | solution.py:138
  70.2 4.8 %collective-permute-start.1 = (bf16[640,128]{1,0:T(8,128)(2,1)S(1)}, bf16[640,128]{1,0:T(8,128)(2,1)S(1)}, u32[]{:S(2)}, u32[]{:S(2)}) collective-permute-start(bf16[640,128]{1,0:T(8,128)(2,1)S(1)} %slice.28), channel_id=1, source_target_pairs={{0,32},{32,0},{1,33},{33,1},{2,34},{34,2},{3,35},{35,3},{4,36},{36... | collective-permute-start | bytes 491528 | tf_op jit(solution)/shard_map/ppermute | solution.py:134
  75.0 0.9 fusion.5
  75.9 5.9 %collective-permute-done.1.w_other_ref = bf16[640,128]{1,0:T(8,128)(2,1)S(1)} collective-permute-done((bf16[640,128]{1,0:T(8,128)(2,1)S(1)}, bf16[640,128]{1,0:T(8,128)(2,1)S(1)}, u32[]{:S(2)}, u32[]{:S(2)}) %collective-permute-start.1) | collective-permute-done | bytes 163872 | tf_op jit(solution)/shard_map/ppermute | solution.py:134
  81.8 3.3 %collective-permute-start.4 = (bf16[640,256]{1,0:T(8,128)(2,1)}, bf16[640,256]{1,0:T(8,128)(2,1)S(1)}, u32[]{:S(2)}, u32[]{:S(2)}) collective-permute-start(bf16[640,256]{1,0:T(8,128)(2,1)} %get-tuple-element.21), channel_id=1, source_target_pairs={{0,32},{32,0},{1,33},{33,1},{2,34},{34,2},{3,35},{35,3},{4,36},{36... | collective-permute-start | bytes 983048 | tf_op jit(solution)/shard_map/ppermute | solution.py:143
  85.1 0.5 multiply_exponential_fusion
  85.7 3.0 %partial_s.1 = bf16[4,272,128]{2,1,0:T(8,128)(2,1)} custom-call(s32[2]{0:T(128)S(1)} %pad_add_fusion.place_ref, bf16[512,1408]{1,0:T(8,128)(2,1)S(1)} %bitcast.21, bf16[512,1408]{1,0:T(8,128)(2,1)} %collective-permute-done.other_ref, bf16[16,1280]{1,0:T(8,128)(2,1)S(1)} %add.39.tail_ref, bf16[640,640]{1,0:T(8,128)(2,1)S(1)} %all_gather.9.w_own_ref, ...), custom_call_target="tpu_custom_call" | custom-call | tf_op jit(solution)/shard_map/partial_s/pallas_call | solution.py:148
  88.7 4.4 %all-to-all-start.1 = ((bf16[4,272,128]{2,1,0:T(8,128)(2,1)}), bf16[4,272,128]{2,1,0:T(8,128)(2,1)S(1)}, u32[]{:S(2)}, u32[]{:S(2)}) async-start(bf16[4,272,128]{2,1,0:T(8,128)(2,1)} %partial_s.1), calls=%async_computation.1 | async-start | bytes 557056 | tf_op jit(solution)/shard_map/all_to_all | solution.py:158
  93.1 3.3 %collective-permute-done.4.w_other_ref = bf16[640,256]{1,0:T(8,128)(2,1)S(1)} collective-permute-done((bf16[640,256]{1,0:T(8,128)(2,1)}, bf16[640,256]{1,0:T(8,128)(2,1)S(1)}, u32[]{:S(2)}, u32[]{:S(2)}) %collective-permute-start.4) | collective-permute-done | bytes 327712 | tf_op jit(solution)/shard_map/ppermute | solution.py:143
  96.4 2.9 %collective-permute-start.5 = (bf16[640,256]{1,0:T(8,128)(2,1)}, bf16[640,256]{1,0:T(8,128)(2,1)}, u32[]{:S(2)}, u32[]{:S(2)}) collective-permute-start(bf16[640,256]{1,0:T(8,128)(2,1)} %get-tuple-element.25), channel_id=1, source_target_pairs={{0,32},{32,0},{1,33},{33,1},{2,34},{34,2},{3,35},{35,3},{4,36},{36... | collective-permute-start | bytes 983048 | tf_op jit(solution)/shard_map/ppermute | solution.py:160
  99.4 3.2 %partial_x.1 = bf16[4,272,256]{2,1,0:T(8,128)(2,1)} custom-call(s32[2]{0:T(128)S(1)} %pad_add_fusion.place_ref, bf16[512,1408]{1,0:T(8,128)(2,1)S(1)} %bitcast.22, bf16[512,1408]{1,0:T(8,128)(2,1)} %collective-permute-done.other_ref, bf16[16,1280]{1,0:T(8,128)(2,1)S(1)} %add.39.tail_ref, bf16[640,640]{1,0:T(8,128)(2,1)S(1)} %all_gather.9.w_own_ref, ...), custom_call_target="tpu_custom_call" | custom-call | tf_op jit(solution)/shard_map/partial_x/pallas_call | solution.py:148
  102.5 0.8 broadcast_select_fusion.1
  103.3 6.3 %all-to-all-start.2 = ((bf16[4,272,256]{2,1,0:T(8,128)(2,1)}), bf16[4,272,256]{2,1,0:T(8,128)(2,1)S(1)}, u32[]{:S(2)}, u32[]{:S(2)}) async-start(bf16[4,272,256]{2,1,0:T(8,128)(2,1)} %partial_x.1), calls=%async_computation.2 | async-start | bytes 1114112 | tf_op jit(solution)/shard_map/all_to_all | solution.py:163
  109.6 0.2 fusion.3
  109.8 0.7 reduce_sum.12
  110.5 18.8 %all-gather = bf16[2176,128]{1,0:T(8,128)(2,1)S(1)} all-gather(bf16[272,128]{1,0:T(8,128)(2,1)} %reduce_sum.12), channel_id=2, replica_groups=mesh['zh'=4,'zl'=4,'yh'=2,'x'=4,'yl'=4,'c'=2] {'yl','c'}, dimensions={0}, use_global_device_ids=true | all-gather | bytes 626688 | tf_op jit(solution)/shard_map/all_gather | solution.py:165
  129.3 3.2 %partial_q.1 = bf16[4,272,256]{2,1,0:T(8,128)(2,1)} custom-call(s32[2]{0:T(128)S(1)} %pad_add_fusion.place_ref, bf16[512,1408]{1,0:T(8,128)(2,1)S(1)} %bitcast.24, bf16[512,1408]{1,0:T(8,128)(2,1)} %collective-permute-done.other_ref, bf16[16,1280]{1,0:T(8,128)(2,1)S(1)} %add.39.tail_ref, bf16[640,640]{1,0:T(8,128)(2,1)S(1)} %all_gather.9.w_own_ref, ...), custom_call_target="tpu_custom_call" | custom-call | tf_op jit(solution)/shard_map/partial_q/pallas_call | solution.py:148
  132.5 4.6 %all-to-all-start.3 = ((bf16[4,272,256]{2,1,0:T(8,128)(2,1)}), bf16[4,272,256]{2,1,0:T(8,128)(2,1)S(1)}, u32[]{:S(2)}, u32[]{:S(2)}) async-start(bf16[4,272,256]{2,1,0:T(8,128)(2,1)} %partial_q.1), calls=%async_computation.3 | async-start | bytes 1114112 | tf_op jit(solution)/shard_map/all_to_all | solution.py:168
  137.1 1.2 fusion.4
  138.3 0.1 pad_maximum_fusion.cos_ref
  138.4 0.1 pad_maximum_fusion.1.sin_ref
  138.5 0.2 fusion.2
  138.8 7.9 %all-to-all-done.3.q_parts_ref = bf16[4,272,256]{2,1,0:T(8,128)(2,1)S(1)} async-done(((bf16[4,272,256]{2,1,0:T(8,128)(2,1)}), bf16[4,272,256]{2,1,0:T(8,128)(2,1)S(1)}, u32[]{:S(2)}, u32[]{:S(2)}) %all-to-all-start.3) | async-done | bytes 557088 | tf_op jit(solution)/shard_map/all_to_all | solution.py:168
  146.7 1.7 %rotate_and_convolve.1 = (bf16[256,256]{1,0:T(8,128)(2,1)}, bf16[256,512]{1,0:T(8,128)(2,1)}, bf16[256,256]{1,0:T(8,128)(2,1)}, bf16[256,512]{1,0:T(8,128)(2,1)}) custom-call(bf16[4,272,256]{2,1,0:T(8,128)(2,1)S(1)} %all-to-all-done.3.q_parts_ref, bf16[4,272,256]{2,1,0:T(8,128)(2,1)S(1)} %all-to-all-done.2.x_parts_ref, bf16[8,272,128]{2,1,0:T(8,128)(2,1)S(1)} %bitcast.25, ...), custom_call_target="tpu_custom_call" | custom-call | tf_op jit(solution)/shard_map/rotate_and_convolve/pallas_call | solution.py:187
  (28 shorter events, 0.3 us)
Async XLA Ops:
  1.4 1.0 copy-start
  4.1 8.1 %copy-start.3 = (bf16[40,256]{1,0:T(8,128)(2,1)S(1)}, bf16[40,256]{1,0:T(8,128)(2,1)}, u32[]{:S(2)}) copy-start(bf16[40,256]{1,0:T(8,128)(2,1)} %param.12) | copy-start | bytes 61444
  4.1 8.1 %copy-start.4 = (bf16[40,256]{1,0:T(8,128)(2,1)S(1)}, bf16[40,256]{1,0:T(8,128)(2,1)}, u32[]{:S(2)}) copy-start(bf16[40,256]{1,0:T(8,128)(2,1)} %param.11) | copy-start | bytes 61444
  4.1 8.2 %copy-start.5 = (bf16[40,128]{1,0:T(8,128)(2,1)S(1)}, bf16[40,128]{1,0:T(8,128)(2,1)}, u32[]{:S(2)}) copy-start(bf16[40,128]{1,0:T(8,128)(2,1)} %param.13) | copy-start | bytes 30724
  4.1 49.6 %all-to-all-start = ((bf16[16,32,1408]{2,1,0:T(8,128)(2,1)}), bf16[16,32,1408]{2,1,0:T(8,128)(2,1)S(1)}, u32[]{:S(2)}, u32[]{:S(2)}) async-start(bf16[16,32,1408]{2,1,0:T(8,128)(2,1)} %permute_columns.1), calls=%async_computation | async-start | bytes 2883584 | tf_op jit(solution)/shard_map/all_to_all | solution.py:128
  53.8 31.9 %collective-permute-start = (bf16[512,1408]{1,0:T(8,128)(2,1)S(1)}, bf16[512,1408]{1,0:T(8,128)(2,1)}, u32[]{:S(2)}, u32[]{:S(2)}) collective-permute-start(bf16[512,1408]{1,0:T(8,128)(2,1)S(1)} %bitcast.19), channel_id=1, source_target_pairs={{0,1},{1,0},{2,3},{3,2},{4,5},{5,4},{6,7},{7,6},{8,9},{9,8},{10,11... | collective-permute-start | bytes 4325384 | tf_op jit(solution)/shard_map/ppermute | solution.py:135
  62.3 13.5 %collective-permute-start.2 = (bf16[16,1280]{1,0:T(8,128)(2,1)S(1)}, bf16[16,1280]{1,0:T(8,128)(2,1)S(1)}, u32[]{:S(2)}, u32[]{:S(2)}) collective-permute-start(bf16[16,1280]{1,0:T(8,128)(2,1)S(1)} %slice.29), channel_id=1, source_target_pairs={{1,32},{33,64},{65,96},{97,128},{129,160},{161,192},{193,224},{225... | collective-permute-start | bytes 122888 | tf_op jit(solution)/shard_map/ppermute | solution.py:138
  66.9 8.9 %collective-permute-start.3 = (bf16[16,1280]{1,0:T(8,128)(2,1)S(1)}, bf16[16,1280]{1,0:T(8,128)(2,1)S(1)}, u32[]{:S(2)}, u32[]{:S(2)}) collective-permute-start(bf16[16,1280]{1,0:T(8,128)(2,1)S(1)} %slice.29), channel_id=1, source_target_pairs={{1,33},{33,65},{65,97},{97,129},{129,161},{161,193},{193,225},{225... | collective-permute-start | bytes 122888 | tf_op jit(solution)/shard_map/ppermute | solution.py:138
  70.2 11.5 %collective-permute-start.1 = (bf16[640,128]{1,0:T(8,128)(2,1)S(1)}, bf16[640,128]{1,0:T(8,128)(2,1)S(1)}, u32[]{:S(2)}, u32[]{:S(2)}) collective-permute-start(bf16[640,128]{1,0:T(8,128)(2,1)S(1)} %slice.28), channel_id=1, source_target_pairs={{0,32},{32,0},{1,33},{33,1},{2,34},{34,2},{3,35},{35,3},{4,36},{36... | collective-permute-start | bytes 491528 | tf_op jit(solution)/shard_map/ppermute | solution.py:134
  81.8 14.6 %collective-permute-start.4 = (bf16[640,256]{1,0:T(8,128)(2,1)}, bf16[640,256]{1,0:T(8,128)(2,1)S(1)}, u32[]{:S(2)}, u32[]{:S(2)}) collective-permute-start(bf16[640,256]{1,0:T(8,128)(2,1)} %get-tuple-element.21), channel_id=1, source_target_pairs={{0,32},{32,0},{1,33},{33,1},{2,34},{34,2},{3,35},{35,3},{4,36},{36... | collective-permute-start | bytes 983048 | tf_op jit(solution)/shard_map/ppermute | solution.py:143
  88.7 14.6 %all-to-all-start.1 = ((bf16[4,272,128]{2,1,0:T(8,128)(2,1)}), bf16[4,272,128]{2,1,0:T(8,128)(2,1)S(1)}, u32[]{:S(2)}, u32[]{:S(2)}) async-start(bf16[4,272,128]{2,1,0:T(8,128)(2,1)} %partial_s.1), calls=%async_computation.1 | async-start | bytes 557056 | tf_op jit(solution)/shard_map/all_to_all | solution.py:158
  96.4 32.9 %collective-permute-start.5 = (bf16[640,256]{1,0:T(8,128)(2,1)}, bf16[640,256]{1,0:T(8,128)(2,1)}, u32[]{:S(2)}, u32[]{:S(2)}) collective-permute-start(bf16[640,256]{1,0:T(8,128)(2,1)} %get-tuple-element.25), channel_id=1, source_target_pairs={{0,32},{32,0},{1,33},{33,1},{2,34},{34,2},{3,35},{35,3},{4,36},{36... | collective-permute-start | bytes 983048 | tf_op jit(solution)/shard_map/ppermute | solution.py:160
  103.3 25.9 %all-to-all-start.2 = ((bf16[4,272,256]{2,1,0:T(8,128)(2,1)}), bf16[4,272,256]{2,1,0:T(8,128)(2,1)S(1)}, u32[]{:S(2)}, u32[]{:S(2)}) async-start(bf16[4,272,256]{2,1,0:T(8,128)(2,1)} %partial_x.1), calls=%async_computation.2 | async-start | bytes 1114112 | tf_op jit(solution)/shard_map/all_to_all | solution.py:163
  132.5 14.2 %copy-start.1 = (f32[4,512]{1,0:T(4,128)S(1)}, f32[4,512]{1,0:T(4,128)}, u32[]{:S(2)}) copy-start(f32[4,512]{1,0:T(4,128)} %tbc_ref.1) | copy-start | bytes 24580
  132.5 14.2 %copy-start.2 = (f32[4,256]{1,0:T(4,128)S(1)}, f32[4,256]{1,0:T(4,128)}, u32[]{:S(2)}) copy-start(f32[4,256]{1,0:T(4,128)} %tx_ref.1) | copy-start | bytes 12292
  132.5 14.1 %all-to-all-start.3 = ((bf16[4,272,256]{2,1,0:T(8,128)(2,1)}), bf16[4,272,256]{2,1,0:T(8,128)(2,1)S(1)}, u32[]{:S(2)}, u32[]{:S(2)}) async-start(bf16[4,272,256]{2,1,0:T(8,128)(2,1)} %partial_q.1), calls=%async_computation.3 | async-start | bytes 1114112 | tf_op jit(solution)/shard_map/all_to_all | solution.py:168

commit v9 on v6

--- a/solution.py
+++ b/solution.py
@@ -16,7 +16,7 @@
 FSDP = AXES[:4]
 
 
-def permute_kernel(tokens_ref, extra_ref, out_ref, stack_ref):
+def permute_kernel(tokens_ref, out_ref, stack_ref):
     for p in range(8):
         stack_ref[p * 32 : (p + 1) * 32, :] = tokens_ref[:, p * 640 : (p + 1) * 640]
     source = lax.broadcasted_iota(jnp.int32, (640, 640), 0)
@@ -34,8 +34,7 @@
             axis=1,
         ).astype(jnp.bfloat16)
         for yl in range(4):
-            out_ref[x * 4 + yl, :, 0:1280] = piece
-            out_ref[x * 4 + yl, :, 1280:] = extra_ref[...]
+            out_ref[x * 4 + yl] = piece
 
 
 def partial_kernel(first, place_ref, own_ref, other_ref, tail_ref, w_own_ref, w_other_ref, out_ref):
@@ -98,8 +97,8 @@
         x_ref[:, cols] = convolved(tx_ref, cols)
     for block in range(4):
         cols = slice(block * HD, (block + 1) * HD)
-        k_ref[:, cols] = turned(s_ref[block, HALO:, :])
-        ext_ref[...] = s_ref[4 + block].astype(jnp.float32)
+        k_ref[:, cols] = turned(s_ref[block, HALO : HALO + rows, :])
+        ext_ref[...] = s_ref[4 + block, 0 : HALO + rows, :].astype(jnp.float32)
         bc_ref[:, cols] = convolved(tbc_ref, cols)
 
 
@@ -114,25 +113,23 @@
     core = lax.axis_index("c").astype(jnp.int32)
     z = ("zh", "zl")
 
-    extra = jnp.stack([positions >> 8, positions & 255, offsets >> 8, offsets & 255], axis=1)
-    extra = jnp.pad(extra, ((0, 0), (0, HD - 4))).astype(bf16)
     split = pl.pallas_call(
         permute_kernel,
-        out_shape=jax.ShapeDtypeStruct((16, rows, quarter + HD), bf16),
-        in_specs=[vmem, vmem],
+        out_shape=jax.ShapeDtypeStruct((16, rows, quarter), bf16),
+        in_specs=[vmem],
         out_specs=vmem,
         scratch_shapes=[pltpu.VMEM((8 * rows, width // 8), bf16)],
         compiler_params=params,
         name="permute_columns",
-    )(tokens, extra)
-    own_t = lax.all_to_all(split, ("x", "yl"), 0, 0).reshape(16 * rows, quarter + HD)
+    )(tokens)
+    own_t = lax.all_to_all(split, ("x", "yl"), 0, 0).reshape(16 * rows, quarter)
 
     weight = jnp.concatenate([q_weight, x_weight, shared_weight], axis=1)
     partner = lax.ppermute(weight, "yh", [(0, 1), (1, 0)])
     w_own = lax.all_gather(weight, z, axis=0, tiled=True)
     own_t, w_own, partner = lax.optimization_barrier((own_t, w_own, partner))
     other_t = lax.ppermute(own_t, "c", [(0, 1), (1, 0)])
-    tail = own_t[16 * rows - HALO :, :quarter]
+    tail = own_t[16 * rows - HALO :]
     sources = [(2 * i + 1, 2 * i + 2) for i in range(31)]
     tail = lax.ppermute(tail, ("zh", "zl", "yh", "c"), sources) + lax.ppermute(
         tail, ("zh", "zl", "yh", "c"), [(source, target + 1) for source, target in sources]
@@ -159,15 +156,12 @@
     s_parts, qx_part = lax.optimization_barrier((s_parts, qx_part))
     qx_parts = lax.all_to_all(qx_part, "x", 0, 0)
     s_own = jnp.sum(s_parts.astype(jnp.float32), axis=0).astype(bf16)
-    s_all = lax.all_gather(s_own, ("yl", "c"), axis=0)
+    extra = jnp.stack([positions >> 8, positions & 255, offsets >> 8, offsets & 255], axis=1)
+    extra = jnp.pad(extra, ((0, 0), (0, HD - 4))).astype(bf16)
+    s_all = lax.all_gather(jnp.concatenate([s_own, extra], axis=0), ("yl", "c"), axis=0)
     qx_parts, s_all = lax.optimization_barrier((qx_parts, s_all))
 
-    at = lax.axis_index("x") * (4 * rows)
-    near = lax.dynamic_slice(own_t, (at, quarter), (4 * rows, HD)).reshape(4, 1, rows, HD)
-    far = lax.dynamic_slice(other_t, (at, quarter), (4 * rows, HD)).reshape(4, 1, rows, HD)
-    first = jnp.where(core == 0, near, far)
-    second = jnp.where(core == 0, far, near)
-    places = jnp.concatenate([first, second], axis=1).reshape(group_rows, HD)[:, :4].astype(jnp.float32)
+    places = s_all[:, HALO + group_rows :, :4].reshape(group_rows, 4).astype(jnp.float32)
     half = HD // 2
     index = jnp.arange(half, dtype=jnp.float32)
     inverse = jnp.exp(-jnp.log(jnp.float32(rope_base)) * index / jnp.float32(half))

time: 138 us -> 138 us (level)
  blocking collectives: 84.8 us -> 82.3 us
  waiting for transfers between devices: 0.75 us -> 3.16 us
  other arithmetic: 2.78 us -> 0.97 us
  starting transfers between devices: 36.4 us -> 37.9 us
    all_to_all x1, waiting for transfers between devices: 0.74 us -> 3.14 us  [shards(): s_parts = lax.all_to_all(s_part, 'x', 0, 0)]
  transfers between devices with their start and end apart: 7 -> 7, of which waited for: 1 -> 1; matrix products, arithmetic and copies ran while one was open for 2% -> 0% of each run, Pallas kernels for 2% -> 2%
where the time goes in v9:
time: 138 us; the launch traced here: 137 us
  blocking collectives  82.3 us (60%)
  starting transfers between devices  37.9 us (27%)
  Pallas kernels  9.55 us (7%)
  waiting for transfers between devices  3.16 us (2%)
  local copies, waits for them, and re-layouts  2.71 us (2%)
    all_gather x1, blocking collectives, shards(): w_own = lax.all_gather(weight, z, axis=0, tiled=True)  40.8 us
    all_gather x1, blocking collectives, shards(): w_other = lax.all_gather(partner, z, axis=0, tiled=True)  25.7 us
    all_gather x1, blocking collectives, shards(): lax.all_gather(jnp.concatenate([s_own, extra], axis=0), ('yl', 'c'), axis=0)  15.7 us
    ppermute x1, starting transfers between devices, shards(): other_t = lax.ppermute(own_t, 'c', [(0, 1), (1, 0)])  9.45 us
    all_to_all x1, starting transfers between devices, shards(): own_t = lax.all_to_all(split, ('x', 'yl'), 0, 0).reshape(16 * rows, quarter)  8.12 us
    pallas_call x2, Pallas kernels, partial(): pl.pallas_call(functools.partial(partial_kernel, first), out_shape=jax.Sh...  6.13 us
    ppermute x1, starting transfers between devices, shards(): partner = lax.ppermute(weight, 'yh', [(0, 1), (1, 0)])  4.76 us
    all_to_all x1, starting transfers between devices, shards(): s_parts = lax.all_to_all(s_part, 'x', 0, 0)  4.4 us
  transfers between devices with their start and end apart: 7, of which 1 were waited for; matrix products, arithmetic and copies ran while one was open for 0% of the time, Pallas kernels for 2%

profile of v9, /device:TPU:1, one launch (start us, length us, event | category | flops | bytes accessed | tf_op | source)
XLA Modules:
  0.0 137.4 jit_solution(1453795377716557416)
XLA Ops:
  0.6 1.0 copy-done.1
  1.6 1.7 %permute_columns.1 = bf16[16,32,1280]{2,1,0:T(8,128)(2,1)} custom-call(bf16[32,5120]{1,0:T(8,128)(2,1)S(1)} %copy-done.1), custom_call_target="tpu_custom_call" | custom-call | tf_op jit(solution)/shard_map/permute_columns/pallas_call | solution.py:116
  3.3 8.1 %all-to-all-start = ((bf16[16,32,1280]{2,1,0:T(8,128)(2,1)}), bf16[16,32,1280]{2,1,0:T(8,128)(2,1)S(1)}, u32[]{:S(2)}, u32[]{:S(2)}) async-start(bf16[16,32,1280]{2,1,0:T(8,128)(2,1)} %permute_columns.1), calls=%async_computation | async-start | bytes 2621440 | tf_op jit(solution)/shard_map/all_to_all | solution.py:125
  11.5 4.8 %collective-permute-start = (bf16[40,640]{1,0:T(8,128)(2,1)S(1)}, bf16[40,640]{1,0:T(8,128)(2,1)S(1)}, u32[]{:S(2)}, u32[]{:S(2)}) collective-permute-start(bf16[40,640]{1,0:T(8,128)(2,1)S(1)} %constant_dynamic-update-slice_fusion), channel_id=1, source_target_pairs={{0,32},{32,0},{1,33},{33,1},{2,34},{34,2},{3,35},{35,3},{4,36},{36... | collective-permute-start | bytes 153608 | tf_op jit(solution)/shard_map/ppermute | solution.py:128
  16.3 40.8 %all_gather.12.w_own_ref = bf16[640,640]{1,0:T(8,128)(2,1)S(1)} all-gather(bf16[40,640]{1,0:T(8,128)(2,1)S(1)} %constant_dynamic-update-slice_fusion), channel_id=1, replica_groups=mesh['zh'=4,'zl'=4,'yh'=2,'x'=4,'yl'=4,'c'=2] {'zh','zl'}, dimensions={0}, use_global_device_ids=true | all-gather | bytes 870400 | tf_op jit(solution)/shard_map/all_gather | solution.py:129
  57.1 9.4 %collective-permute-start.3 = (bf16[512,1280]{1,0:T(8,128)(2,1)S(1)}, bf16[512,1280]{1,0:T(8,128)(2,1)}, u32[]{:S(2)}, u32[]{:S(2)}) collective-permute-start(bf16[512,1280]{1,0:T(8,128)(2,1)S(1)} %bitcast.17), channel_id=1, source_target_pairs={{0,1},{1,0},{2,3},{3,2},{4,5},{5,4},{6,7},{7,6},{8,9},{9,8},{10,11... | collective-permute-start | bytes 3932168 | tf_op jit(solution)/shard_map/ppermute | solution.py:131
  66.5 0.1 pad_add_fusion.place_ref
  66.6 4.3 %collective-permute-start.1 = (bf16[16,1280]{1,0:T(8,128)(2,1)S(1)}, bf16[16,1280]{1,0:T(8,128)(2,1)S(1)}, u32[]{:S(2)}, u32[]{:S(2)}) collective-permute-start(bf16[16,1280]{1,0:T(8,128)(2,1)S(1)} %slice.18), channel_id=1, source_target_pairs={{1,32},{33,64},{65,96},{97,128},{129,160},{161,192},{193,224},{225... | collective-permute-start | bytes 122888 | tf_op jit(solution)/shard_map/ppermute | solution.py:134
  70.9 3.3 %collective-permute-start.2 = (bf16[16,1280]{1,0:T(8,128)(2,1)S(1)}, bf16[16,1280]{1,0:T(8,128)(2,1)S(1)}, u32[]{:S(2)}, u32[]{:S(2)}) collective-permute-start(bf16[16,1280]{1,0:T(8,128)(2,1)S(1)} %slice.18), channel_id=1, source_target_pairs={{1,33},{33,65},{65,97},{97,129},{129,161},{161,193},{193,225},{225... | collective-permute-start | bytes 122888 | tf_op jit(solution)/shard_map/ppermute | solution.py:134
  74.2 25.7 %all_gather.13.w_other_ref = bf16[640,640]{1,0:T(8,128)(2,1)S(1)} all-gather(bf16[40,640]{1,0:T(8,128)(2,1)S(1)} %collective-permute-done), channel_id=1, replica_groups=mesh['zh'=4,'zl'=4,'yh'=2,'x'=4,'yl'=4,'c'=2] {'zh','zl'}, dimensions={0}, use_global_device_ids=true | all-gather | bytes 870400 | tf_op jit(solution)/shard_map/all_gather | solution.py:138
  100.0 0.0 collective-permute-done.2
  100.0 0.0 collective-permute-done.3.other_ref
  100.0 3.0 %partial_s.1 = bf16[4,272,128]{2,1,0:T(8,128)(2,1)} custom-call(s32[2]{0:T(128)S(1)} %pad_add_fusion.place_ref, bf16[512,1280]{1,0:T(8,128)(2,1)S(1)} %bitcast.19, bf16[512,1280]{1,0:T(8,128)(2,1)} %collective-permute-done.3.other_ref, bf16[16,1280]{1,0:T(8,128)(2,1)S(1)} %add.35.tail_ref, bf16[640,640]{1,0:T(8,128)(2,1)S(1)} %all_gather.12.w_own_ref, ...), custom_call_target="tpu_custom_call" | custom-call | tf_op jit(solution)/shard_map/partial_s/pallas_call | solution.py:143
  103.0 4.4 %all-to-all-start.1 = ((bf16[4,272,128]{2,1,0:T(8,128)(2,1)}), bf16[4,272,128]{2,1,0:T(8,128)(2,1)S(1)}, u32[]{:S(2)}, u32[]{:S(2)}) async-start(bf16[4,272,128]{2,1,0:T(8,128)(2,1)} %partial_s.1), calls=%async_computation.1 | async-start | bytes 557056 | tf_op jit(solution)/shard_map/all_to_all | solution.py:154
  107.4 3.2 %partial_qx.1 = bf16[4,272,512]{2,1,0:T(8,128)(2,1)S(1)} custom-call(s32[2]{0:T(128)S(1)} %pad_add_fusion.place_ref, bf16[512,1280]{1,0:T(8,128)(2,1)S(1)} %bitcast.20, bf16[512,1280]{1,0:T(8,128)(2,1)} %collective-permute-done.3.other_ref, bf16[16,1280]{1,0:T(8,128)(2,1)S(1)} %add.35.tail_ref, bf16[640,640]{1,0:T(8,128)(2,1)S(1)} %all_gather.12.w_own_ref, ...), custom_call_target="tpu_custom_call" | custom-call | tf_op jit(solution)/shard_map/partial_qx/pallas_call | solution.py:143
  110.6 1.0 copy-done
  111.6 3.1 %all-to-all-done.1 = bf16[4,272,128]{2,1,0:T(8,128)(2,1)S(1)} async-done(((bf16[4,272,128]{2,1,0:T(8,128)(2,1)}), bf16[4,272,128]{2,1,0:T(8,128)(2,1)S(1)}, u32[]{:S(2)}, u32[]{:S(2)}) %all-to-all-start.1) | async-done | bytes 278560 | tf_op jit(solution)/shard_map/all_to_all | solution.py:154
  114.7 3.5 %all-to-all-start.2 = ((bf16[4,272,512]{2,1,0:T(8,128)(2,1)}), bf16[4,272,512]{2,1,0:T(8,128)(2,1)S(1)}, u32[]{:S(2)}, u32[]{:S(2)}) async-start(bf16[4,272,512]{2,1,0:T(8,128)(2,1)} %copy-done), calls=%async_computation.2 | async-start | bytes 2228224 | tf_op jit(solution)/shard_map/all_to_all | solution.py:157
  118.3 0.1 copy.22
  118.5 15.7 %all-gather = bf16[2432,128]{1,0:T(8,128)(2,1)S(1)} all-gather(bf16[304,128]{1,0:T(8,128)(2,1)S(1)} %fusion.1), channel_id=2, replica_groups=mesh['zh'=4,'zl'=4,'yh'=2,'x'=4,'yl'=4,'c'=2] {'yl','c'}, dimensions={0}, use_global_device_ids=true | all-gather | bytes 700416 | tf_op jit(solution)/shard_map/all_gather | solution.py:161
  134.2 0.0 copy-start.2
  134.3 0.0 copy-start.3
  134.3 0.2 fusion.3
  134.4 0.1 copy.19
  134.5 0.1 copy.18
  134.6 0.6 fusion.2
  135.2 0.1 pad_maximum_fusion.cos_ref
  135.3 0.1 copy.21
  135.4 0.1 copy.20
  135.4 0.1 pad_maximum_fusion.1.sin_ref
  135.6 0.1 broadcast_in_dim.5.rel_ref
  135.7 1.7 %rotate_and_convolve.1 = (bf16[256,256]{1,0:T(8,128)(2,1)}, bf16[256,512]{1,0:T(8,128)(2,1)}, bf16[256,256]{1,0:T(8,128)(2,1)}, bf16[256,512]{1,0:T(8,128)(2,1)}) custom-call(bf16[4,272,512]{2,1,0:T(8,128)(2,1)S(1)} %all-to-all-done.2.parts_ref, bf16[8,304,128]{2,1,0:T(8,128)(2,1)S(1)} %bitcast.22, f32[256,128]{1,0:T(8,128)S(1)} %pad_maximum_fusion.cos_ref, ...), custom_call_target="tpu_custom_call" | custom-call | tf_op jit(solution)/shard_map/rotate_and_convolve/pallas_call | solution.py:176
  (32 shorter events, 0.2 us)
Async XLA Ops:
  0.6 1.0 copy-start.1
  3.3 8.1 %copy-start.4 = (bf16[40,256]{1,0:T(8,128)(2,1)S(1)}, bf16[40,256]{1,0:T(8,128)(2,1)}, u32[]{:S(2)}) copy-start(bf16[40,256]{1,0:T(8,128)(2,1)} %param.11) | copy-start | bytes 61444
  3.3 8.2 %copy-start.5 = (bf16[40,256]{1,0:T(8,128)(2,1)S(1)}, bf16[40,256]{1,0:T(8,128)(2,1)}, u32[]{:S(2)}) copy-start(bf16[40,256]{1,0:T(8,128)(2,1)} %param.12) | copy-start | bytes 61444
  3.3 8.2 %copy-start.6 = (bf16[40,128]{1,0:T(8,128)(2,1)S(1)}, bf16[40,128]{1,0:T(8,128)(2,1)}, u32[]{:S(2)}) copy-start(bf16[40,128]{1,0:T(8,128)(2,1)} %param.13) | copy-start | bytes 30724
  3.3 53.8 %all-to-all-start = ((bf16[16,32,1280]{2,1,0:T(8,128)(2,1)}), bf16[16,32,1280]{2,1,0:T(8,128)(2,1)S(1)}, u32[]{:S(2)}, u32[]{:S(2)}) async-start(bf16[16,32,1280]{2,1,0:T(8,128)(2,1)} %permute_columns.1), calls=%async_computation | async-start | bytes 2621440 | tf_op jit(solution)/shard_map/all_to_all | solution.py:125
  11.5 45.6 %collective-permute-start = (bf16[40,640]{1,0:T(8,128)(2,1)S(1)}, bf16[40,640]{1,0:T(8,128)(2,1)S(1)}, u32[]{:S(2)}, u32[]{:S(2)}) collective-permute-start(bf16[40,640]{1,0:T(8,128)(2,1)S(1)} %constant_dynamic-update-slice_fusion), channel_id=1, source_target_pairs={{0,32},{32,0},{1,33},{33,1},{2,34},{34,2},{3,35},{35,3},{4,36},{36... | collective-permute-start | bytes 153608 | tf_op jit(solution)/shard_map/ppermute | solution.py:128
  57.1 42.9 %collective-permute-start.3 = (bf16[512,1280]{1,0:T(8,128)(2,1)S(1)}, bf16[512,1280]{1,0:T(8,128)(2,1)}, u32[]{:S(2)}, u32[]{:S(2)}) collective-permute-start(bf16[512,1280]{1,0:T(8,128)(2,1)S(1)} %bitcast.17), channel_id=1, source_target_pairs={{0,1},{1,0},{2,3},{3,2},{4,5},{5,4},{6,7},{7,6},{8,9},{9,8},{10,11... | collective-permute-start | bytes 3932168 | tf_op jit(solution)/shard_map/ppermute | solution.py:131
  66.6 33.4 %collective-permute-start.1 = (bf16[16,1280]{1,0:T(8,128)(2,1)S(1)}, bf16[16,1280]{1,0:T(8,128)(2,1)S(1)}, u32[]{:S(2)}, u32[]{:S(2)}) collective-permute-start(bf16[16,1280]{1,0:T(8,128)(2,1)S(1)} %slice.18), channel_id=1, source_target_pairs={{1,32},{33,64},{65,96},{97,128},{129,160},{161,192},{193,224},{225... | collective-permute-start | bytes 122888 | tf_op jit(solution)/shard_map/ppermute | solution.py:134
  70.9 29.1 %collective-permute-start.2 = (bf16[16,1280]{1,0:T(8,128)(2,1)S(1)}, bf16[16,1280]{1,0:T(8,128)(2,1)S(1)}, u32[]{:S(2)}, u32[]{:S(2)}) collective-permute-start(bf16[16,1280]{1,0:T(8,128)(2,1)S(1)} %slice.18), channel_id=1, source_target_pairs={{1,33},{33,65},{65,97},{97,129},{129,161},{161,193},{193,225},{225... | collective-permute-start | bytes 122888 | tf_op jit(solution)/shard_map/ppermute | solution.py:134
  103.0 11.7 %all-to-all-start.1 = ((bf16[4,272,128]{2,1,0:T(8,128)(2,1)}), bf16[4,272,128]{2,1,0:T(8,128)(2,1)S(1)}, u32[]{:S(2)}, u32[]{:S(2)}) async-start(bf16[4,272,128]{2,1,0:T(8,128)(2,1)} %partial_s.1), calls=%async_computation.1 | async-start | bytes 557056 | tf_op jit(solution)/shard_map/all_to_all | solution.py:154
  110.6 1.0 copy-start
  111.6 6.7 %copy-start.7 = (s32[32]{0:T(128)S(1)}, s32[32]{0:T(128)}, u32[]{:S(2)}) copy-start(s32[32]{0:T(128)} %param.10) | copy-start | bytes 388
  111.6 6.7 %copy-start.8 = (s32[32]{0:T(128)S(1)}, s32[32]{0:T(128)}, u32[]{:S(2)}) copy-start(s32[32]{0:T(128)} %param.9) | copy-start | bytes 388
  114.7 19.5 %all-to-all-start.2 = ((bf16[4,272,512]{2,1,0:T(8,128)(2,1)}), bf16[4,272,512]{2,1,0:T(8,128)(2,1)S(1)}, u32[]{:S(2)}, u32[]{:S(2)}) async-start(bf16[4,272,512]{2,1,0:T(8,128)(2,1)} %copy-done), calls=%async_computation.2 | async-start | bytes 2228224 | tf_op jit(solution)/shard_map/all_to_all | solution.py:157
  134.2 1.4 %copy-start.2 = (f32[4,512]{1,0:T(4,128)S(1)}, f32[4,512]{1,0:T(4,128)}, u32[]{:S(2)}) copy-start(f32[4,512]{1,0:T(4,128)} %tbc_ref.1) | copy-start | bytes 24580
  134.3 1.4 %copy-start.3 = (f32[4,256]{1,0:T(4,128)S(1)}, f32[4,256]{1,0:T(4,128)}, u32[]{:S(2)}) copy-start(f32[4,256]{1,0:T(4,128)} %tx_ref.1) | copy-start | bytes 12292

commit v10 on v9

--- a/solution.py
+++ b/solution.py
@@ -45,22 +45,18 @@
     columns = out_ref.shape[2]
     for start in range(0, columns, 256):
         cols = slice(start, min(start + 256, columns))
-        w_cols = slice(first + cols.start, first + cols.stop)
-        for mine in (True, False):
-            part = 0.0
-            for at_k, w_ref in ((near, w_own_ref), (far, w_other_ref)):
-                rows = (own_ref if mine else other_ref)[:, at_k]
-                if not mine:
-                    rows = jnp.concatenate([rows, tail_ref[:, at_k]], axis=0)
-                part = part + jnp.dot(rows, w_ref[:, w_cols], preferred_element_type=jnp.float32)
+        own_cols = slice(first + cols.start, first + cols.stop)
+        for rows_ref, place in ((own_ref, core), (other_ref, 1 - core), (tail_ref, None)):
+            part = jnp.dot(rows_ref[:, near], w_own_ref[:, own_cols], preferred_element_type=jnp.float32)
+            part = part + jnp.dot(rows_ref[:, far], w_other_ref[:, own_cols], preferred_element_type=jnp.float32)
             part = part.astype(jnp.bfloat16)
-            place = core if mine else 1 - core
+            if place is None:
+                out_ref[0, 0:HALO, cols] = part
+                continue
             for x in range(4):
                 for yl in range(4):
                     at = pl.multiple_of(HALO + yl * 64 + place * 32, 16)
                     out_ref[x, pl.ds(at, 32), cols] = part[(x * 4 + yl) * 32 : (x * 4 + yl + 1) * 32]
-            if not mine:
-                out_ref[0, 0:HALO, cols] = part[512 : 512 + HALO]
     for x in range(3):
         out_ref[x + 1, 0:HALO, :] = out_ref[x, 256 : 256 + HALO, :]
 

time: 138 us -> 138 us (level)
  no operation moved by 1% of the time
where the time goes in v10:
time: 138 us; the launch traced here: 137 us
  blocking collectives  82.3 us (60%)
  starting transfers between devices  37.9 us (27%)
  Pallas kernels  9.66 us (7%)
  waiting for transfers between devices  3.02 us (2%)
  local copies, waits for them, and re-layouts  2.71 us (2%)
    all_gather x1, blocking collectives, shards(): w_own = lax.all_gather(weight, z, axis=0, tiled=True)  40.8 us
    all_gather x1, blocking collectives, shards(): w_other = lax.all_gather(partner, z, axis=0, tiled=True)  25.7 us
    all_gather x1, blocking collectives, shards(): lax.all_gather(jnp.concatenate([s_own, extra], axis=0), ('yl', 'c'), axis=0)  15.7 us
    ppermute x1, starting transfers between devices, shards(): other_t = lax.ppermute(own_t, 'c', [(0, 1), (1, 0)])  9.45 us
    all_to_all x1, starting transfers between devices, shards(): own_t = lax.all_to_all(split, ('x', 'yl'), 0, 0).reshape(16 * rows, quarter)  8.12 us
    pallas_call x2, Pallas kernels, partial(): pl.pallas_call(functools.partial(partial_kernel, first), out_shape=jax.Sh...  6.24 us
    ppermute x1, starting transfers between devices, shards(): partner = lax.ppermute(weight, 'yh', [(0, 1), (1, 0)])  4.76 us
    all_to_all x1, starting transfers between devices, shards(): s_parts = lax.all_to_all(s_part, 'x', 0, 0)  4.41 us
  transfers between devices with their start and end apart: 7, of which 1 were waited for; matrix products, arithmetic and copies ran while one was open for 0% of the time, Pallas kernels for 2%

profile of v10, /device:TPU:1, one launch (start us, length us, event | category | flops | bytes accessed | tf_op | source)
XLA Modules:
  0.0 137.4 jit_solution(13967219604779274824)
XLA Ops:
  0.6 1.0 copy-done.1
  1.6 1.7 %permute_columns.1 = bf16[16,32,1280]{2,1,0:T(8,128)(2,1)} custom-call(bf16[32,5120]{1,0:T(8,128)(2,1)S(1)} %copy-done.1), custom_call_target="tpu_custom_call" | custom-call | tf_op jit(solution)/shard_map/permute_columns/pallas_call | solution.py:112
  3.3 8.1 %all-to-all-start = ((bf16[16,32,1280]{2,1,0:T(8,128)(2,1)}), bf16[16,32,1280]{2,1,0:T(8,128)(2,1)S(1)}, u32[]{:S(2)}, u32[]{:S(2)}) async-start(bf16[16,32,1280]{2,1,0:T(8,128)(2,1)} %permute_columns.1), calls=%async_computation | async-start | bytes 2621440 | tf_op jit(solution)/shard_map/all_to_all | solution.py:121
  11.5 4.8 %collective-permute-start = (bf16[40,640]{1,0:T(8,128)(2,1)S(1)}, bf16[40,640]{1,0:T(8,128)(2,1)S(1)}, u32[]{:S(2)}, u32[]{:S(2)}) collective-permute-start(bf16[40,640]{1,0:T(8,128)(2,1)S(1)} %constant_dynamic-update-slice_fusion), channel_id=1, source_target_pairs={{0,32},{32,0},{1,33},{33,1},{2,34},{34,2},{3,35},{35,3},{4,36},{36... | collective-permute-start | bytes 153608 | tf_op jit(solution)/shard_map/ppermute | solution.py:124
  16.3 40.8 %all_gather.12.w_own_ref = bf16[640,640]{1,0:T(8,128)(2,1)S(1)} all-gather(bf16[40,640]{1,0:T(8,128)(2,1)S(1)} %constant_dynamic-update-slice_fusion), channel_id=1, replica_groups=mesh['zh'=4,'zl'=4,'yh'=2,'x'=4,'yl'=4,'c'=2] {'zh','zl'}, dimensions={0}, use_global_device_ids=true | all-gather | bytes 870400 | tf_op jit(solution)/shard_map/all_gather | solution.py:125
  57.1 0.0 all-to-all-done
  57.1 9.4 %collective-permute-start.3 = (bf16[512,1280]{1,0:T(8,128)(2,1)S(1)}, bf16[512,1280]{1,0:T(8,128)(2,1)}, u32[]{:S(2)}, u32[]{:S(2)}) collective-permute-start(bf16[512,1280]{1,0:T(8,128)(2,1)S(1)} %bitcast.17), channel_id=1, source_target_pairs={{0,1},{1,0},{2,3},{3,2},{4,5},{5,4},{6,7},{7,6},{8,9},{9,8},{10,11... | collective-permute-start | bytes 3932168 | tf_op jit(solution)/shard_map/ppermute | solution.py:127
  66.5 0.1 pad_add_fusion.place_ref
  66.6 4.3 %collective-permute-start.1 = (bf16[16,1280]{1,0:T(8,128)(2,1)S(1)}, bf16[16,1280]{1,0:T(8,128)(2,1)S(1)}, u32[]{:S(2)}, u32[]{:S(2)}) collective-permute-start(bf16[16,1280]{1,0:T(8,128)(2,1)S(1)} %slice.18), channel_id=1, source_target_pairs={{1,32},{33,64},{65,96},{97,128},{129,160},{161,192},{193,224},{225... | collective-permute-start | bytes 122888 | tf_op jit(solution)/shard_map/ppermute | solution.py:130
  70.9 3.3 %collective-permute-start.2 = (bf16[16,1280]{1,0:T(8,128)(2,1)S(1)}, bf16[16,1280]{1,0:T(8,128)(2,1)S(1)}, u32[]{:S(2)}, u32[]{:S(2)}) collective-permute-start(bf16[16,1280]{1,0:T(8,128)(2,1)S(1)} %slice.18), channel_id=1, source_target_pairs={{1,33},{33,65},{65,97},{97,129},{129,161},{161,193},{193,225},{225... | collective-permute-start | bytes 122888 | tf_op jit(solution)/shard_map/ppermute | solution.py:130
  74.2 25.7 %all_gather.13.w_other_ref = bf16[640,640]{1,0:T(8,128)(2,1)S(1)} all-gather(bf16[40,640]{1,0:T(8,128)(2,1)S(1)} %collective-permute-done), channel_id=1, replica_groups=mesh['zh'=4,'zl'=4,'yh'=2,'x'=4,'yl'=4,'c'=2] {'zh','zl'}, dimensions={0}, use_global_device_ids=true | all-gather | bytes 870400 | tf_op jit(solution)/shard_map/all_gather | solution.py:134
  100.0 0.0 collective-permute-done.1
  100.0 2.9 %partial_s.1 = bf16[4,272,128]{2,1,0:T(8,128)(2,1)} custom-call(s32[2]{0:T(128)S(1)} %pad_add_fusion.place_ref, bf16[512,1280]{1,0:T(8,128)(2,1)S(1)} %bitcast.19, bf16[512,1280]{1,0:T(8,128)(2,1)} %collective-permute-done.3.other_ref, bf16[16,1280]{1,0:T(8,128)(2,1)S(1)} %add.35.tail_ref, bf16[640,640]{1,0:T(8,128)(2,1)S(1)} %all_gather.12.w_own_ref, ...), custom_call_target="tpu_custom_call" | custom-call | tf_op jit(solution)/shard_map/partial_s/pallas_call | solution.py:139
  102.9 4.4 %all-to-all-start.1 = ((bf16[4,272,128]{2,1,0:T(8,128)(2,1)}), bf16[4,272,128]{2,1,0:T(8,128)(2,1)S(1)}, u32[]{:S(2)}, u32[]{:S(2)}) async-start(bf16[4,272,128]{2,1,0:T(8,128)(2,1)} %partial_s.1), calls=%async_computation.1 | async-start | bytes 557056 | tf_op jit(solution)/shard_map/all_to_all | solution.py:150
  107.4 3.3 %partial_qx.1 = bf16[4,272,512]{2,1,0:T(8,128)(2,1)S(1)} custom-call(s32[2]{0:T(128)S(1)} %pad_add_fusion.place_ref, bf16[512,1280]{1,0:T(8,128)(2,1)S(1)} %bitcast.20, bf16[512,1280]{1,0:T(8,128)(2,1)} %collective-permute-done.3.other_ref, bf16[16,1280]{1,0:T(8,128)(2,1)S(1)} %add.35.tail_ref, bf16[640,640]{1,0:T(8,128)(2,1)S(1)} %all_gather.12.w_own_ref, ...), custom_call_target="tpu_custom_call" | custom-call | tf_op jit(solution)/shard_map/partial_qx/pallas_call | solution.py:139
  110.7 1.0 copy-done
  111.7 3.0 %all-to-all-done.1 = bf16[4,272,128]{2,1,0:T(8,128)(2,1)S(1)} async-done(((bf16[4,272,128]{2,1,0:T(8,128)(2,1)}), bf16[4,272,128]{2,1,0:T(8,128)(2,1)S(1)}, u32[]{:S(2)}, u32[]{:S(2)}) %all-to-all-start.1) | async-done | bytes 278560 | tf_op jit(solution)/shard_map/all_to_all | solution.py:150
  114.7 3.5 %all-to-all-start.2 = ((bf16[4,272,512]{2,1,0:T(8,128)(2,1)}), bf16[4,272,512]{2,1,0:T(8,128)(2,1)S(1)}, u32[]{:S(2)}, u32[]{:S(2)}) async-start(bf16[4,272,512]{2,1,0:T(8,128)(2,1)} %copy-done), calls=%async_computation.2 | async-start | bytes 2228224 | tf_op jit(solution)/shard_map/all_to_all | solution.py:153
  118.3 0.1 copy.22
  118.5 15.7 %all-gather = bf16[2432,128]{1,0:T(8,128)(2,1)S(1)} all-gather(bf16[304,128]{1,0:T(8,128)(2,1)S(1)} %fusion.1), channel_id=2, replica_groups=mesh['zh'=4,'zl'=4,'yh'=2,'x'=4,'yl'=4,'c'=2] {'yl','c'}, dimensions={0}, use_global_device_ids=true | all-gather | bytes 700416 | tf_op jit(solution)/shard_map/all_gather | solution.py:157
  134.2 0.0 copy-start.2
  134.2 0.0 copy-start.3
  134.2 0.2 fusion.3
  134.4 0.1 copy.19
  134.5 0.1 copy.18
  134.6 0.6 fusion.2
  135.1 0.1 pad_maximum_fusion.cos_ref
  135.2 0.1 copy.21
  135.3 0.1 copy.20
  135.4 0.1 pad_maximum_fusion.1.sin_ref
  135.5 0.1 broadcast_in_dim.5.rel_ref
  135.7 1.7 %rotate_and_convolve.1 = (bf16[256,256]{1,0:T(8,128)(2,1)}, bf16[256,512]{1,0:T(8,128)(2,1)}, bf16[256,256]{1,0:T(8,128)(2,1)}, bf16[256,512]{1,0:T(8,128)(2,1)}) custom-call(bf16[4,272,512]{2,1,0:T(8,128)(2,1)S(1)} %all-to-all-done.2.parts_ref, bf16[8,304,128]{2,1,0:T(8,128)(2,1)S(1)} %bitcast.22, f32[256,128]{1,0:T(8,128)S(1)} %pad_maximum_fusion.cos_ref, ...), custom_call_target="tpu_custom_call" | custom-call | tf_op jit(solution)/shard_map/rotate_and_convolve/pallas_call | solution.py:172
  (32 shorter events, 0.2 us)
Async XLA Ops:
  0.6 1.0 copy-start.1
  3.3 8.1 %copy-start.4 = (bf16[40,256]{1,0:T(8,128)(2,1)S(1)}, bf16[40,256]{1,0:T(8,128)(2,1)}, u32[]{:S(2)}) copy-start(bf16[40,256]{1,0:T(8,128)(2,1)} %param.11) | copy-start | bytes 61444
  3.3 8.2 %copy-start.5 = (bf16[40,256]{1,0:T(8,128)(2,1)S(1)}, bf16[40,256]{1,0:T(8,128)(2,1)}, u32[]{:S(2)}) copy-start(bf16[40,256]{1,0:T(8,128)(2,1)} %param.12) | copy-start | bytes 61444
  3.3 8.2 %copy-start.6 = (bf16[40,128]{1,0:T(8,128)(2,1)S(1)}, bf16[40,128]{1,0:T(8,128)(2,1)}, u32[]{:S(2)}) copy-start(bf16[40,128]{1,0:T(8,128)(2,1)} %param.13) | copy-start | bytes 30724
  3.3 53.8 %all-to-all-start = ((bf16[16,32,1280]{2,1,0:T(8,128)(2,1)}), bf16[16,32,1280]{2,1,0:T(8,128)(2,1)S(1)}, u32[]{:S(2)}, u32[]{:S(2)}) async-start(bf16[16,32,1280]{2,1,0:T(8,128)(2,1)} %permute_columns.1), calls=%async_computation | async-start | bytes 2621440 | tf_op jit(solution)/shard_map/all_to_all | solution.py:121
  11.5 45.6 %collective-permute-start = (bf16[40,640]{1,0:T(8,128)(2,1)S(1)}, bf16[40,640]{1,0:T(8,128)(2,1)S(1)}, u32[]{:S(2)}, u32[]{:S(2)}) collective-permute-start(bf16[40,640]{1,0:T(8,128)(2,1)S(1)} %constant_dynamic-update-slice_fusion), channel_id=1, source_target_pairs={{0,32},{32,0},{1,33},{33,1},{2,34},{34,2},{3,35},{35,3},{4,36},{36... | collective-permute-start | bytes 153608 | tf_op jit(solution)/shard_map/ppermute | solution.py:124
  57.1 42.9 %collective-permute-start.3 = (bf16[512,1280]{1,0:T(8,128)(2,1)S(1)}, bf16[512,1280]{1,0:T(8,128)(2,1)}, u32[]{:S(2)}, u32[]{:S(2)}) collective-permute-start(bf16[512,1280]{1,0:T(8,128)(2,1)S(1)} %bitcast.17), channel_id=1, source_target_pairs={{0,1},{1,0},{2,3},{3,2},{4,5},{5,4},{6,7},{7,6},{8,9},{9,8},{10,11... | collective-permute-start | bytes 3932168 | tf_op jit(solution)/shard_map/ppermute | solution.py:127
  66.6 33.4 %collective-permute-start.1 = (bf16[16,1280]{1,0:T(8,128)(2,1)S(1)}, bf16[16,1280]{1,0:T(8,128)(2,1)S(1)}, u32[]{:S(2)}, u32[]{:S(2)}) collective-permute-start(bf16[16,1280]{1,0:T(8,128)(2,1)S(1)} %slice.18), channel_id=1, source_target_pairs={{1,32},{33,64},{65,96},{97,128},{129,160},{161,192},{193,224},{225... | collective-permute-start | bytes 122888 | tf_op jit(solution)/shard_map/ppermute | solution.py:130
  70.9 29.1 %collective-permute-start.2 = (bf16[16,1280]{1,0:T(8,128)(2,1)S(1)}, bf16[16,1280]{1,0:T(8,128)(2,1)S(1)}, u32[]{:S(2)}, u32[]{:S(2)}) collective-permute-start(bf16[16,1280]{1,0:T(8,128)(2,1)S(1)} %slice.18), channel_id=1, source_target_pairs={{1,33},{33,65},{65,97},{97,129},{129,161},{161,193},{193,225},{225... | collective-permute-start | bytes 122888 | tf_op jit(solution)/shard_map/ppermute | solution.py:130
  102.9 11.8 %all-to-all-start.1 = ((bf16[4,272,128]{2,1,0:T(8,128)(2,1)}), bf16[4,272,128]{2,1,0:T(8,128)(2,1)S(1)}, u32[]{:S(2)}, u32[]{:S(2)}) async-start(bf16[4,272,128]{2,1,0:T(8,128)(2,1)} %partial_s.1), calls=%async_computation.1 | async-start | bytes 557056 | tf_op jit(solution)/shard_map/all_to_all | solution.py:150
  110.7 1.0 copy-start
  111.7 6.5 %copy-start.7 = (s32[32]{0:T(128)S(1)}, s32[32]{0:T(128)}, u32[]{:S(2)}) copy-start(s32[32]{0:T(128)} %param.10) | copy-start | bytes 388
  111.7 6.5 %copy-start.8 = (s32[32]{0:T(128)S(1)}, s32[32]{0:T(128)}, u32[]{:S(2)}) copy-start(s32[32]{0:T(128)} %param.9) | copy-start | bytes 388
  114.7 19.5 %all-to-all-start.2 = ((bf16[4,272,512]{2,1,0:T(8,128)(2,1)}), bf16[4,272,512]{2,1,0:T(8,128)(2,1)S(1)}, u32[]{:S(2)}, u32[]{:S(2)}) async-start(bf16[4,272,512]{2,1,0:T(8,128)(2,1)} %copy-done), calls=%async_computation.2 | async-start | bytes 2228224 | tf_op jit(solution)/shard_map/all_to_all | solution.py:153
  134.2 1.4 %copy-start.2 = (f32[4,512]{1,0:T(4,128)S(1)}, f32[4,512]{1,0:T(4,128)}, u32[]{:S(2)}) copy-start(f32[4,512]{1,0:T(4,128)} %tbc_ref.1) | copy-start | bytes 24580
  134.2 1.4 %copy-start.3 = (f32[4,256]{1,0:T(4,128)S(1)}, f32[4,256]{1,0:T(4,128)}, u32[]{:S(2)}) copy-start(f32[4,256]{1,0:T(4,128)} %tx_ref.1) | copy-start | bytes 12292
